TPU v7x, 32 devices: a whole 2x2x4 slice. The times are simulated.
32 devices in a mesh: parts: 2 (over x), row: 16 (over z, y, core).
Axes of the slice: x: 2, y: 2, z: 4, core: 2. Of those that a mesh axis runs over, the one named last changes fastest.
Arguments:
- tile_values: bfloat16 [2048, 128, 128], P(('parts', 'row')), parts along dimension 0, may hold values from -0.09375 to 0.09375
- tile_row: int32 [2048], P(('parts', 'row')), parts along dimension 0, may hold values from 0 to 1
- tile_col: int32 [2048], P(('parts', 'row')), parts along dimension 0, may hold values from 0 to 15
- primal_start: float32 [4096, 128], P(('parts', 'row')), parts along dimension 0, may hold values from 0 to 1
- objective: float32 [4096, 128], P(('parts', 'row')), parts along dimension 0, may hold values from -3 to 3
- upper_bound: float32 [4096], P(('parts', 'row')), parts along dimension 0, may hold values from 0.3 to 3
- dual_start: float32 [8192, 128], P(('parts', 'row')), parts along dimension 0, may hold values from 0 to 1
- row_bound: float32 [8192, 128], P(('parts', 'row')), parts along dimension 0, may hold values from -6 to 6
Outputs:
- primal: float32 [4096, 128], P(('parts', 'row')), parts along dimension 0
- dual: float32 [8192, 128], P(('parts', 'row')), parts along dimension 0
There are 2 independent parts, one for each index of `parts`. A program takes and returns all parts, laid end to end along the dimension named above; each array names one. Nothing has to cross between parts.
All inputs are finite; a program needn't handle non-finite values.
Results may differ from a plain program's by a relative error of at most 0.0023.
Values may be sent and summed in bfloat16 or wider, within the bound.
No kernel may reach another device: no remote copies, remote signals or barrier semaphores. Data moves between devices by JAX's collectives and lax.ppermute only.
A program may use at most 64 MiB of HBM per device.

v0:
```python
import jax
import jax.numpy as jnp
from jax import lax
from jax.sharding import PartitionSpec as P

ITERS = 3


def body(
    tile_values, tile_row, tile_col, primal_start, objective, upper_bound, dual_start, row_bound
):
    devices = lax.axis_size("row")
    tile_size = tile_values.shape[1]
    scenarios = primal_start.shape[1]
    column_blocks = devices * primal_start.shape[0] // tile_size
    row_blocks = dual_start.shape[0] // tile_size
    primal = primal_start
    dual = dual_start
    for iteration in range(ITERS):
        dual_low = dual.astype(jnp.bfloat16).reshape(row_blocks, tile_size, scenarios)
        picked = jnp.take(dual_low, tile_row, axis=0)
        partial_value = jnp.einsum(
            "tij,tis->tjs", tile_values, picked, preferred_element_type=jnp.float32
        )
        local_sums = jax.ops.segment_sum(partial_value, tile_col, num_segments=column_blocks)
        pieces = lax.all_to_all(local_sums, "row", split_axis=0, concat_axis=0, tiled=True)
        column_sum = jnp.sum(pieces, axis=0)
        updated = jnp.clip(primal - 0.4 * (objective - column_sum), 0.0, upper_bound[:, None])
        extrapolated = (2.0 * updated - primal).astype(jnp.bfloat16)
        gathered = lax.all_gather(extrapolated, "row", axis=0, tiled=True).reshape(
            column_blocks, tile_size, scenarios
        )
        chosen = jnp.take(gathered, tile_col, axis=0)
        products = jnp.einsum(
            "tij,tjs->tis", tile_values, chosen, preferred_element_type=jnp.float32
        )
        row_image = jax.ops.segment_sum(products, tile_row, num_segments=row_blocks).reshape(
            dual.shape
        )
        dual = jnp.maximum(dual + 0.4 * (row_bound - row_image), 0.0)
        primal = updated
    return (primal, dual)


def solution(mesh):
    return jax.shard_map(
        body,
        mesh=mesh,
        in_specs=(
            P(("parts", "row"), None, None),
            P(("parts", "row")),
            P(("parts", "row")),
            P(("parts", "row"), None),
            P(("parts", "row"), None),
            P(("parts", "row")),
            P(("parts", "row"), None),
            P(("parts", "row"), None),
        ),
        out_specs=(P(("parts", "row"), None), P(("parts", "row"), None)),
        check_vma=False,
    )
```

profile of v0, /device:TPU:0, one launch (start us, length us, event | category | flops | bytes accessed | tf_op | source)
XLA Modules:
  0.0 300.1 jit_solution(7222354940513220245)
XLA Ops:
  5.2 4.5 %convolution_bitcast_fusion.5 = f32[64,128,128]{1,2,0:T(8,128)} fusion(bf16[64,128,128]{2,1,0:T(8,128)(2,1)S(1)} %copy-done, bf16[64,128,128]{2,1,0:T(8,128)(2,1)} %gather_fusion, pred[64]{0:T(512)(128)(4,1)S(1)} %compare_and_fusion.1), kind=kOutput, calls=%fused_computation.17 | convolution fusion | flops 269484032 | bytes 8388672 | tf_op jit(solution)/shard_map/tij,tis->tjs/dot_general | solution.py:22
  9.7 5.6 %copy.17 = f32[64,128,128]{2,1,0:T(8,128)} copy(f32[64,128,128]{1,2,0:T(8,128)} %convolution_bitcast_fusion.5) | data formatting | bytes 8388608 | tf_op jit(solution)/shard_map/tij,tis->tjs/dot_general | solution.py:22
  16.4 13.3 %scatter_fusion = f32[16,128,128]{2,1,0:T(8,128)} fusion(f32[16,128,128]{2,1,0:T(8,128)} %broadcast.25.clone, s32[64]{0:T(128)S(1)} %copy-done.6, f32[64,128,128]{2,1,0:T(8,128)} %copy.17), kind=kCustom, calls=%fused_computation.6 | custom fusion | flops 1048576 | bytes 12583168 | tf_op jit(solution)/shard_map/scatter-add | solution.py:25
  29.7 7.5 %all-to-all-start = ((f32[16,128,128]{2,1,0:T(8,128)}), f32[16,128,128]{2,1,0:T(8,128)S(1)}, u32[]{:S(2)}, u32[]{:S(2)}) async-start(f32[16,128,128]{2,1,0:T(8,128)} %scatter_fusion), calls=%async_computation | async-start | bytes 2097152 | tf_op jit(solution)/shard_map/all_to_all | solution.py:26
  37.2 22.9 %all-to-all-done = f32[16,128,128]{2,1,0:T(8,128)S(1)} async-done(((f32[16,128,128]{2,1,0:T(8,128)}), f32[16,128,128]{2,1,0:T(8,128)S(1)}, u32[]{:S(2)}, u32[]{:S(2)}) %all-to-all-start) | async-done | bytes 1048608 | tf_op jit(solution)/shard_map/all_to_all | solution.py:26
  60.9 24.1 %all_gather.9 = bf16[2048,128]{1,0:T(8,128)(2,1)S(1)} all-gather(bf16[128,128]{1,0:T(8,128)(2,1)S(1)} %get-tuple-element.8), channel_id=1, replica_groups=mesh['parts'=2,'row'=16] {'row'}, dimensions={0}, use_global_device_ids=true | all-gather | bytes 557056 | tf_op jit(solution)/shard_map/all_gather | solution.py:30
  87.1 5.3 %convolution_bitcast_fusion.4 = f32[64,128,128]{1,2,0:T(8,128)} fusion(bf16[64,128,128]{2,1,0:T(8,128)(2,1)S(1)} %copy-done, bf16[64,128,128]{2,1,0:T(8,128)(2,1)} %gather_fusion.1, pred[64]{0:T(512)(128)(4,1)S(1)} %compare_and_fusion), kind=kOutput, calls=%fused_computation.16 | convolution fusion | flops 269484032 | bytes 8388672 | tf_op jit(solution)/shard_map/tij,tjs->tis/dot_general | solution.py:34
  92.4 5.6 %copy.19 = f32[64,128,128]{2,1,0:T(8,128)} copy(f32[64,128,128]{1,2,0:T(8,128)} %convolution_bitcast_fusion.4) | data formatting | bytes 8388608 | tf_op jit(solution)/shard_map/tij,tjs->tis/dot_general | solution.py:34
  98.1 8.8 %scatter_fusion.1 = f32[2,128,128]{2,1,0:T(8,128)S(1)} fusion(f32[2,128,128]{2,1,0:T(8,128)S(1)} %broadcast.27.clone, s32[64]{0:T(128)S(1)} %copy-done.8, f32[64,128,128]{2,1,0:T(8,128)} %copy.19), kind=kCustom, calls=%fused_computation.7 | custom fusion | flops 1048576 | bytes 12583168 | tf_op jit(solution)/shard_map/scatter-add | solution.py:37
  109.1 4.5 %convolution_bitcast_fusion.3 = f32[64,128,128]{1,2,0:T(8,128)} fusion(bf16[64,128,128]{2,1,0:T(8,128)(2,1)S(1)} %copy-done, bf16[64,128,128]{2,1,0:T(8,128)(2,1)} %gather_fusion.2, pred[64]{0:T(512)(128)(4,1)S(1)} %copy-done.15), kind=kOutput, calls=%fused_computation.15 | convolution fusion | flops 269484032 | bytes 8388672 | tf_op jit(solution)/shard_map/tij,tis->tjs/dot_general | solution.py:22
  113.5 5.6 %copy.21 = f32[64,128,128]{2,1,0:T(8,128)} copy(f32[64,128,128]{1,2,0:T(8,128)} %convolution_bitcast_fusion.3) | data formatting | bytes 8388608 | tf_op jit(solution)/shard_map/tij,tis->tjs/dot_general | solution.py:22
  119.2 8.8 %scatter_fusion.2 = f32[16,128,128]{2,1,0:T(8,128)S(1)} fusion(f32[16,128,128]{2,1,0:T(8,128)S(1)} %broadcast.25.clone.1, s32[64]{0:T(128)S(1)} %copy-done.6, f32[64,128,128]{2,1,0:T(8,128)} %copy.21), kind=kCustom, calls=%fused_computation.8 | custom fusion | flops 1048576 | bytes 12583168 | tf_op jit(solution)/shard_map/scatter-add | solution.py:25
  128.1 28.1 %all_to_all.15 = f32[16,128,128]{2,1,0:T(8,128)} all-to-all(f32[16,128,128]{2,1,0:T(8,128)S(1)} %scatter_fusion.2), channel_id=1, replica_groups=mesh['parts'=2,'row'=16] {'row'}, dimensions={0} | all-to-all | bytes 2097152 | tf_op jit(solution)/shard_map/all_to_all | solution.py:26
  159.0 22.3 %all_gather.10 = bf16[2048,128]{1,0:T(8,128)(2,1)S(1)} all-gather(bf16[128,128]{1,0:T(8,128)(2,1)S(1)} %get-tuple-element.6), channel_id=1, replica_groups=mesh['parts'=2,'row'=16] {'row'}, dimensions={0}, use_global_device_ids=true | all-gather | bytes 557056 | tf_op jit(solution)/shard_map/all_gather | solution.py:30
  183.5 5.3 %convolution_bitcast_fusion.2 = f32[64,128,128]{1,2,0:T(8,128)} fusion(bf16[64,128,128]{2,1,0:T(8,128)(2,1)S(1)} %copy-done, bf16[64,128,128]{2,1,0:T(8,128)(2,1)} %gather_fusion.3, pred[64]{0:T(512)(128)(4,1)S(1)} %copy-done.12), kind=kOutput, calls=%fused_computation.14 | convolution fusion | flops 269484032 | bytes 8388672 | tf_op jit(solution)/shard_map/tij,tjs->tis/dot_general | solution.py:34
  188.8 5.6 %copy.23 = f32[64,128,128]{2,1,0:T(8,128)} copy(f32[64,128,128]{1,2,0:T(8,128)} %convolution_bitcast_fusion.2) | data formatting | bytes 8388608 | tf_op jit(solution)/shard_map/tij,tjs->tis/dot_general | solution.py:34
  194.4 8.8 %scatter_fusion.3 = f32[2,128,128]{2,1,0:T(8,128)S(1)} fusion(f32[2,128,128]{2,1,0:T(8,128)S(1)} %broadcast.27.clone.1, s32[64]{0:T(128)S(1)} %copy-done.9, f32[64,128,128]{2,1,0:T(8,128)} %copy.23), kind=kCustom, calls=%fused_computation.9 | custom fusion | flops 1048576 | bytes 12583168 | tf_op jit(solution)/shard_map/scatter-add | solution.py:37
  209.9 5.6 %copy.25 = f32[64,128,128]{2,1,0:T(8,128)} copy(f32[64,128,128]{1,2,0:T(8,128)} %convolution_bitcast_fusion.1) | data formatting | bytes 8388608 | tf_op jit(solution)/shard_map/tij,tis->tjs/dot_general | solution.py:22
  215.6 8.8 %scatter_fusion.4 = f32[16,128,128]{2,1,0:T(8,128)S(1)} fusion(f32[16,128,128]{2,1,0:T(8,128)S(1)} %broadcast.25, s32[64]{0:T(128)S(1)} %copy-done.6, f32[64,128,128]{2,1,0:T(8,128)} %copy.25), kind=kCustom, calls=%fused_computation.10 | custom fusion | flops 1048576 | bytes 12583168 | tf_op jit(solution)/shard_map/scatter-add | solution.py:25
  224.4 28.1 %all_to_all.16 = f32[16,128,128]{2,1,0:T(8,128)} all-to-all(f32[16,128,128]{2,1,0:T(8,128)S(1)} %scatter_fusion.4), channel_id=1, replica_groups=mesh['parts'=2,'row'=16] {'row'}, dimensions={0} | all-to-all | bytes 2097152 | tf_op jit(solution)/shard_map/all_to_all | solution.py:26
  255.3 22.1 %all_gather.11 = bf16[2048,128]{1,0:T(8,128)(2,1)S(1)} all-gather(bf16[128,128]{1,0:T(8,128)(2,1)S(1)} %get-tuple-element.4), channel_id=1, replica_groups=mesh['parts'=2,'row'=16] {'row'}, dimensions={0}, use_global_device_ids=true | all-gather | bytes 557056 | tf_op jit(solution)/shard_map/all_gather | solution.py:30
  279.6 5.3 %convolution_bitcast_fusion = f32[64,128,128]{1,2,0:T(8,128)} fusion(bf16[64,128,128]{2,1,0:T(8,128)(2,1)S(1)} %copy-done, bf16[64,128,128]{2,1,0:T(8,128)(2,1)} %gather_fusion.5, pred[64]{0:T(512)(128)(4,1)S(1)} %copy-done.13), kind=kOutput, calls=%fused_computation.12 | convolution fusion | flops 269484032 | bytes 8388672 | tf_op jit(solution)/shard_map/tij,tjs->tis/dot_general | solution.py:34
  284.9 5.6 %copy.27 = f32[64,128,128]{2,1,0:T(8,128)} copy(f32[64,128,128]{1,2,0:T(8,128)} %convolution_bitcast_fusion) | data formatting | bytes 8388608 | tf_op jit(solution)/shard_map/tij,tjs->tis/dot_general | solution.py:34
  290.6 8.8 %scatter_fusion.5 = f32[2,128,128]{2,1,0:T(8,128)S(1)} fusion(f32[2,128,128]{2,1,0:T(8,128)S(1)} %broadcast.27, s32[64]{0:T(128)S(1)} %copy-done.10, f32[64,128,128]{2,1,0:T(8,128)} %copy.27), kind=kCustom, calls=%fused_computation.11 | custom fusion | flops 1048576 | bytes 12583168 | tf_op jit(solution)/shard_map/scatter-add | solution.py:37
  (63 shorter events, 28.4 us)
Async XLA Ops:
  0.6 4.6 %copy-start = (bf16[64,128,128]{2,1,0:T(8,128)(2,1)S(1)}, bf16[64,128,128]{2,1,0:T(8,128)(2,1)}, u32[]{:S(2)}) copy-start(bf16[64,128,128]{2,1,0:T(8,128)(2,1)} %param.12) | copy-start | bytes 6291460
  2.1 3.1 %copy-start.14 = (pred[64]{0:T(512)(128)(4,1)}, pred[64]{0:T(512)(128)(4,1)S(1)}, u32[]{:S(2)}) copy-start(pred[64]{0:T(512)(128)(4,1)S(1)} %compare_and_fusion.1) | copy-start | bytes 196
  9.7 6.7 %copy-start.6 = (s32[64]{0:T(128)S(1)}, s32[64]{0:T(128)}, u32[]{:S(2)}) copy-start(s32[64]{0:T(128)} %param.14) | copy-start | bytes 772
  29.7 30.5 %copy-start.4 = (f32[128,128]{1,0:T(8,128)S(1)}, f32[128,128]{1,0:T(8,128)}, u32[]{:S(2)}) copy-start(f32[128,128]{1,0:T(8,128)} %param.16) | copy-start | bytes 196612
  29.7 30.5 %copy-start.5 = (f32[128,128]{1,0:T(8,128)S(1)}, f32[128,128]{1,0:T(8,128)}, u32[]{:S(2)}) copy-start(f32[128,128]{1,0:T(8,128)} %param.15) | copy-start | bytes 196612
  29.7 30.5 %copy-start.7 = (f32[128]{0:T(128)S(1)}, f32[128]{0:T(128)}, u32[]{:S(2)}) copy-start(f32[128]{0:T(128)} %param.17) | copy-start | bytes 1540
  29.7 30.4 %all-to-all-start = ((f32[16,128,128]{2,1,0:T(8,128)}), f32[16,128,128]{2,1,0:T(8,128)S(1)}, u32[]{:S(2)}, u32[]{:S(2)}) async-start(f32[16,128,128]{2,1,0:T(8,128)} %scatter_fusion), calls=%async_computation | async-start | bytes 2097152 | tf_op jit(solution)/shard_map/all_to_all | solution.py:26
  37.2 50.0 %copy-start.11 = (pred[64]{0:T(512)(128)(4,1)}, pred[64]{0:T(512)(128)(4,1)S(1)}, u32[]{:S(2)}) copy-start(pred[64]{0:T(512)(128)(4,1)S(1)} %compare_and_fusion) | copy-start | bytes 196
  92.4 5.6 %copy-start.8 = (s32[64]{0:T(128)S(1)}, s32[64]{0:T(128)}, u32[]{:S(2)}) copy-start(s32[64]{0:T(128)} %param.13) | copy-start | bytes 772
  98.1 8.8 %copy-start.1 = (f32[256,128]{1,0:T(8,128)S(1)}, f32[256,128]{1,0:T(8,128)}, u32[]{:S(2)}) copy-start(f32[256,128]{1,0:T(8,128)} %param.18) | copy-start | bytes 393220
  98.1 8.8 %copy-start.2 = (f32[256,128]{1,0:T(8,128)S(1)}, f32[256,128]{1,0:T(8,128)}, u32[]{:S(2)}) copy-start(f32[256,128]{1,0:T(8,128)} %param.19) | copy-start | bytes 393220
  106.9 2.2 copy-start.15
  181.3 2.1 copy-start.12
  188.8 5.6 %copy-start.9 = (s32[64]{0:T(128)S(1)}, s32[64]{0:T(128)}, u32[]{:S(2)}) copy-start(s32[64]{0:T(128)} %param.13) | copy-start | bytes 772
  203.3 2.2 copy-start.16
  277.5 2.1 copy-start.13
  284.9 5.6 %copy-start.10 = (s32[64]{0:T(128)S(1)}, s32[64]{0:T(128)}, u32[]{:S(2)}) copy-start(s32[64]{0:T(128)} %param.13) | copy-start | bytes 772
  290.6 8.8 %copy-start.3 = (f32[256,128]{1,0:T(8,128)S(1)}, f32[256,128]{1,0:T(8,128)}, u32[]{:S(2)}) copy-start(f32[256,128]{1,0:T(8,128)} %param.19) | copy-start | bytes 393220
where the time goes:
time: 302 us; the launch traced here: 300 us
  blocking collectives  125 us (41%)
  other arithmetic  66.9 us (22%)
  local copies, waits for them, and re-layouts  47.9 us (16%)
  matrix products  29.3 us (10%)
  waiting for transfers between devices  22.9 us (8%)
  starting transfers between devices  7.45 us (2%)
    all_gather x3, blocking collectives, body(): lax.all_gather(extrapolated, 'row', axis=0, tiled=True)  68.6 us
    all_to_all x2, blocking collectives, body(): lax.all_to_all(local_sums, 'row', split_axis=0, concat_axis=0, tiled=True)  56.2 us
    scatter-add x3, other arithmetic, body(): jax.ops.segment_sum(partial_value, tile_col, num_segments=column_blocks)  30.9 us
    scatter-add x3, other arithmetic, body(): jax.ops.segment_sum(products, tile_row, num_segments=row_blocks)  26.3 us
    all_to_all x1, waiting for transfers between devices, body(): lax.all_to_all(local_sums, 'row', split_axis=0, concat_axis=0, tiled=True)  22.9 us
    dot_general x3, local copies, waits for them, and re-layouts, body(): jnp.einsum('tij,tjs->tis', tile_values, chosen, preferred_element_type=jn...  16.8 us
    dot_general x3, local copies, waits for them, and re-layouts, body(): jnp.einsum('tij,tis->tjs', tile_values, picked, preferred_element_type=jn...  16.8 us
    dot_general x3, matrix products, body(): jnp.einsum('tij,tjs->tis', tile_values, chosen, preferred_element_type=jn...  15.9 us
  transfers between devices with their start and end apart: 1, of which 1 were waited for; matrix products, arithmetic and copies ran while one was open for 0% of the time, Pallas kernels for 0%

commit v1 on v0

v1 whole, which is shorter than its diff:
```python
import functools

import jax
import jax.numpy as jnp
from jax import lax
from jax.experimental import pallas as pl
from jax.experimental.pallas import tpu as pltpu
from jax.sharding import PartitionSpec as P

ITERS = 3
STEP = 0.4
CORES = 2
PAIRS = 2
VMEM = pl.BlockSpec(memory_space=pltpu.VMEM)
SMEM = pl.BlockSpec(memory_space=pltpu.SMEM)
F32, BF16 = jnp.float32, jnp.bfloat16


def params(limit=24 * 2**20):
    return pltpu.CompilerParams(vmem_limit_bytes=limit)


def place():
    me = lax.axis_index("row")
    return me // (CORES * PAIRS), (me // CORES) % PAIRS, me % CORES


def dense_kernel(groups, span, row_ref, col_ref, tile_ref, own_ref, other_ref, acc):
    tiles, size, _ = tile_ref.shape
    row_blocks = own_ref.shape[2] // size
    core = place()[2]
    acc[...] = jnp.zeros_like(acc)

    def add(t, _):
        at = col_ref[t] * row_blocks + row_ref[t]
        acc[at] = acc[at] + tile_ref[t].astype(F32)
        return 0

    lax.fori_loop(0, tiles, add, 0, unroll=4)
    for ref, half in ((own_ref, core), (other_ref, 1 - core)):
        for z in range(groups):
            for y in range(PAIRS):
                for s in range(span):
                    column = (((z * PAIRS + y) * CORES + half) * span + s) * row_blocks
                    for r in range(row_blocks):
                        block = acc[column + r]
                        high = block.astype(BF16)
                        low = (block - high.astype(F32)).astype(BF16)
                        rows = pl.ds(r * size, size)
                        cols = pl.ds((y * span + s) * size, size)
                        ref[0, z, rows, cols] = high
                        ref[1, z, rows, cols] = low


def dense(tile_values, tile_row, tile_col, groups, span, row_blocks):
    tiles, size, _ = tile_values.shape
    half = jax.ShapeDtypeStruct((2, groups, row_blocks * size, PAIRS * span * size), BF16)
    return pl.pallas_call(
        functools.partial(dense_kernel, groups, span),
        out_shape=(half, half),
        in_specs=[SMEM, SMEM, VMEM],
        out_specs=(VMEM, VMEM),
        scratch_shapes=[
            pltpu.VMEM((groups * PAIRS * CORES * span * row_blocks, size, size), F32)
        ],
        compiler_params=params(),
    )(tile_row, tile_col, tile_values)


def tn(a, b):
    return lax.dot_general(a, b, (((0,), (0,)), ((), ())), preferred_element_type=F32)


def nt(a, b):
    return lax.dot_general(a, b, (((1,), (1,)), ((), ())), preferred_element_type=F32)


def column_kernel(first, groups, *refs):
    if first:
        (a_own, a_mate, dual_own, dual_mate), outs = refs[:4], refs[4:]
        new = (dual_own[...], dual_mate[...])
        pieces = outs
    else:
        (a_own, a_mate, dual_own, dual_mate, bound_own, bound_mate, image, image_in), outs = (
            refs[:8],
            refs[8:],
        )
        rows = dual_own.shape[0]
        new = []
        for i, (d, b) in enumerate(((dual_own, bound_own), (dual_mate, bound_mate))):
            total = image[i] + image_in[1 - i]
            new.append(jnp.maximum(d[...] + STEP * (b[...] - total), 0.0))
            outs[i][...] = new[i]
        pieces = outs[2:]
    low_own, low_mate = (n.astype(BF16) for n in new)
    me = place()[0]
    for k in range(groups):
        z = me ^ k
        total = tn(low_own, a_own[0, z]) + tn(low_mate, a_mate[0, z])
        total += tn(low_own, a_own[1, z]) + tn(low_mate, a_mate[1, z])
        pieces[k][...] = total.astype(pieces[k].dtype)


def row_kernel(groups, a_own, a_mate, *refs):
    pieces, image = refs[:groups], refs[groups]
    me = place()[0]
    for i, a in enumerate((a_own, a_mate)):
        total = None
        for k in range(groups):
            z = me ^ k
            part = nt(a[0, z], pieces[k][...]) + nt(a[1, z], pieces[k][...])
            total = part if total is None else total + part
        image[i] = total


def body(
    tile_values, tile_row, tile_col, primal_start, objective, upper_bound, dual_start, row_bound
):
    devices = lax.axis_size("row")
    size = tile_values.shape[1]
    width, scenarios = primal_start.shape
    rows = dual_start.shape[0]
    groups = devices // (CORES * PAIRS)
    span = width // size
    both = PAIRS * width
    y = place()[1]

    def swap(x, mask):
        return lax.ppermute(x, "row", [(i, i ^ mask) for i in range(devices)])

    own, other = dense(tile_values, tile_row, tile_col, groups, span, rows // size)
    mate = swap(other, 1)
    duals = (dual_start, swap(dual_start, 1))
    bounds = (row_bound, swap(row_bound, 1))

    mine = jnp.concatenate(
        [primal_start.T, objective.T, jnp.broadcast_to(upper_bound[None, :], (8, width))], 0
    )
    theirs = swap(mine, CORES)
    joint = jnp.where(
        y == 0, jnp.concatenate([mine, theirs], 1), jnp.concatenate([theirs, mine], 1)
    )
    primal, cost, limit = (
        joint[:scenarios],
        joint[scenarios : 2 * scenarios],
        joint[2 * scenarios : 2 * scenarios + 1],
    )

    piece = jax.ShapeDtypeStruct((scenarios, both), BF16)
    kept = jax.ShapeDtypeStruct((scenarios, both), F32)
    side = jax.ShapeDtypeStruct((rows, scenarios), F32)
    image_shape = jax.ShapeDtypeStruct((2, rows, scenarios), F32)
    images = None
    for iteration in range(ITERS):
        first = iteration == 0
        operands = (own, mate, *duals)
        if not first:
            operands += (*bounds, *images)
        out = pl.pallas_call(
            functools.partial(column_kernel, first, groups),
            out_shape=(() if first else (side, side)) + (kept,) + (piece,) * (groups - 1),
            in_specs=[VMEM] * len(operands),
            out_specs=(VMEM,) * (groups + (0 if first else 2)),
            compiler_params=params(),
        )(*operands)
        if not first:
            duals, out = out[:2], out[2:]
        total = out[0]
        for k in range(1, groups):
            total = total + swap(out[k], k * CORES * PAIRS).astype(F32)
        total = total + swap(total.astype(BF16), CORES).astype(F32)
        updated = jnp.clip(primal - STEP * (cost - total), 0.0, limit)
        ahead = (2.0 * updated - primal).astype(BF16)
        primal = updated
        pieces = [ahead] + [swap(ahead, k * CORES * PAIRS) for k in range(1, groups)]
        image = pl.pallas_call(
            functools.partial(row_kernel, groups),
            out_shape=image_shape,
            in_specs=[VMEM] * (groups + 2),
            out_specs=VMEM,
            compiler_params=params(),
        )(own, mate, *pieces)
        if iteration < ITERS - 1:
            images = (image, swap(image, 1))
        else:
            total = image[0] + swap(image[1], 1)
            dual = jnp.maximum(duals[0] + STEP * (row_bound - total), 0.0)
    mine = jnp.where(y == 0, primal[:, :width], primal[:, width:]).T
    return (mine, dual)


def solution(mesh):
    return jax.shard_map(
        body,
        mesh=mesh,
        in_specs=(
            P(("parts", "row"), None, None),
            P(("parts", "row")),
            P(("parts", "row")),
            P(("parts", "row"), None),
            P(("parts", "row"), None),
            P(("parts", "row")),
            P(("parts", "row"), None),
            P(("parts", "row"), None),
        ),
        out_specs=(P(("parts", "row"), None), P(("parts", "row"), None)),
        check_vma=False,
    )
```

time: 302 us -> 84.8 us (0.28)
  blocking collectives: 125 us -> 0 us
  other arithmetic: 66.9 us -> 1.05 us
  local copies, waits for them, and re-layouts: 47.9 us -> 5.13 us
  matrix products: 29.3 us -> 0 us
  starting transfers between devices: 7.45 us -> 35.7 us
  waiting for transfers between devices: 22.9 us -> 36.3 us
  Pallas kernels: 0 us -> 5.56 us
    all_gather x3 -> x0, blocking collectives: 68.6 us -> none  [body(): lax.all_gather(extrapolated, 'row', axis=0, tiled=True)]
    scatter-add x6 -> x0, other arithmetic: 57.2 us -> none  [the longest x3 30.9 us: body(): jax.ops.segment_sum(partial_value, tile_col, num_segments=column_blocks)]
    all_to_all x2 -> x0, blocking collectives: 56.2 us -> none  [body(): lax.all_to_all(local_sums, 'row', split_axis=0, concat_axis=0, tiled=True)]
    ppermute x0 -> x28, waiting for transfers between devices: none -> 36.3 us  [swap(): return lax.ppermute(x, 'row', [(i, i ^ mask) for i in range(devices)])]
    ppermute x0 -> x28, starting transfers between devices: none -> 35.7 us  [swap(): return lax.ppermute(x, 'row', [(i, i ^ mask) for i in range(devices)])]
    dot_general x6 -> x0, local copies, waits for them, and re-layouts: 33.6 us -> none  [the longest x3 16.8 us: body(): jnp.einsum('tij,tjs->tis', tile_values, chosen, preferred_element_type=jn...]
    dot_general x6 -> x0, matrix products: 29.3 us -> none  [the longest x3 15.9 us: body(): jnp.einsum('tij,tjs->tis', tile_values, chosen, preferred_element_type=jn...]
    all_to_all x1 -> x0, waiting for transfers between devices: 22.9 us -> none  [body(): lax.all_to_all(local_sums, 'row', split_axis=0, concat_axis=0, tiled=True)]
  transfers between devices with their start and end apart: 1 -> 28, of which waited for: 1 -> 17; matrix products, arithmetic and copies ran while one was open for 0% -> 3% of each run, Pallas kernels for 0% -> 0%
where the time goes in v1:
time: 84.8 us; the launch traced here: 84.6 us
  waiting for transfers between devices  36.3 us (43%)
  starting transfers between devices  35.7 us (42%)
  Pallas kernels  5.56 us (7%)
  local copies, waits for them, and re-layouts  5.13 us (6%)
  other arithmetic  1.05 us (1%)
  between operations  0.85 us (1%)
    ppermute x28, waiting for transfers between devices, swap(): return lax.ppermute(x, 'row', [(i, i ^ mask) for i in range(devices)])  36.3 us
    ppermute x28, starting transfers between devices, swap(): return lax.ppermute(x, 'row', [(i, i ^ mask) for i in range(devices)])  35.7 us
    unnamed x27, local copies, waits for them, and re-layouts  5.12 us
    pallas_call x3, Pallas kernels, body(): pl.pallas_call(functools.partial(row_kernel, groups), out_shape=image_sha...  2.07 us
    pallas_call x3, Pallas kernels, body(): pl.pallas_call(functools.partial(column_kernel, first, groups), out_shape...  1.98 us
  transfers between devices with their start and end apart: 28, of which 17 were waited for; matrix products, arithmetic and copies ran while one was open for 3% of the time, Pallas kernels for 0%

profile of v1, /device:TPU:0, one launch (start us, length us, event | category | flops | bytes accessed | tf_op | source)
XLA Modules:
  0.0 84.6 jit_solution(3108752713444189146)
XLA Ops:
  8.5 3.0 %collective-permute-start.3 = (bf16[128,256]{1,0:T(8,128)(2,1)S(1)}, bf16[128,256]{1,0:T(8,128)(2,1)S(1)}, u32[]{:S(2)}, u32[]{:S(2)}) collective-permute-start(bf16[128,256]{1,0:T(8,128)(2,1)S(1)} %get-tuple-element.22), channel_id=1, source_target_pairs={{0,4},{1,5},{2,6},{3,7},{4,0},{5,1},{6,2},{7,3},{8,12},{9,13},{10,... | collective-permute-start | bytes 196616 | tf_op jit(solution)/shard_map/ppermute | solution.py:129
  11.6 2.6 %collective-permute-start.4 = (bf16[128,256]{1,0:T(8,128)(2,1)S(1)}, bf16[128,256]{1,0:T(8,128)(2,1)S(1)}, u32[]{:S(2)}, u32[]{:S(2)}) collective-permute-start(bf16[128,256]{1,0:T(8,128)(2,1)S(1)} %get-tuple-element.23), channel_id=1, source_target_pairs={{0,8},{1,9},{2,10},{3,11},{4,12},{5,13},{6,14},{7,15},{8,0},{9,1},... | collective-permute-start | bytes 196616 | tf_op jit(solution)/shard_map/ppermute | solution.py:129
  14.2 1.8 %collective-permute-start = (f32[264,128]{1,0:T(8,128)S(1)}, f32[264,128]{1,0:T(8,128)S(1)}, u32[]{:S(2)}, u32[]{:S(2)}) collective-permute-start(f32[264,128]{1,0:T(8,128)S(1)} %pad_maximum_fusion), channel_id=1, source_target_pairs={{0,2},{1,3},{2,0},{3,1},{4,6},{5,7},{6,4},{7,5},{8,10},{9,11},{10,... | collective-permute-start | bytes 405512 | tf_op jit(solution)/shard_map/ppermute | solution.py:129
  16.0 3.1 %collective-permute-done.4 = bf16[128,256]{1,0:T(8,128)(2,1)S(1)} collective-permute-done((bf16[128,256]{1,0:T(8,128)(2,1)S(1)}, bf16[128,256]{1,0:T(8,128)(2,1)S(1)}, u32[]{:S(2)}, u32[]{:S(2)}) %collective-permute-start.4) | collective-permute-done | bytes 65568 | tf_op jit(solution)/shard_map/ppermute | solution.py:129
  20.4 1.6 %collective-permute-start.6 = (bf16[128,256]{1,0:T(8,128)(2,1)S(1)}, bf16[128,256]{1,0:T(8,128)(2,1)S(1)}, u32[]{:S(2)}, u32[]{:S(2)}) collective-permute-start(bf16[128,256]{1,0:T(8,128)(2,1)S(1)} %fusion.6), channel_id=1, source_target_pairs={{0,2},{1,3},{2,0},{3,1},{4,6},{5,7},{6,4},{7,5},{8,10},{9,11},{10,... | collective-permute-start | bytes 196616 | tf_op jit(solution)/shard_map/ppermute | solution.py:129
  22.0 2.7 %collective-permute-done.6 = bf16[128,256]{1,0:T(8,128)(2,1)S(1)} collective-permute-done((bf16[128,256]{1,0:T(8,128)(2,1)S(1)}, bf16[128,256]{1,0:T(8,128)(2,1)S(1)}, u32[]{:S(2)}, u32[]{:S(2)}) %collective-permute-start.6) | collective-permute-done | bytes 65568 | tf_op jit(solution)/shard_map/ppermute | solution.py:129
  24.8 2.0 %collective-permute-start.10 = (bf16[128,256]{1,0:T(8,128)(2,1)S(1)}, bf16[128,256]{1,0:T(8,128)(2,1)S(1)}, u32[]{:S(2)}, u32[]{:S(2)}) collective-permute-start(bf16[128,256]{1,0:T(8,128)(2,1)S(1)} %get-tuple-element.42.refs_0_), channel_id=1, source_target_pairs={{0,12},{1,13},{2,14},{3,15},{4,8},{5,9},{6,10},{7,11},{8,4},{9,5},... | collective-permute-start | bytes 196616 | tf_op jit(solution)/shard_map/ppermute | solution.py:129
  27.1 2.1 %collective-permute-start.8 = (bf16[128,256]{1,0:T(8,128)(2,1)S(1)}, bf16[128,256]{1,0:T(8,128)(2,1)S(1)}, u32[]{:S(2)}, u32[]{:S(2)}) collective-permute-start(bf16[128,256]{1,0:T(8,128)(2,1)S(1)} %get-tuple-element.42.refs_0_), channel_id=1, source_target_pairs={{0,4},{1,5},{2,6},{3,7},{4,0},{5,1},{6,2},{7,3},{8,12},{9,13},{10,... | collective-permute-start | bytes 196616 | tf_op jit(solution)/shard_map/ppermute | solution.py:129
  29.2 1.7 %collective-permute-done.10.refs_3_ = bf16[128,256]{1,0:T(8,128)(2,1)S(1)} collective-permute-done((bf16[128,256]{1,0:T(8,128)(2,1)S(1)}, bf16[128,256]{1,0:T(8,128)(2,1)S(1)}, u32[]{:S(2)}, u32[]{:S(2)}) %collective-permute-start.10) | collective-permute-done | bytes 65568 | tf_op jit(solution)/shard_map/ppermute | solution.py:129
  38.1 1.8 %collective-permute-start.14 = (bf16[128,256]{1,0:T(8,128)(2,1)S(1)}, bf16[128,256]{1,0:T(8,128)(2,1)S(1)}, u32[]{:S(2)}, u32[]{:S(2)}) collective-permute-start(bf16[128,256]{1,0:T(8,128)(2,1)S(1)} %get-tuple-element.28), channel_id=1, source_target_pairs={{0,12},{1,13},{2,14},{3,15},{4,8},{5,9},{6,10},{7,11},{8,4},{9,5},... | collective-permute-start | bytes 196616 | tf_op jit(solution)/shard_map/ppermute | solution.py:129
  39.9 4.9 %collective-permute-done.13 = bf16[128,256]{1,0:T(8,128)(2,1)S(1)} collective-permute-done((bf16[128,256]{1,0:T(8,128)(2,1)S(1)}, bf16[128,256]{1,0:T(8,128)(2,1)S(1)}, u32[]{:S(2)}, u32[]{:S(2)}) %collective-permute-start.13) | collective-permute-done | bytes 65568 | tf_op jit(solution)/shard_map/ppermute | solution.py:129
  46.4 2.7 %collective-permute-done.15 = bf16[128,256]{1,0:T(8,128)(2,1)S(1)} collective-permute-done((bf16[128,256]{1,0:T(8,128)(2,1)S(1)}, bf16[128,256]{1,0:T(8,128)(2,1)S(1)}, u32[]{:S(2)}, u32[]{:S(2)}) %collective-permute-start.15) | collective-permute-done | bytes 65568 | tf_op jit(solution)/shard_map/ppermute | solution.py:129
  49.3 2.0 %collective-permute-start.18 = (bf16[128,256]{1,0:T(8,128)(2,1)S(1)}, bf16[128,256]{1,0:T(8,128)(2,1)S(1)}, u32[]{:S(2)}, u32[]{:S(2)}) collective-permute-start(bf16[128,256]{1,0:T(8,128)(2,1)S(1)} %get-tuple-element.40.refs_0_), channel_id=1, source_target_pairs={{0,12},{1,13},{2,14},{3,15},{4,8},{5,9},{6,10},{7,11},{8,4},{9,5},... | collective-permute-start | bytes 196616 | tf_op jit(solution)/shard_map/ppermute | solution.py:129
  52.0 1.7 %collective-permute-start.16 = (bf16[128,256]{1,0:T(8,128)(2,1)S(1)}, bf16[128,256]{1,0:T(8,128)(2,1)S(1)}, u32[]{:S(2)}, u32[]{:S(2)}) collective-permute-start(bf16[128,256]{1,0:T(8,128)(2,1)S(1)} %get-tuple-element.40.refs_0_), channel_id=1, source_target_pairs={{0,4},{1,5},{2,6},{3,7},{4,0},{5,1},{6,2},{7,3},{8,12},{9,13},{10,... | collective-permute-start | bytes 196616 | tf_op jit(solution)/shard_map/ppermute | solution.py:129
  53.7 1.7 %collective-permute-done.18.refs_3_ = bf16[128,256]{1,0:T(8,128)(2,1)S(1)} collective-permute-done((bf16[128,256]{1,0:T(8,128)(2,1)S(1)}, bf16[128,256]{1,0:T(8,128)(2,1)S(1)}, u32[]{:S(2)}, u32[]{:S(2)}) %collective-permute-start.18) | collective-permute-done | bytes 65568 | tf_op jit(solution)/shard_map/ppermute | solution.py:129
  55.4 1.6 %collective-permute-done.17.refs_2_ = bf16[128,256]{1,0:T(8,128)(2,1)S(1)} collective-permute-done((bf16[128,256]{1,0:T(8,128)(2,1)S(1)}, bf16[128,256]{1,0:T(8,128)(2,1)S(1)}, u32[]{:S(2)}, u32[]{:S(2)}) %collective-permute-start.17) | collective-permute-done | bytes 65568 | tf_op jit(solution)/shard_map/ppermute | solution.py:129
  61.3 1.6 %collective-permute-start.21 = (bf16[128,256]{1,0:T(8,128)(2,1)S(1)}, bf16[128,256]{1,0:T(8,128)(2,1)S(1)}, u32[]{:S(2)}, u32[]{:S(2)}) collective-permute-start(bf16[128,256]{1,0:T(8,128)(2,1)S(1)} %get-tuple-element.33), channel_id=1, source_target_pairs={{0,8},{1,9},{2,10},{3,11},{4,12},{5,13},{6,14},{7,15},{8,0},{9,1},... | collective-permute-start | bytes 196616 | tf_op jit(solution)/shard_map/ppermute | solution.py:129
  62.9 1.8 %collective-permute-start.22 = (bf16[128,256]{1,0:T(8,128)(2,1)S(1)}, bf16[128,256]{1,0:T(8,128)(2,1)S(1)}, u32[]{:S(2)}, u32[]{:S(2)}) collective-permute-start(bf16[128,256]{1,0:T(8,128)(2,1)S(1)} %get-tuple-element.34), channel_id=1, source_target_pairs={{0,12},{1,13},{2,14},{3,15},{4,8},{5,9},{6,10},{7,11},{8,4},{9,5},... | collective-permute-start | bytes 196616 | tf_op jit(solution)/shard_map/ppermute | solution.py:129
  64.7 4.8 %collective-permute-done.21 = bf16[128,256]{1,0:T(8,128)(2,1)S(1)} collective-permute-done((bf16[128,256]{1,0:T(8,128)(2,1)S(1)}, bf16[128,256]{1,0:T(8,128)(2,1)S(1)}, u32[]{:S(2)}, u32[]{:S(2)}) %collective-permute-start.21) | collective-permute-done | bytes 65568 | tf_op jit(solution)/shard_map/ppermute | solution.py:129
  71.2 2.7 %collective-permute-done.23 = bf16[128,256]{1,0:T(8,128)(2,1)S(1)} collective-permute-done((bf16[128,256]{1,0:T(8,128)(2,1)S(1)}, bf16[128,256]{1,0:T(8,128)(2,1)S(1)}, u32[]{:S(2)}, u32[]{:S(2)}) %collective-permute-start.23) | collective-permute-done | bytes 65568 | tf_op jit(solution)/shard_map/ppermute | solution.py:129
  74.0 2.1 %collective-permute-start.26 = (bf16[128,256]{1,0:T(8,128)(2,1)S(1)}, bf16[128,256]{1,0:T(8,128)(2,1)S(1)}, u32[]{:S(2)}, u32[]{:S(2)}) collective-permute-start(bf16[128,256]{1,0:T(8,128)(2,1)S(1)} %get-tuple-element.38.refs_0_), channel_id=1, source_target_pairs={{0,12},{1,13},{2,14},{3,15},{4,8},{5,9},{6,10},{7,11},{8,4},{9,5},... | collective-permute-start | bytes 196616 | tf_op jit(solution)/shard_map/ppermute | solution.py:129
  76.8 1.7 %collective-permute-start.24 = (bf16[128,256]{1,0:T(8,128)(2,1)S(1)}, bf16[128,256]{1,0:T(8,128)(2,1)S(1)}, u32[]{:S(2)}, u32[]{:S(2)}) collective-permute-start(bf16[128,256]{1,0:T(8,128)(2,1)S(1)} %get-tuple-element.38.refs_0_), channel_id=1, source_target_pairs={{0,4},{1,5},{2,6},{3,7},{4,0},{5,1},{6,2},{7,3},{8,12},{9,13},{10,... | collective-permute-start | bytes 196616 | tf_op jit(solution)/shard_map/ppermute | solution.py:129
  78.5 1.7 %collective-permute-done.26.refs_3_ = bf16[128,256]{1,0:T(8,128)(2,1)S(1)} collective-permute-done((bf16[128,256]{1,0:T(8,128)(2,1)S(1)}, bf16[128,256]{1,0:T(8,128)(2,1)S(1)}, u32[]{:S(2)}, u32[]{:S(2)}) %collective-permute-start.26) | collective-permute-done | bytes 65568 | tf_op jit(solution)/shard_map/ppermute | solution.py:129
  80.1 1.6 %collective-permute-done.25.refs_2_ = bf16[128,256]{1,0:T(8,128)(2,1)S(1)} collective-permute-done((bf16[128,256]{1,0:T(8,128)(2,1)S(1)}, bf16[128,256]{1,0:T(8,128)(2,1)S(1)}, u32[]{:S(2)}, u32[]{:S(2)}) %collective-permute-start.25) | collective-permute-done | bytes 65568 | tf_op jit(solution)/shard_map/ppermute | solution.py:129
  (79 shorter events, 28.7 us)
Async XLA Ops:
  5.1 3.0 %collective-permute-start.1 = (bf16[2,4,256,256]{3,2,1,0:T(8,128)(2,1)S(1)}, bf16[2,4,256,256]{3,2,1,0:T(8,128)(2,1)S(1)}, u32[]{:S(2)}, u32[]{:S(2)}) collective-permute-start(bf16[2,4,256,256]{3,2,1,0:T(8,128)(2,1)S(1)} %get-tuple-element.20), channel_id=1, source_target_pairs={{0,1},{1,0},{2,3},{3,2},{4,5},{5,4},{6,7},{7,6},{8,9},{9,8},{10,11... | collective-permute-start | bytes 3145736 | tf_op jit(solution)/shard_map/ppermute | solution.py:129
  5.6 2.5 %collective-permute-start.2 = (f32[256,128]{1,0:T(8,128)S(1)}, f32[256,128]{1,0:T(8,128)S(1)}, u32[]{:S(2)}, u32[]{:S(2)}) collective-permute-start(f32[256,128]{1,0:T(8,128)S(1)} %copy-done.2), channel_id=1, source_target_pairs={{0,1},{1,0},{2,3},{3,2},{4,5},{5,4},{6,7},{7,6},{8,9},{9,8},{10,11... | collective-permute-start | bytes 393224 | tf_op jit(solution)/shard_map/ppermute | solution.py:129
  8.5 7.5 %collective-permute-start.3 = (bf16[128,256]{1,0:T(8,128)(2,1)S(1)}, bf16[128,256]{1,0:T(8,128)(2,1)S(1)}, u32[]{:S(2)}, u32[]{:S(2)}) collective-permute-start(bf16[128,256]{1,0:T(8,128)(2,1)S(1)} %get-tuple-element.22), channel_id=1, source_target_pairs={{0,4},{1,5},{2,6},{3,7},{4,0},{5,1},{6,2},{7,3},{8,12},{9,13},{10,... | collective-permute-start | bytes 196616 | tf_op jit(solution)/shard_map/ppermute | solution.py:129
  11.6 7.5 %collective-permute-start.4 = (bf16[128,256]{1,0:T(8,128)(2,1)S(1)}, bf16[128,256]{1,0:T(8,128)(2,1)S(1)}, u32[]{:S(2)}, u32[]{:S(2)}) collective-permute-start(bf16[128,256]{1,0:T(8,128)(2,1)S(1)} %get-tuple-element.23), channel_id=1, source_target_pairs={{0,8},{1,9},{2,10},{3,11},{4,12},{5,13},{6,14},{7,15},{8,0},{9,1},... | collective-permute-start | bytes 196616 | tf_op jit(solution)/shard_map/ppermute | solution.py:129
  14.1 6.2 %collective-permute-start.5 = (bf16[128,256]{1,0:T(8,128)(2,1)S(1)}, bf16[128,256]{1,0:T(8,128)(2,1)S(1)}, u32[]{:S(2)}, u32[]{:S(2)}) collective-permute-start(bf16[128,256]{1,0:T(8,128)(2,1)S(1)} %get-tuple-element.24), channel_id=1, source_target_pairs={{0,12},{1,13},{2,14},{3,15},{4,8},{5,9},{6,10},{7,11},{8,4},{9,5},... | collective-permute-start | bytes 196616 | tf_op jit(solution)/shard_map/ppermute | solution.py:129
  14.2 7.8 %collective-permute-start = (f32[264,128]{1,0:T(8,128)S(1)}, f32[264,128]{1,0:T(8,128)S(1)}, u32[]{:S(2)}, u32[]{:S(2)}) collective-permute-start(f32[264,128]{1,0:T(8,128)S(1)} %pad_maximum_fusion), channel_id=1, source_target_pairs={{0,2},{1,3},{2,0},{3,1},{4,6},{5,7},{6,4},{7,5},{8,10},{9,11},{10,... | collective-permute-start | bytes 405512 | tf_op jit(solution)/shard_map/ppermute | solution.py:129
  20.4 4.3 %collective-permute-start.6 = (bf16[128,256]{1,0:T(8,128)(2,1)S(1)}, bf16[128,256]{1,0:T(8,128)(2,1)S(1)}, u32[]{:S(2)}, u32[]{:S(2)}) collective-permute-start(bf16[128,256]{1,0:T(8,128)(2,1)S(1)} %fusion.6), channel_id=1, source_target_pairs={{0,2},{1,3},{2,0},{3,1},{4,6},{5,7},{6,4},{7,5},{8,10},{9,11},{10,... | collective-permute-start | bytes 196616 | tf_op jit(solution)/shard_map/ppermute | solution.py:129
  24.8 6.1 %collective-permute-start.10 = (bf16[128,256]{1,0:T(8,128)(2,1)S(1)}, bf16[128,256]{1,0:T(8,128)(2,1)S(1)}, u32[]{:S(2)}, u32[]{:S(2)}) collective-permute-start(bf16[128,256]{1,0:T(8,128)(2,1)S(1)} %get-tuple-element.42.refs_0_), channel_id=1, source_target_pairs={{0,12},{1,13},{2,14},{3,15},{4,8},{5,9},{6,10},{7,11},{8,4},{9,5},... | collective-permute-start | bytes 196616 | tf_op jit(solution)/shard_map/ppermute | solution.py:129
  26.8 5.7 %collective-permute-start.9 = (bf16[128,256]{1,0:T(8,128)(2,1)S(1)}, bf16[128,256]{1,0:T(8,128)(2,1)S(1)}, u32[]{:S(2)}, u32[]{:S(2)}) collective-permute-start(bf16[128,256]{1,0:T(8,128)(2,1)S(1)} %get-tuple-element.42.refs_0_), channel_id=1, source_target_pairs={{0,8},{1,9},{2,10},{3,11},{4,12},{5,13},{6,14},{7,15},{8,0},{9,1},... | collective-permute-start | bytes 196616 | tf_op jit(solution)/shard_map/ppermute | solution.py:129
  27.1 5.4 %collective-permute-start.8 = (bf16[128,256]{1,0:T(8,128)(2,1)S(1)}, bf16[128,256]{1,0:T(8,128)(2,1)S(1)}, u32[]{:S(2)}, u32[]{:S(2)}) collective-permute-start(bf16[128,256]{1,0:T(8,128)(2,1)S(1)} %get-tuple-element.42.refs_0_), channel_id=1, source_target_pairs={{0,4},{1,5},{2,6},{3,7},{4,0},{5,1},{6,2},{7,3},{8,12},{9,13},{10,... | collective-permute-start | bytes 196616 | tf_op jit(solution)/shard_map/ppermute | solution.py:129
  35.5 4.5 %collective-permute-start.12 = (bf16[128,256]{1,0:T(8,128)(2,1)S(1)}, bf16[128,256]{1,0:T(8,128)(2,1)S(1)}, u32[]{:S(2)}, u32[]{:S(2)}) collective-permute-start(bf16[128,256]{1,0:T(8,128)(2,1)S(1)} %get-tuple-element.26), channel_id=1, source_target_pairs={{0,4},{1,5},{2,6},{3,7},{4,0},{5,1},{6,2},{7,3},{8,12},{9,13},{10,... | collective-permute-start | bytes 196616 | tf_op jit(solution)/shard_map/ppermute | solution.py:129
  36.5 8.3 %collective-permute-start.13 = (bf16[128,256]{1,0:T(8,128)(2,1)S(1)}, bf16[128,256]{1,0:T(8,128)(2,1)S(1)}, u32[]{:S(2)}, u32[]{:S(2)}) collective-permute-start(bf16[128,256]{1,0:T(8,128)(2,1)S(1)} %get-tuple-element.27), channel_id=1, source_target_pairs={{0,8},{1,9},{2,10},{3,11},{4,12},{5,13},{6,14},{7,15},{8,0},{9,1},... | collective-permute-start | bytes 196616 | tf_op jit(solution)/shard_map/ppermute | solution.py:129
  38.1 6.7 %collective-permute-start.14 = (bf16[128,256]{1,0:T(8,128)(2,1)S(1)}, bf16[128,256]{1,0:T(8,128)(2,1)S(1)}, u32[]{:S(2)}, u32[]{:S(2)}) collective-permute-start(bf16[128,256]{1,0:T(8,128)(2,1)S(1)} %get-tuple-element.28), channel_id=1, source_target_pairs={{0,12},{1,13},{2,14},{3,15},{4,8},{5,9},{6,10},{7,11},{8,4},{9,5},... | collective-permute-start | bytes 196616 | tf_op jit(solution)/shard_map/ppermute | solution.py:129
  44.8 4.3 %collective-permute-start.15 = (bf16[128,256]{1,0:T(8,128)(2,1)S(1)}, bf16[128,256]{1,0:T(8,128)(2,1)S(1)}, u32[]{:S(2)}, u32[]{:S(2)}) collective-permute-start(bf16[128,256]{1,0:T(8,128)(2,1)S(1)} %fusion.7), channel_id=1, source_target_pairs={{0,2},{1,3},{2,0},{3,1},{4,6},{5,7},{6,4},{7,5},{8,10},{9,11},{10,... | collective-permute-start | bytes 196616 | tf_op jit(solution)/shard_map/ppermute | solution.py:129
  49.3 6.1 %collective-permute-start.18 = (bf16[128,256]{1,0:T(8,128)(2,1)S(1)}, bf16[128,256]{1,0:T(8,128)(2,1)S(1)}, u32[]{:S(2)}, u32[]{:S(2)}) collective-permute-start(bf16[128,256]{1,0:T(8,128)(2,1)S(1)} %get-tuple-element.40.refs_0_), channel_id=1, source_target_pairs={{0,12},{1,13},{2,14},{3,15},{4,8},{5,9},{6,10},{7,11},{8,4},{9,5},... | collective-permute-start | bytes 196616 | tf_op jit(solution)/shard_map/ppermute | solution.py:129
  51.3 5.7 %collective-permute-start.17 = (bf16[128,256]{1,0:T(8,128)(2,1)S(1)}, bf16[128,256]{1,0:T(8,128)(2,1)S(1)}, u32[]{:S(2)}, u32[]{:S(2)}) collective-permute-start(bf16[128,256]{1,0:T(8,128)(2,1)S(1)} %get-tuple-element.40.refs_0_), channel_id=1, source_target_pairs={{0,8},{1,9},{2,10},{3,11},{4,12},{5,13},{6,14},{7,15},{8,0},{9,1},... | collective-permute-start | bytes 196616 | tf_op jit(solution)/shard_map/ppermute | solution.py:129
  52.0 5.0 %collective-permute-start.16 = (bf16[128,256]{1,0:T(8,128)(2,1)S(1)}, bf16[128,256]{1,0:T(8,128)(2,1)S(1)}, u32[]{:S(2)}, u32[]{:S(2)}) collective-permute-start(bf16[128,256]{1,0:T(8,128)(2,1)S(1)} %get-tuple-element.40.refs_0_), channel_id=1, source_target_pairs={{0,4},{1,5},{2,6},{3,7},{4,0},{5,1},{6,2},{7,3},{8,12},{9,13},{10,... | collective-permute-start | bytes 196616 | tf_op jit(solution)/shard_map/ppermute | solution.py:129
  60.3 4.4 %collective-permute-start.20 = (bf16[128,256]{1,0:T(8,128)(2,1)S(1)}, bf16[128,256]{1,0:T(8,128)(2,1)S(1)}, u32[]{:S(2)}, u32[]{:S(2)}) collective-permute-start(bf16[128,256]{1,0:T(8,128)(2,1)S(1)} %get-tuple-element.32), channel_id=1, source_target_pairs={{0,4},{1,5},{2,6},{3,7},{4,0},{5,1},{6,2},{7,3},{8,12},{9,13},{10,... | collective-permute-start | bytes 196616 | tf_op jit(solution)/shard_map/ppermute | solution.py:129
  61.3 8.3 %collective-permute-start.21 = (bf16[128,256]{1,0:T(8,128)(2,1)S(1)}, bf16[128,256]{1,0:T(8,128)(2,1)S(1)}, u32[]{:S(2)}, u32[]{:S(2)}) collective-permute-start(bf16[128,256]{1,0:T(8,128)(2,1)S(1)} %get-tuple-element.33), channel_id=1, source_target_pairs={{0,8},{1,9},{2,10},{3,11},{4,12},{5,13},{6,14},{7,15},{8,0},{9,1},... | collective-permute-start | bytes 196616 | tf_op jit(solution)/shard_map/ppermute | solution.py:129
  62.9 6.7 %collective-permute-start.22 = (bf16[128,256]{1,0:T(8,128)(2,1)S(1)}, bf16[128,256]{1,0:T(8,128)(2,1)S(1)}, u32[]{:S(2)}, u32[]{:S(2)}) collective-permute-start(bf16[128,256]{1,0:T(8,128)(2,1)S(1)} %get-tuple-element.34), channel_id=1, source_target_pairs={{0,12},{1,13},{2,14},{3,15},{4,8},{5,9},{6,10},{7,11},{8,4},{9,5},... | collective-permute-start | bytes 196616 | tf_op jit(solution)/shard_map/ppermute | solution.py:129
  69.6 4.3 %collective-permute-start.23 = (bf16[128,256]{1,0:T(8,128)(2,1)S(1)}, bf16[128,256]{1,0:T(8,128)(2,1)S(1)}, u32[]{:S(2)}, u32[]{:S(2)}) collective-permute-start(bf16[128,256]{1,0:T(8,128)(2,1)S(1)} %fusion.8), channel_id=1, source_target_pairs={{0,2},{1,3},{2,0},{3,1},{4,6},{5,7},{6,4},{7,5},{8,10},{9,11},{10,... | collective-permute-start | bytes 196616 | tf_op jit(solution)/shard_map/ppermute | solution.py:129
  74.0 6.1 %collective-permute-start.26 = (bf16[128,256]{1,0:T(8,128)(2,1)S(1)}, bf16[128,256]{1,0:T(8,128)(2,1)S(1)}, u32[]{:S(2)}, u32[]{:S(2)}) collective-permute-start(bf16[128,256]{1,0:T(8,128)(2,1)S(1)} %get-tuple-element.38.refs_0_), channel_id=1, source_target_pairs={{0,12},{1,13},{2,14},{3,15},{4,8},{5,9},{6,10},{7,11},{8,4},{9,5},... | collective-permute-start | bytes 196616 | tf_op jit(solution)/shard_map/ppermute | solution.py:129
  76.1 5.7 %collective-permute-start.25 = (bf16[128,256]{1,0:T(8,128)(2,1)S(1)}, bf16[128,256]{1,0:T(8,128)(2,1)S(1)}, u32[]{:S(2)}, u32[]{:S(2)}) collective-permute-start(bf16[128,256]{1,0:T(8,128)(2,1)S(1)} %get-tuple-element.38.refs_0_), channel_id=1, source_target_pairs={{0,8},{1,9},{2,10},{3,11},{4,12},{5,13},{6,14},{7,15},{8,0},{9,1},... | collective-permute-start | bytes 196616 | tf_op jit(solution)/shard_map/ppermute | solution.py:129
  76.8 5.0 %collective-permute-start.24 = (bf16[128,256]{1,0:T(8,128)(2,1)S(1)}, bf16[128,256]{1,0:T(8,128)(2,1)S(1)}, u32[]{:S(2)}, u32[]{:S(2)}) collective-permute-start(bf16[128,256]{1,0:T(8,128)(2,1)S(1)} %get-tuple-element.38.refs_0_), channel_id=1, source_target_pairs={{0,4},{1,5},{2,6},{3,7},{4,0},{5,1},{6,2},{7,3},{8,12},{9,13},{10,... | collective-permute-start | bytes 196616 | tf_op jit(solution)/shard_map/ppermute | solution.py:129
  (16 other events, 81.8 us)

commit v2 on v0

v2 whole, which is shorter than its diff:
```python
import functools

import jax
import jax.numpy as jnp
from jax import lax
from jax.experimental import pallas as pl
from jax.experimental.pallas import tpu as pltpu
from jax.sharding import PartitionSpec as P

ITERS = 3
STEP = 0.4
CORES = 2
QUAD = 4
UNIT = CORES * QUAD
VMEM = pl.BlockSpec(memory_space=pltpu.VMEM)
SMEM = pl.BlockSpec(memory_space=pltpu.SMEM)
F32, BF16 = jnp.float32, jnp.bfloat16


def params(limit=32 * 2**20):
    return pltpu.CompilerParams(vmem_limit_bytes=limit)


def place():
    me = lax.axis_index("row")
    return me // UNIT, (me // CORES) % QUAD, me % CORES


def swap(x, mask):
    return lax.ppermute(x, "row", [(i, i ^ mask) for i in range(lax.axis_size("row"))])


def dot(a, b, over_a, over_b):
    return lax.dot_general(
        a, b, (((over_a,), (over_b,)), ((), ())), preferred_element_type=F32
    )


def dense_kernel(span, at_ref, tile_ref, out_ref, acc):
    tiles, size, _ = tile_ref.shape
    row_blocks = out_ref.shape[2] // size
    acc[...] = jnp.zeros_like(acc)

    def add(t, _):
        at = at_ref[t]
        acc[at] = acc[at] + tile_ref[t].astype(F32)
        return 0

    lax.fori_loop(0, tiles, add, 0, unroll=4)
    for column in range(acc.shape[0] // row_blocks):
        owner, s = divmod(column, span)
        far, q, core = owner // UNIT, (owner // CORES) % QUAD, owner % CORES
        cols = pl.ds(((far * CORES + core) * span + s) * size, size)
        for r in range(row_blocks):
            block = acc[column * row_blocks + r]
            high = block.astype(BF16)
            rows = pl.ds(r * size, size)
            out_ref[0, q, rows, cols] = high
            out_ref[1, q, rows, cols] = (block - high.astype(F32)).astype(BF16)


def dense(tile_values, at, span, row_blocks, columns):
    size = tile_values.shape[1]
    wide = columns * size // QUAD
    return pl.pallas_call(
        functools.partial(dense_kernel, span),
        out_shape=jax.ShapeDtypeStruct((2, QUAD, row_blocks * size, wide), BF16),
        in_specs=[SMEM, VMEM],
        out_specs=VMEM,
        scratch_shapes=[pltpu.VMEM((columns * row_blocks, size, size), F32)],
        compiler_params=params(),
    )(at, tile_values)


def variables_kernel(*refs):
    packs, (primal_ref, cost_ref, limit_ref) = refs[:-3], refs[-3:]
    far, _, core = place()
    width = (packs[0].shape[0] - 8) // 2
    half = primal_ref.shape[0]
    for j, ref in enumerate(packs):
        owner = (far * CORES + core) ^ j
        cols = pl.ds(pl.multiple_of(owner * width, width), width)
        for base, out in ((0, primal_ref), (width, cost_ref)):
            turned = ref[base : base + width].T
            out[:, cols] = jnp.where(core == 0, turned[:half], turned[half:])
        limit_ref[:, cols] = ref[2 * width : 2 * width + 1]


def column_kernel(first, *refs):
    a, duals = refs[0:2], refs[2:4]
    if first:
        bounds, images, stepped, pieces = None, None, None, refs[4:]
    else:
        bounds, images, stepped, pieces = refs[4:6], refs[6:8], refs[8:10], refs[10:]
    low = []
    for i in range(2):
        new = duals[i][...]
        if not first:
            new = jnp.maximum(new + STEP * (bounds[i][...] - images[i][...]), 0.0)
            stepped[i][...] = new
        low.append(new.astype(BF16).T)
    me = place()[1]
    for k in range(QUAD):
        total = None
        for i in range(2):
            for h in range(2):
                part = dot(low[i], a[i][h, me ^ k], 1, 0)
                total = part if total is None else total + part
        pieces[k][...] = total.astype(pieces[k].dtype)


def row_kernel(*refs):
    a, pieces, images = refs[0:2], refs[2 : 2 + QUAD], refs[2 + QUAD :]
    me = place()[1]
    for i in range(len(images)):
        total = None
        for k in range(QUAD):
            for h in range(2):
                part = dot(a[i][h, me ^ k], pieces[k][...], 1, 1)
                total = part if total is None else total + part
        images[i][...] = total


def body(
    tile_values, tile_row, tile_col, primal_start, objective, upper_bound, dual_start, row_bound
):
    devices = lax.axis_size("row")
    size = tile_values.shape[1]
    width, scenarios = primal_start.shape
    rows = dual_start.shape[0]
    half = scenarios // CORES
    span = width // size
    far_masks = []
    while UNIT << len(far_masks) < devices:
        far_masks.append(UNIT << len(far_masks))
    wide = devices * width // QUAD
    core = place()[2]

    at = tile_col * (rows // size) + tile_row
    make = functools.partial(
        dense, span=span, row_blocks=rows // size, columns=devices * span
    )
    a = (make(tile_values, at), make(swap(tile_values, 1), swap(at, 1)))

    pack = jnp.concatenate(
        [primal_start, objective, jnp.broadcast_to(upper_bound[:, None], (width, scenarios)).T[:8]], 0
    )
    packs = [pack]
    for mask in far_masks:
        packs = packs + [swap(p, mask) for p in packs]
    packs = [p for pair in zip(packs, [swap(p, 1) for p in packs]) for p in pair]
    state = jax.ShapeDtypeStruct((half, wide), F32)
    primal, cost, limit = pl.pallas_call(
        variables_kernel,
        out_shape=(state, state, jax.ShapeDtypeStruct((1, wide), F32)),
        in_specs=[VMEM] * len(packs),
        out_specs=(VMEM,) * 3,
        compiler_params=params(),
    )(*packs)

    def split(x):
        mine = jnp.where(core == 0, x[:, :half], x[:, half:])
        other = jnp.where(core == 0, x[:, half:], x[:, :half])
        return mine, swap(other, 1)

    duals, bounds = split(dual_start), split(row_bound)

    piece = jax.ShapeDtypeStruct((half, wide), BF16)
    side = jax.ShapeDtypeStruct((rows, half), F32)
    images = None
    for iteration in range(ITERS):
        first = iteration == 0
        operands = (*a, *duals)
        if not first:
            operands += (*bounds, *images)
        out = pl.pallas_call(
            functools.partial(column_kernel, first),
            out_shape=(() if first else (side, side)) + (state,) + (piece,) * (QUAD - 1),
            in_specs=[VMEM] * len(operands),
            out_specs=(VMEM,) * (QUAD + (0 if first else 2)),
            compiler_params=params(),
        )(*operands)
        if not first:
            duals, out = out[:2], out[2:]
        total = out[0]
        for k in range(1, QUAD):
            total = total + swap(out[k], k * CORES).astype(F32)
        for mask in far_masks:
            total = total + swap(total.astype(BF16), mask).astype(F32)
        updated = jnp.clip(primal - STEP * (cost - total), 0.0, limit)
        ahead = (2.0 * updated - primal).astype(BF16)
        primal = updated
        pieces = [ahead] + [swap(ahead, k * CORES) for k in range(1, QUAD)]
        images = pl.pallas_call(
            row_kernel,
            out_shape=(side, side),
            in_specs=[VMEM] * (2 + QUAD),
            out_specs=(VMEM,) * 2,
            compiler_params=params(),
        )(*a, *pieces)

    def join(mine, other):
        other = swap(other, 1)
        return jnp.where(
            core == 0, jnp.concatenate([mine, other], 1), jnp.concatenate([other, mine], 1)
        )

    place_at = (place()[0] * CORES + core) * width
    theirs = (place()[0] * CORES + 1 - core) * width
    primal = join(
        lax.dynamic_slice_in_dim(primal, place_at, width, 1).T,
        lax.dynamic_slice_in_dim(primal, theirs, width, 1).T,
    )
    last = [
        jnp.maximum(d + STEP * (b - i), 0.0)
        for d, b, i in zip(duals, bounds, images)
    ]
    return (primal, join(*last))


def solution(mesh):
    return jax.shard_map(
        body,
        mesh=mesh,
        in_specs=(
            P(("parts", "row"), None, None),
            P(("parts", "row")),
            P(("parts", "row")),
            P(("parts", "row"), None),
            P(("parts", "row"), None),
            P(("parts", "row")),
            P(("parts", "row"), None),
            P(("parts", "row"), None),
        ),
        out_specs=(P(("parts", "row"), None), P(("parts", "row"), None)),
        check_vma=False,
    )
```

time: 302 us -> 87.4 us (0.29)
  blocking collectives: 125 us -> 0 us
  other arithmetic: 66.9 us -> 3.94 us
  local copies, waits for them, and re-layouts: 47.9 us -> 4.6 us
  matrix products: 29.3 us -> 0 us
  starting transfers between devices: 7.45 us -> 27.8 us
  waiting for transfers between devices: 22.9 us -> 39.4 us
  Pallas kernels: 0 us -> 10.5 us
    all_gather x3 -> x0, blocking collectives: 68.6 us -> none  [body(): lax.all_gather(extrapolated, 'row', axis=0, tiled=True)]
    scatter-add x6 -> x0, other arithmetic: 57.2 us -> none  [the longest x3 30.9 us: body(): jax.ops.segment_sum(partial_value, tile_col, num_segments=column_blocks)]
    all_to_all x2 -> x0, blocking collectives: 56.2 us -> none  [body(): lax.all_to_all(local_sums, 'row', split_axis=0, concat_axis=0, tiled=True)]
    ppermute x0 -> x30, waiting for transfers between devices: none -> 39.4 us  [swap(): lax.ppermute(x, 'row', [(i, i ^ mask) for i in range(lax.axis_size('row'))])]
    dot_general x6 -> x0, local copies, waits for them, and re-layouts: 33.6 us -> none  [the longest x3 16.8 us: body(): jnp.einsum('tij,tjs->tis', tile_values, chosen, preferred_element_type=jn...]
    dot_general x6 -> x0, matrix products: 29.3 us -> none  [the longest x3 15.9 us: body(): jnp.einsum('tij,tjs->tis', tile_values, chosen, preferred_element_type=jn...]
    ppermute x0 -> x30, starting transfers between devices: none -> 27.8 us  [swap(): lax.ppermute(x, 'row', [(i, i ^ mask) for i in range(lax.axis_size('row'))])]
    all_to_all x1 -> x0, waiting for transfers between devices: 22.9 us -> none  [body(): lax.all_to_all(local_sums, 'row', split_axis=0, concat_axis=0, tiled=True)]
  transfers between devices with their start and end apart: 1 -> 30, of which waited for: 1 -> 22; matrix products, arithmetic and copies ran while one was open for 0% -> 5% of each run, Pallas kernels for 0% -> 7%
where the time goes in v2:
time: 87.4 us; the launch traced here: 87.1 us
  waiting for transfers between devices  39.4 us (45%)
  starting transfers between devices  27.8 us (32%)
  Pallas kernels  10.5 us (12%)
  local copies, waits for them, and re-layouts  4.6 us (5%)
  other arithmetic  3.94 us (5%)
  between operations  0.9 us (1%)
    ppermute x30, waiting for transfers between devices, swap(): lax.ppermute(x, 'row', [(i, i ^ mask) for i in range(lax.axis_size('row'))])  39.4 us
    ppermute x30, starting transfers between devices, swap(): lax.ppermute(x, 'row', [(i, i ^ mask) for i in range(lax.axis_size('row'))])  27.8 us
    pallas_call x2, Pallas kernels, dense(): pl.pallas_call(functools.partial(dense_kernel, span), out_shape=jax.Shape...  4.04 us
    unnamed x9, local copies, waits for them, and re-layouts  3.92 us
    pallas_call x3, Pallas kernels, body(): pl.pallas_call(row_kernel, out_shape=(side, side), in_specs=[VMEM] * (2 +...  3.65 us
    pallas_call x3, Pallas kernels, body(): pl.pallas_call(functools.partial(column_kernel, first), out_shape=(() if...  2.65 us
  transfers between devices with their start and end apart: 30, of which 22 were waited for; matrix products, arithmetic and copies ran while one was open for 5% of the time, Pallas kernels for 7%

profile of v2, /device:TPU:0, one launch (start us, length us, event | category | flops | bytes accessed | tf_op | source)
XLA Modules:
  0.0 87.1 jit_solution(14416140886075612604)
XLA Ops:
  3.9 4.1 %collective-permute-start.1 = (f32[264,128]{1,0:T(8,128)S(1)}, f32[264,128]{1,0:T(8,128)S(1)}, u32[]{:S(2)}, u32[]{:S(2)}) collective-permute-start(f32[264,128]{1,0:T(8,128)S(1)} %pad_maximum_fusion.refs_0_), channel_id=1, source_target_pairs={{0,8},{1,9},{2,10},{3,11},{4,12},{5,13},{6,14},{7,15},{8,0},{9,1},... | collective-permute-start | bytes 405512 | tf_op jit(solution)/shard_map/ppermute | solution.py:30
  8.7 1.6 %copy-done.2 = bf16[64,128,128]{2,1,0:T(8,128)(2,1)S(1)} copy-done((bf16[64,128,128]{2,1,0:T(8,128)(2,1)S(1)}, bf16[64,128,128]{2,1,0:T(8,128)(2,1)}, u32[]{:S(2)}) %copy-start.2) | copy-done | bytes 2097176
  10.3 1.5 %shard_map.96.refs_0_ = bf16[2,4,256,512]{3,2,1,0:T(8,128)(2,1)S(1)} custom-call(s32[64]{0:T(128)S(1)} %multiply_add_fusion.at_ref, bf16[64,128,128]{2,1,0:T(8,128)(2,1)S(1)} %copy-done.2), custom_call_target="tpu_custom_call" | custom-call | tf_op jit(solution)/shard_map/pallas_call | solution.py:65
  11.8 2.6 %shard_map.97.refs_1_ = bf16[2,4,256,512]{3,2,1,0:T(8,128)(2,1)S(1)} custom-call(s32[64]{0:T(128)S(1)} %collective-permute-done.3.at_ref, bf16[64,128,128]{2,1,0:T(8,128)(2,1)} %collective-permute-done.4.tile_ref), custom_call_target="tpu_custom_call" | custom-call | tf_op jit(solution)/shard_map/pallas_call | solution.py:65
  15.3 1.6 %collective-permute-start.6 = (bf16[64,512]{1,0:T(8,128)(2,1)S(1)}, bf16[64,512]{1,0:T(8,128)(2,1)S(1)}, u32[]{:S(2)}, u32[]{:S(2)}) collective-permute-start(bf16[64,512]{1,0:T(8,128)(2,1)S(1)} %get-tuple-element.31), channel_id=1, source_target_pairs={{0,2},{1,3},{2,0},{3,1},{4,6},{5,7},{6,4},{7,5},{8,10},{9,11},{10,... | collective-permute-start | bytes 196616 | tf_op jit(solution)/shard_map/ppermute | solution.py:30
  16.8 1.6 %collective-permute-start.7 = (bf16[64,512]{1,0:T(8,128)(2,1)S(1)}, bf16[64,512]{1,0:T(8,128)(2,1)S(1)}, u32[]{:S(2)}, u32[]{:S(2)}) collective-permute-start(bf16[64,512]{1,0:T(8,128)(2,1)S(1)} %get-tuple-element.32), channel_id=1, source_target_pairs={{0,4},{1,5},{2,6},{3,7},{4,0},{5,1},{6,2},{7,3},{8,12},{9,13},{10,... | collective-permute-start | bytes 196616 | tf_op jit(solution)/shard_map/ppermute | solution.py:30
  19.8 1.6 %collective-permute-done.7 = bf16[64,512]{1,0:T(8,128)(2,1)S(1)} collective-permute-done((bf16[64,512]{1,0:T(8,128)(2,1)S(1)}, bf16[64,512]{1,0:T(8,128)(2,1)S(1)}, u32[]{:S(2)}, u32[]{:S(2)}) %collective-permute-start.7) | collective-permute-done | bytes 65568 | tf_op jit(solution)/shard_map/ppermute | solution.py:30
  21.4 2.2 %collective-permute-done.8 = bf16[64,512]{1,0:T(8,128)(2,1)S(1)} collective-permute-done((bf16[64,512]{1,0:T(8,128)(2,1)S(1)}, bf16[64,512]{1,0:T(8,128)(2,1)S(1)}, u32[]{:S(2)}, u32[]{:S(2)}) %collective-permute-start.8) | collective-permute-done | bytes 65568 | tf_op jit(solution)/shard_map/ppermute | solution.py:30
  24.4 5.1 %collective-permute-done.9 = bf16[64,512]{1,0:T(8,128)(2,1)S(1)} collective-permute-done((bf16[64,512]{1,0:T(8,128)(2,1)S(1)}, bf16[64,512]{1,0:T(8,128)(2,1)S(1)}, u32[]{:S(2)}, u32[]{:S(2)}) %collective-permute-start.9) | collective-permute-done | bytes 65568 | tf_op jit(solution)/shard_map/ppermute | solution.py:30
  30.9 2.2 %collective-permute-start.13 = (bf16[64,512]{1,0:T(8,128)(2,1)S(1)}, bf16[64,512]{1,0:T(8,128)(2,1)S(1)}, u32[]{:S(2)}, u32[]{:S(2)}) collective-permute-start(bf16[64,512]{1,0:T(8,128)(2,1)S(1)} %get-tuple-element.58.refs_2_), channel_id=1, source_target_pairs={{0,6},{1,7},{2,4},{3,5},{4,2},{5,3},{6,0},{7,1},{8,14},{9,15},{10,... | collective-permute-start | bytes 196616 | tf_op jit(solution)/shard_map/ppermute | solution.py:30
  33.9 2.2 %collective-permute-done.13.refs_5_ = bf16[64,512]{1,0:T(8,128)(2,1)S(1)} collective-permute-done((bf16[64,512]{1,0:T(8,128)(2,1)S(1)}, bf16[64,512]{1,0:T(8,128)(2,1)S(1)}, u32[]{:S(2)}, u32[]{:S(2)}) %collective-permute-start.13) | collective-permute-done | bytes 65568 | tf_op jit(solution)/shard_map/ppermute | solution.py:30
  39.0 2.0 %collective-permute-start.15 = (bf16[64,512]{1,0:T(8,128)(2,1)S(1)}, bf16[64,512]{1,0:T(8,128)(2,1)S(1)}, u32[]{:S(2)}, u32[]{:S(2)}) collective-permute-start(bf16[64,512]{1,0:T(8,128)(2,1)S(1)} %get-tuple-element.38), channel_id=1, source_target_pairs={{0,4},{1,5},{2,6},{3,7},{4,0},{5,1},{6,2},{7,3},{8,12},{9,13},{10,... | collective-permute-start | bytes 196616 | tf_op jit(solution)/shard_map/ppermute | solution.py:30
  43.3 2.9 %collective-permute-done.16 = bf16[64,512]{1,0:T(8,128)(2,1)S(1)} collective-permute-done((bf16[64,512]{1,0:T(8,128)(2,1)S(1)}, bf16[64,512]{1,0:T(8,128)(2,1)S(1)}, u32[]{:S(2)}, u32[]{:S(2)}) %collective-permute-start.16) | collective-permute-done | bytes 65568 | tf_op jit(solution)/shard_map/ppermute | solution.py:30
  46.3 5.6 %collective-permute-done.17 = bf16[64,512]{1,0:T(8,128)(2,1)S(1)} collective-permute-done((bf16[64,512]{1,0:T(8,128)(2,1)S(1)}, bf16[64,512]{1,0:T(8,128)(2,1)S(1)}, u32[]{:S(2)}, u32[]{:S(2)}) %collective-permute-start.17) | collective-permute-done | bytes 65568 | tf_op jit(solution)/shard_map/ppermute | solution.py:30
  52.1 1.7 %collective-permute-start.19 = (bf16[64,512]{1,0:T(8,128)(2,1)S(1)}, bf16[64,512]{1,0:T(8,128)(2,1)S(1)}, u32[]{:S(2)}, u32[]{:S(2)}) collective-permute-start(bf16[64,512]{1,0:T(8,128)(2,1)S(1)} %get-tuple-element.56.refs_2_), channel_id=1, source_target_pairs={{0,4},{1,5},{2,6},{3,7},{4,0},{5,1},{6,2},{7,3},{8,12},{9,13},{10,... | collective-permute-start | bytes 196616 | tf_op jit(solution)/shard_map/ppermute | solution.py:30
  53.8 1.7 %collective-permute-start.20 = (bf16[64,512]{1,0:T(8,128)(2,1)S(1)}, bf16[64,512]{1,0:T(8,128)(2,1)S(1)}, u32[]{:S(2)}, u32[]{:S(2)}) collective-permute-start(bf16[64,512]{1,0:T(8,128)(2,1)S(1)} %get-tuple-element.56.refs_2_), channel_id=1, source_target_pairs={{0,6},{1,7},{2,4},{3,5},{4,2},{5,3},{6,0},{7,1},{8,14},{9,15},{10,... | collective-permute-start | bytes 196616 | tf_op jit(solution)/shard_map/ppermute | solution.py:30
  56.4 3.3 %collective-permute-done.20.refs_5_ = bf16[64,512]{1,0:T(8,128)(2,1)S(1)} collective-permute-done((bf16[64,512]{1,0:T(8,128)(2,1)S(1)}, bf16[64,512]{1,0:T(8,128)(2,1)S(1)}, u32[]{:S(2)}, u32[]{:S(2)}) %collective-permute-start.20) | collective-permute-done | bytes 65568 | tf_op jit(solution)/shard_map/ppermute | solution.py:30
  63.5 1.8 %collective-permute-start.23 = (bf16[64,512]{1,0:T(8,128)(2,1)S(1)}, bf16[64,512]{1,0:T(8,128)(2,1)S(1)}, u32[]{:S(2)}, u32[]{:S(2)}) collective-permute-start(bf16[64,512]{1,0:T(8,128)(2,1)S(1)} %get-tuple-element.47), channel_id=1, source_target_pairs={{0,6},{1,7},{2,4},{3,5},{4,2},{5,3},{6,0},{7,1},{8,14},{9,15},{10,... | collective-permute-start | bytes 196616 | tf_op jit(solution)/shard_map/ppermute | solution.py:30
  66.5 2.2 %collective-permute-done.23 = bf16[64,512]{1,0:T(8,128)(2,1)S(1)} collective-permute-done((bf16[64,512]{1,0:T(8,128)(2,1)S(1)}, bf16[64,512]{1,0:T(8,128)(2,1)S(1)}, u32[]{:S(2)}, u32[]{:S(2)}) %collective-permute-start.23) | collective-permute-done | bytes 65568 | tf_op jit(solution)/shard_map/ppermute | solution.py:30
  69.3 5.3 %collective-permute-done.24 = bf16[64,512]{1,0:T(8,128)(2,1)S(1)} collective-permute-done((bf16[64,512]{1,0:T(8,128)(2,1)S(1)}, bf16[64,512]{1,0:T(8,128)(2,1)S(1)}, u32[]{:S(2)}, u32[]{:S(2)}) %collective-permute-start.24) | collective-permute-done | bytes 65568 | tf_op jit(solution)/shard_map/ppermute | solution.py:30
  75.0 1.7 %collective-permute-start.27 = (bf16[64,512]{1,0:T(8,128)(2,1)S(1)}, bf16[64,512]{1,0:T(8,128)(2,1)S(1)}, u32[]{:S(2)}, u32[]{:S(2)}) collective-permute-start(bf16[64,512]{1,0:T(8,128)(2,1)S(1)} %get-tuple-element.54.refs_2_), channel_id=1, source_target_pairs={{0,4},{1,5},{2,6},{3,7},{4,0},{5,1},{6,2},{7,3},{8,12},{9,13},{10,... | collective-permute-start | bytes 196616 | tf_op jit(solution)/shard_map/ppermute | solution.py:30
  76.7 1.8 %collective-permute-start.28 = (bf16[64,512]{1,0:T(8,128)(2,1)S(1)}, bf16[64,512]{1,0:T(8,128)(2,1)S(1)}, u32[]{:S(2)}, u32[]{:S(2)}) collective-permute-start(bf16[64,512]{1,0:T(8,128)(2,1)S(1)} %get-tuple-element.54.refs_2_), channel_id=1, source_target_pairs={{0,6},{1,7},{2,4},{3,5},{4,2},{5,3},{6,0},{7,1},{8,14},{9,15},{10,... | collective-permute-start | bytes 196616 | tf_op jit(solution)/shard_map/ppermute | solution.py:30
  79.6 2.4 %collective-permute-done.28.refs_5_ = bf16[64,512]{1,0:T(8,128)(2,1)S(1)} collective-permute-done((bf16[64,512]{1,0:T(8,128)(2,1)S(1)}, bf16[64,512]{1,0:T(8,128)(2,1)S(1)}, u32[]{:S(2)}, u32[]{:S(2)}) %collective-permute-start.28) | collective-permute-done | bytes 65568 | tf_op jit(solution)/shard_map/ppermute | solution.py:30
  82.1 1.6 %copy-done.1 = bf16[2,4,256,512]{3,2,1,0:T(8,128)(2,1)S(1)} copy-done((bf16[2,4,256,512]{3,2,1,0:T(8,128)(2,1)S(1)}, bf16[2,4,256,512]{3,2,1,0:T(8,128)(2,1)}, u32[]{:S(2)}) %copy-start.1) | copy-done | bytes 2097176
  (70 shorter events, 26.1 us)
Async XLA Ops:
  0.6 11.1 %collective-permute-start.4 = (bf16[64,128,128]{2,1,0:T(8,128)(2,1)}, bf16[64,128,128]{2,1,0:T(8,128)(2,1)}, u32[]{:S(2)}, u32[]{:S(2)}) collective-permute-start(bf16[64,128,128]{2,1,0:T(8,128)(2,1)} %tile_ref.1), channel_id=1, source_target_pairs={{0,1},{1,0},{2,3},{3,2},{4,5},{5,4},{6,7},{7,6},{8,9},{9,8},{10,11... | collective-permute-start | bytes 6291464 | tf_op jit(solution)/shard_map/ppermute | solution.py:30
  2.2 12.1 %collective-permute-start.5 = (f32[256,64]{1,0:T(8,128)S(1)}, f32[256,64]{1,0:T(8,128)S(1)}, u32[]{:S(2)}, u32[]{:S(2)}) collective-permute-start(f32[256,64]{1,0:T(8,128)S(1)} %get-tuple-element.64), channel_id=1, source_target_pairs={{0,1},{1,0},{2,3},{3,2},{4,5},{5,4},{6,7},{7,6},{8,9},{9,8},{10,11... | collective-permute-start | bytes 196616 | tf_op jit(solution)/shard_map/ppermute | solution.py:30
  3.9 14.9 %collective-permute-start.1 = (f32[264,128]{1,0:T(8,128)S(1)}, f32[264,128]{1,0:T(8,128)S(1)}, u32[]{:S(2)}, u32[]{:S(2)}) collective-permute-start(f32[264,128]{1,0:T(8,128)S(1)} %pad_maximum_fusion.refs_0_), channel_id=1, source_target_pairs={{0,8},{1,9},{2,10},{3,11},{4,12},{5,13},{6,14},{7,15},{8,0},{9,1},... | collective-permute-start | bytes 405512 | tf_op jit(solution)/shard_map/ppermute | solution.py:30
  15.3 4.6 %collective-permute-start.6 = (bf16[64,512]{1,0:T(8,128)(2,1)S(1)}, bf16[64,512]{1,0:T(8,128)(2,1)S(1)}, u32[]{:S(2)}, u32[]{:S(2)}) collective-permute-start(bf16[64,512]{1,0:T(8,128)(2,1)S(1)} %get-tuple-element.31), channel_id=1, source_target_pairs={{0,2},{1,3},{2,0},{3,1},{4,6},{5,7},{6,4},{7,5},{8,10},{9,11},{10,... | collective-permute-start | bytes 196616 | tf_op jit(solution)/shard_map/ppermute | solution.py:30
  16.8 4.5 %collective-permute-start.7 = (bf16[64,512]{1,0:T(8,128)(2,1)S(1)}, bf16[64,512]{1,0:T(8,128)(2,1)S(1)}, u32[]{:S(2)}, u32[]{:S(2)}) collective-permute-start(bf16[64,512]{1,0:T(8,128)(2,1)S(1)} %get-tuple-element.32), channel_id=1, source_target_pairs={{0,4},{1,5},{2,6},{3,7},{4,0},{5,1},{6,2},{7,3},{8,12},{9,13},{10,... | collective-permute-start | bytes 196616 | tf_op jit(solution)/shard_map/ppermute | solution.py:30
  18.4 5.2 %collective-permute-start.8 = (bf16[64,512]{1,0:T(8,128)(2,1)S(1)}, bf16[64,512]{1,0:T(8,128)(2,1)S(1)}, u32[]{:S(2)}, u32[]{:S(2)}) collective-permute-start(bf16[64,512]{1,0:T(8,128)(2,1)S(1)} %get-tuple-element.33), channel_id=1, source_target_pairs={{0,6},{1,7},{2,4},{3,5},{4,2},{5,3},{6,0},{7,1},{8,14},{9,15},{10,... | collective-permute-start | bytes 196616 | tf_op jit(solution)/shard_map/ppermute | solution.py:30
  18.8 5.3 %collective-permute-start = (f32[264,128]{1,0:T(8,128)S(1)}, f32[264,128]{1,0:T(8,128)S(1)}, u32[]{:S(2)}, u32[]{:S(2)}) collective-permute-start(f32[264,128]{1,0:T(8,128)S(1)} %pad_maximum_fusion.refs_0_), channel_id=1, source_target_pairs={{0,1},{1,0},{2,3},{3,2},{4,5},{5,4},{6,7},{7,6},{8,9},{9,8},{10,11... | collective-permute-start | bytes 405512 | tf_op jit(solution)/shard_map/ppermute | solution.py:30
  18.8 5.3 %collective-permute-start.2 = (f32[264,128]{1,0:T(8,128)S(1)}, f32[264,128]{1,0:T(8,128)S(1)}, u32[]{:S(2)}, u32[]{:S(2)}) collective-permute-start(f32[264,128]{1,0:T(8,128)S(1)} %collective-permute-done.1.refs_2_), channel_id=1, source_target_pairs={{0,1},{1,0},{2,3},{3,2},{4,5},{5,4},{6,7},{7,6},{8,9},{9,8},{10,11... | collective-permute-start | bytes 405512 | tf_op jit(solution)/shard_map/ppermute | solution.py:30
  23.6 5.8 %collective-permute-start.9 = (bf16[64,512]{1,0:T(8,128)(2,1)S(1)}, bf16[64,512]{1,0:T(8,128)(2,1)S(1)}, u32[]{:S(2)}, u32[]{:S(2)}) collective-permute-start(bf16[64,512]{1,0:T(8,128)(2,1)S(1)} %fusion), channel_id=1, source_target_pairs={{0,8},{1,9},{2,10},{3,11},{4,12},{5,13},{6,14},{7,15},{8,0},{9,1},... | collective-permute-start | bytes 196616 | tf_op jit(solution)/shard_map/ppermute | solution.py:30
  29.5 4.3 %collective-permute-start.11 = (bf16[64,512]{1,0:T(8,128)(2,1)S(1)}, bf16[64,512]{1,0:T(8,128)(2,1)S(1)}, u32[]{:S(2)}, u32[]{:S(2)}) collective-permute-start(bf16[64,512]{1,0:T(8,128)(2,1)S(1)} %get-tuple-element.58.refs_2_), channel_id=1, source_target_pairs={{0,2},{1,3},{2,0},{3,1},{4,6},{5,7},{6,4},{7,5},{8,10},{9,11},{10,... | collective-permute-start | bytes 196616 | tf_op jit(solution)/shard_map/ppermute | solution.py:30
  29.6 4.3 %collective-permute-start.12 = (bf16[64,512]{1,0:T(8,128)(2,1)S(1)}, bf16[64,512]{1,0:T(8,128)(2,1)S(1)}, u32[]{:S(2)}, u32[]{:S(2)}) collective-permute-start(bf16[64,512]{1,0:T(8,128)(2,1)S(1)} %get-tuple-element.58.refs_2_), channel_id=1, source_target_pairs={{0,4},{1,5},{2,6},{3,7},{4,0},{5,1},{6,2},{7,3},{8,12},{9,13},{10,... | collective-permute-start | bytes 196616 | tf_op jit(solution)/shard_map/ppermute | solution.py:30
  30.9 5.2 %collective-permute-start.13 = (bf16[64,512]{1,0:T(8,128)(2,1)S(1)}, bf16[64,512]{1,0:T(8,128)(2,1)S(1)}, u32[]{:S(2)}, u32[]{:S(2)}) collective-permute-start(bf16[64,512]{1,0:T(8,128)(2,1)S(1)} %get-tuple-element.58.refs_2_), channel_id=1, source_target_pairs={{0,6},{1,7},{2,4},{3,5},{4,2},{5,3},{6,0},{7,1},{8,14},{9,15},{10,... | collective-permute-start | bytes 196616 | tf_op jit(solution)/shard_map/ppermute | solution.py:30
  38.2 4.3 %collective-permute-start.14 = (bf16[64,512]{1,0:T(8,128)(2,1)S(1)}, bf16[64,512]{1,0:T(8,128)(2,1)S(1)}, u32[]{:S(2)}, u32[]{:S(2)}) collective-permute-start(bf16[64,512]{1,0:T(8,128)(2,1)S(1)} %get-tuple-element.37), channel_id=1, source_target_pairs={{0,2},{1,3},{2,0},{3,1},{4,6},{5,7},{6,4},{7,5},{8,10},{9,11},{10,... | collective-permute-start | bytes 196616 | tf_op jit(solution)/shard_map/ppermute | solution.py:30
  39.0 4.3 %collective-permute-start.15 = (bf16[64,512]{1,0:T(8,128)(2,1)S(1)}, bf16[64,512]{1,0:T(8,128)(2,1)S(1)}, u32[]{:S(2)}, u32[]{:S(2)}) collective-permute-start(bf16[64,512]{1,0:T(8,128)(2,1)S(1)} %get-tuple-element.38), channel_id=1, source_target_pairs={{0,4},{1,5},{2,6},{3,7},{4,0},{5,1},{6,2},{7,3},{8,12},{9,13},{10,... | collective-permute-start | bytes 196616 | tf_op jit(solution)/shard_map/ppermute | solution.py:30
  41.0 5.2 %collective-permute-start.16 = (bf16[64,512]{1,0:T(8,128)(2,1)S(1)}, bf16[64,512]{1,0:T(8,128)(2,1)S(1)}, u32[]{:S(2)}, u32[]{:S(2)}) collective-permute-start(bf16[64,512]{1,0:T(8,128)(2,1)S(1)} %get-tuple-element.39), channel_id=1, source_target_pairs={{0,6},{1,7},{2,4},{3,5},{4,2},{5,3},{6,0},{7,1},{8,14},{9,15},{10,... | collective-permute-start | bytes 196616 | tf_op jit(solution)/shard_map/ppermute | solution.py:30
  46.2 5.7 %collective-permute-start.17 = (bf16[64,512]{1,0:T(8,128)(2,1)S(1)}, bf16[64,512]{1,0:T(8,128)(2,1)S(1)}, u32[]{:S(2)}, u32[]{:S(2)}) collective-permute-start(bf16[64,512]{1,0:T(8,128)(2,1)S(1)} %fusion.1), channel_id=1, source_target_pairs={{0,8},{1,9},{2,10},{3,11},{4,12},{5,13},{6,14},{7,15},{8,0},{9,1},... | collective-permute-start | bytes 196616 | tf_op jit(solution)/shard_map/ppermute | solution.py:30
  52.0 4.3 %collective-permute-start.18 = (bf16[64,512]{1,0:T(8,128)(2,1)S(1)}, bf16[64,512]{1,0:T(8,128)(2,1)S(1)}, u32[]{:S(2)}, u32[]{:S(2)}) collective-permute-start(bf16[64,512]{1,0:T(8,128)(2,1)S(1)} %get-tuple-element.56.refs_2_), channel_id=1, source_target_pairs={{0,2},{1,3},{2,0},{3,1},{4,6},{5,7},{6,4},{7,5},{8,10},{9,11},{10,... | collective-permute-start | bytes 196616 | tf_op jit(solution)/shard_map/ppermute | solution.py:30
  53.8 5.9 %collective-permute-start.20 = (bf16[64,512]{1,0:T(8,128)(2,1)S(1)}, bf16[64,512]{1,0:T(8,128)(2,1)S(1)}, u32[]{:S(2)}, u32[]{:S(2)}) collective-permute-start(bf16[64,512]{1,0:T(8,128)(2,1)S(1)} %get-tuple-element.56.refs_2_), channel_id=1, source_target_pairs={{0,6},{1,7},{2,4},{3,5},{4,2},{5,3},{6,0},{7,1},{8,14},{9,15},{10,... | collective-permute-start | bytes 196616 | tf_op jit(solution)/shard_map/ppermute | solution.py:30
  61.8 4.3 %collective-permute-start.21 = (bf16[64,512]{1,0:T(8,128)(2,1)S(1)}, bf16[64,512]{1,0:T(8,128)(2,1)S(1)}, u32[]{:S(2)}, u32[]{:S(2)}) collective-permute-start(bf16[64,512]{1,0:T(8,128)(2,1)S(1)} %get-tuple-element.45), channel_id=1, source_target_pairs={{0,2},{1,3},{2,0},{3,1},{4,6},{5,7},{6,4},{7,5},{8,10},{9,11},{10,... | collective-permute-start | bytes 196616 | tf_op jit(solution)/shard_map/ppermute | solution.py:30
  63.5 5.2 %collective-permute-start.23 = (bf16[64,512]{1,0:T(8,128)(2,1)S(1)}, bf16[64,512]{1,0:T(8,128)(2,1)S(1)}, u32[]{:S(2)}, u32[]{:S(2)}) collective-permute-start(bf16[64,512]{1,0:T(8,128)(2,1)S(1)} %get-tuple-element.47), channel_id=1, source_target_pairs={{0,6},{1,7},{2,4},{3,5},{4,2},{5,3},{6,0},{7,1},{8,14},{9,15},{10,... | collective-permute-start | bytes 196616 | tf_op jit(solution)/shard_map/ppermute | solution.py:30
  68.8 5.9 %collective-permute-start.24 = (bf16[64,512]{1,0:T(8,128)(2,1)S(1)}, bf16[64,512]{1,0:T(8,128)(2,1)S(1)}, u32[]{:S(2)}, u32[]{:S(2)}) collective-permute-start(bf16[64,512]{1,0:T(8,128)(2,1)S(1)} %fusion.2), channel_id=1, source_target_pairs={{0,8},{1,9},{2,10},{3,11},{4,12},{5,13},{6,14},{7,15},{8,0},{9,1},... | collective-permute-start | bytes 196616 | tf_op jit(solution)/shard_map/ppermute | solution.py:30
  74.9 4.5 %collective-permute-start.26 = (bf16[64,512]{1,0:T(8,128)(2,1)S(1)}, bf16[64,512]{1,0:T(8,128)(2,1)S(1)}, u32[]{:S(2)}, u32[]{:S(2)}) collective-permute-start(bf16[64,512]{1,0:T(8,128)(2,1)S(1)} %get-tuple-element.54.refs_2_), channel_id=1, source_target_pairs={{0,2},{1,3},{2,0},{3,1},{4,6},{5,7},{6,4},{7,5},{8,10},{9,11},{10,... | collective-permute-start | bytes 196616 | tf_op jit(solution)/shard_map/ppermute | solution.py:30
  75.0 4.7 %collective-permute-start.27 = (bf16[64,512]{1,0:T(8,128)(2,1)S(1)}, bf16[64,512]{1,0:T(8,128)(2,1)S(1)}, u32[]{:S(2)}, u32[]{:S(2)}) collective-permute-start(bf16[64,512]{1,0:T(8,128)(2,1)S(1)} %get-tuple-element.54.refs_2_), channel_id=1, source_target_pairs={{0,4},{1,5},{2,6},{3,7},{4,0},{5,1},{6,2},{7,3},{8,12},{9,13},{10,... | collective-permute-start | bytes 196616 | tf_op jit(solution)/shard_map/ppermute | solution.py:30
  76.7 5.4 %collective-permute-start.28 = (bf16[64,512]{1,0:T(8,128)(2,1)S(1)}, bf16[64,512]{1,0:T(8,128)(2,1)S(1)}, u32[]{:S(2)}, u32[]{:S(2)}) collective-permute-start(bf16[64,512]{1,0:T(8,128)(2,1)S(1)} %get-tuple-element.54.refs_2_), channel_id=1, source_target_pairs={{0,6},{1,7},{2,4},{3,5},{4,2},{5,3},{6,0},{7,1},{8,14},{9,15},{10,... | collective-permute-start | bytes 196616 | tf_op jit(solution)/shard_map/ppermute | solution.py:30
  (10 other events, 80.3 us)

commit v3 on v0

v3 whole, which is shorter than its diff:
```python
import functools

import jax
import jax.numpy as jnp
from jax import lax
from jax.experimental import pallas as pl
from jax.experimental.pallas import tpu as pltpu
from jax.sharding import PartitionSpec as P

ITERS = 3
STEP = 0.4
CORES = 2
QUAD = 4
UNIT = CORES * QUAD
VMEM = pl.BlockSpec(memory_space=pltpu.VMEM)
F32, BF16 = jnp.float32, jnp.bfloat16


def params(a_bytes):
    return pltpu.CompilerParams(vmem_limit_bytes=8 * 2**20 + 3 * a_bytes)


def place():
    me = lax.axis_index("row")
    return me // UNIT, (me // CORES) % QUAD, me % CORES


def swap(x, mask):
    return lax.ppermute(x, "row", [(i, i ^ mask) for i in range(lax.axis_size("row"))])


def dot(a, b, over_a, over_b):
    return lax.dot_general(
        a, b, (((over_a,), (over_b,)), ((), ())), preferred_element_type=F32
    )


def first_kernel(span, chunks, at_hbm, tile_hbm, dual_ref, *rest):
    high_ref, low_ref = rest[:2]
    keeps, sends = rest[2 : 2 + QUAD], rest[2 + QUAD : 2 + 2 * QUAD]
    at_s, tile_s, acc, sems = rest[2 + 2 * QUAD :]
    tiles, size, _ = tile_s.shape
    row_blocks = high_ref.shape[1] // size
    step = tiles // chunks
    index_copy = pltpu.make_async_copy(at_hbm, at_s, sems.at[0])
    tile_copies = [
        pltpu.make_async_copy(
            tile_hbm.at[pl.ds(c * step, step)], tile_s.at[pl.ds(c * step, step)], sems.at[1 + c]
        )
        for c in range(chunks)
    ]
    for copy in [index_copy] + tile_copies:
        copy.start()
    acc[...] = jnp.zeros_like(acc)
    low = dual_ref[...].astype(BF16).T

    def add(t, _):
        at = at_s[t]
        acc[at] = acc[at] + tile_s[t].astype(F32)
        return 0

    index_copy.wait()
    for c in range(chunks):
        tile_copies[c].wait()
        lax.fori_loop(c * step, (c + 1) * step, add, 0, unroll=4)
    for column in range(acc.shape[0] // row_blocks):
        owner, s = divmod(column, span)
        far, q, core = owner // UNIT, (owner // CORES) % QUAD, owner % CORES
        cols = pl.ds(((far * CORES + core) * span + s) * size, size)
        for r in range(row_blocks):
            block = acc[column * row_blocks + r]
            high = block.astype(BF16)
            rows = pl.ds(r * size, size)
            high_ref[q, rows, cols] = high
            low_ref[q, rows, cols] = (block - high.astype(F32)).astype(BF16)
    _, me, core = place()
    half = keeps[0].shape[0]
    for k in range(QUAD):
        total = dot(low, high_ref[me ^ k], 1, 0) + dot(low, low_ref[me ^ k], 1, 0)
        keeps[k][...] = jnp.where(core == 0, total[:half], total[half:])
        sends[k][...] = jnp.where(core == 0, total[half:], total[:half])


def first_columns(tile_values, at, dual, span, columns, half):
    tiles, size, _ = tile_values.shape
    rows = dual.shape[0]
    wide = columns * size // QUAD
    chunks = 4 if tiles % 16 == 0 else 1
    any_spec = pl.BlockSpec(memory_space=pltpu.HBM)
    part = jax.ShapeDtypeStruct((half, wide), F32)
    out = pl.pallas_call(
        functools.partial(first_kernel, span, chunks),
        out_shape=(jax.ShapeDtypeStruct((QUAD, rows, wide), BF16),) * 2 + (part,) * (2 * QUAD),
        in_specs=[any_spec, any_spec, VMEM],
        out_specs=(VMEM,) * (2 + 2 * QUAD),
        scratch_shapes=[
            pltpu.SMEM((tiles,), jnp.int32),
            pltpu.VMEM((tiles, size, size), BF16),
            pltpu.VMEM((columns * rows // size, size, size), F32),
            pltpu.SemaphoreType.DMA((1 + chunks,)),
        ],
        compiler_params=pltpu.CompilerParams(vmem_limit_bytes=49 * 2**20),
    )(at, tile_values, dual)
    return out[:2], out[2 : 2 + QUAD], out[2 + QUAD :]


def prepare_kernel(dual, bound, mine, other):
    core = place()[2]
    half = mine.shape[2]
    for i, ref in enumerate((dual, bound)):
        left, right = ref[:, :half], ref[:, half:]
        mine[i] = jnp.where(core == 0, left, right)
        other[i] = jnp.where(core == 0, right, left)


def give_kernel(primal, mine, other):
    far, _, core = place()
    width = mine.shape[1]
    for c, out in ((core, mine), (1 - core, other)):
        out[...] = primal[:, pl.ds(pl.multiple_of((far * CORES + c) * width, width), width)]


def join_variables_kernel(mine, other, out):
    core = place()[2]
    both = jnp.where(
        core == 0,
        jnp.concatenate([mine[...], other[...]], 0),
        jnp.concatenate([other[...], mine[...]], 0),
    )
    out[...] = both.T


def join_rows_kernel(mine, other, out):
    core = place()[2]
    out[...] = jnp.where(
        core == 0,
        jnp.concatenate([mine[...], other[...]], 1),
        jnp.concatenate([other[...], mine[...]], 1),
    )


def variables_kernel(*refs):
    packs, costs, (primal_ref, cost_ref, limit_ref) = refs[:-5], refs[-5:-3], refs[-3:]
    far, _, core = place()
    width = costs[0].shape[0]
    half = primal_ref.shape[0]

    def turn(block):
        turned = block.T
        return jnp.where(core == 0, turned[:half], turned[half:])

    cost_ref[...] = jnp.zeros_like(cost_ref)
    for j, ref in enumerate(packs):
        owner = (far * CORES + core) ^ j
        cols = pl.ds(pl.multiple_of(owner * width, width), width)
        primal_ref[:, cols] = turn(ref[:width])
        limit_ref[:, cols] = ref[width : width + 1]
        if j < CORES:
            cost_ref[:, cols] = turn(costs[j][...])


def row_product(a, pieces, members, me):
    total = None
    for piece, k in zip(pieces, members):
        for h in range(2):
            part = dot(a[h][me ^ k], piece[...], 1, 1)
            total = part if total is None else total + part
    return total


def column_product(low, a, member):
    total = None
    for i in range(2):
        for h in range(2):
            part = dot(low[i], a[i][h][member], 1, 0)
            total = part if total is None else total + part
    return total


def near_rows_kernel(*refs):
    a, pieces, images = (refs[0:2], refs[2:4]), refs[4 : 3 + QUAD], refs[3 + QUAD :]
    me = place()[1]
    for i in range(2):
        images[i][...] = row_product(a[i], pieces, range(QUAD - 1), me)


def turn_kernel(first, *refs):
    a, images, last, sides = (refs[0:2], refs[2:4]), refs[4:6], refs[6], refs[7:9]
    at = 9 if first else 11
    duals = [s.at[0] for s in sides] if first else refs[9:11]
    stepped, lows, pieces = refs[at : at + 2], refs[at + 2 : at + 4], refs[at + 4 :]
    me = place()[1]
    low = []
    for i in range(2):
        image = images[i][...] + row_product(a[i], (last,), (QUAD - 1,), me)
        new = jnp.maximum(duals[i][...] + STEP * (sides[i][1] - image), 0.0)
        stepped[i][...] = new
        low.append(new.astype(BF16).T)
        lows[i][...] = low[i]
    for k in range(1, QUAD):
        pieces[k - 1][...] = column_product(low, a, me ^ k).astype(BF16)


def own_columns_kernel(*refs):
    a, lows, got, out = (refs[0:2], refs[2:4]), refs[4:6], refs[6:-1], refs[-1]
    total = column_product([r[...] for r in lows], a, place()[1])
    for piece in got:
        total = total + piece[...].astype(F32)
    out[...] = total


def finish_kernel(high, low, image, last, side, dual, out):
    total = image[...] + row_product((high, low), (last,), (QUAD - 1,), place()[1])
    out[...] = jnp.maximum(dual[...] + STEP * (side[1] - total), 0.0)


def body(
    tile_values, tile_row, tile_col, primal_start, objective, upper_bound, dual_start, row_bound
):
    devices = lax.axis_size("row")
    size = tile_values.shape[1]
    width, scenarios = primal_start.shape
    rows = dual_start.shape[0]
    half = scenarios // CORES
    span = width // size
    far_masks = []
    while UNIT << len(far_masks) < devices:
        far_masks.append(UNIT << len(far_masks))
    wide = devices * width // QUAD
    core = place()[2]
    limits = params(4 * QUAD * rows * wide)
    state = jax.ShapeDtypeStruct((half, wide), F32)
    piece = jax.ShapeDtypeStruct((half, wide), BF16)
    side = jax.ShapeDtypeStruct((rows, half), F32)

    def call(kernel, out_shape, *operands):
        many = isinstance(out_shape, tuple)
        return pl.pallas_call(
            kernel,
            out_shape=out_shape,
            in_specs=[VMEM] * len(operands),
            out_specs=(VMEM,) * len(out_shape) if many else VMEM,
            compiler_params=limits,
        )(*operands)

    own, keeps, sends = first_columns(
        tile_values, tile_col * (rows // size) + tile_row, dual_start, span, devices * span, half
    )
    sums = [k + swap(s, 1) for k, s in zip(keeps, sends)]
    pieces = [s.astype(BF16) for s in sums[1:]]
    got = [swap(p, k * CORES) for k, p in enumerate(pieces, 1)]

    pack = jnp.concatenate(
        [primal_start, jnp.broadcast_to(upper_bound[None, :], (8, width))], 0
    )
    packs = [pack]
    for mask in far_masks:
        packs = packs + [swap(p, mask) for p in packs]
    later, _ = lax.optimization_barrier((packs[1:], got[:]))
    mates = [swap(p, 1) for p in [pack, *later]]
    packs = [p for pair in zip(packs, mates) for p in pair]
    primal, cost, limit = call(
        variables_kernel,
        (state, state, jax.ShapeDtypeStruct((1, wide), F32)),
        *packs,
        objective,
        swap(objective, 1),
    )
    sent, dual_start, row_bound, _, _ = lax.optimization_barrier(
        (own, dual_start, row_bound, pieces, sums[0])
    )
    a = (*own, *[swap(s, 1) for s in sent])
    halves = jax.ShapeDtypeStruct((2, rows, half), F32)
    mine, other = call(prepare_kernel, (halves, halves), dual_start, row_bound)
    sides = (mine, swap(other, 1))

    duals = ()
    for iteration in range(ITERS):
        if iteration == 0:
            total = sums[0] - cost
            for g in got[:-1]:
                total = total + g.astype(F32)
        else:
            got = [swap(p, k * CORES) for k, p in enumerate(pieces, 1)]
            total = call(own_columns_kernel, state, *a, *lows, *got[:-1]) - cost
        total = total + got[-1].astype(F32)
        for mask in far_masks:
            total = total + swap(total.astype(BF16), mask).astype(F32)
        updated = jnp.clip(primal + STEP * total, 0.0, limit)
        ahead = (2.0 * updated - primal).astype(BF16)
        primal = updated
        around = [ahead] + [swap(ahead, k * CORES) for k in range(1, QUAD)]
        images = call(near_rows_kernel, (side, side), *a, *around[:-1])
        if iteration < ITERS - 1:
            out = call(
                functools.partial(turn_kernel, iteration == 0),
                (side,) * 2
                + (jax.ShapeDtypeStruct((half, rows), BF16),) * 2
                + (piece,) * (QUAD - 1),
                *a,
                *images,
                around[-1],
                *sides,
                *duals,
            )
            duals, lows, pieces = out[0:2], out[2:4], out[4:]

    part = jax.ShapeDtypeStruct((half, width), F32)
    mine, other = call(give_kernel, (part, part), primal)
    primal = call(
        join_variables_kernel,
        jax.ShapeDtypeStruct((width, scenarios), F32),
        mine,
        swap(other, 1),
    )
    mine, other = [
        call(finish_kernel, side, *a[2 * i : 2 * i + 2], images[i], around[-1], sides[i], duals[i])
        for i in range(2)
    ]
    dual = call(
        join_rows_kernel, jax.ShapeDtypeStruct((rows, scenarios), F32), mine, swap(other, 1)
    )
    return (primal, dual)


def solution(mesh):
    return jax.shard_map(
        body,
        mesh=mesh,
        in_specs=(
            P(("parts", "row"), None, None),
            P(("parts", "row")),
            P(("parts", "row")),
            P(("parts", "row"), None),
            P(("parts", "row"), None),
            P(("parts", "row")),
            P(("parts", "row"), None),
            P(("parts", "row"), None),
        ),
        out_specs=(P(("parts", "row"), None), P(("parts", "row"), None)),
        check_vma=False,
    )
```

time: 302 us -> 83.2 us (0.28)
  blocking collectives: 125 us -> 0 us
  other arithmetic: 66.9 us -> 1.03 us
  local copies, waits for them, and re-layouts: 47.9 us -> 0.92 us
  matrix products: 29.3 us -> 0 us
  starting transfers between devices: 7.45 us -> 31.9 us
  waiting for transfers between devices: 22.9 us -> 37.7 us
  Pallas kernels: 0 us -> 10.6 us
    all_gather x3 -> x0, blocking collectives: 68.6 us -> none  [body(): lax.all_gather(extrapolated, 'row', axis=0, tiled=True)]
    scatter-add x6 -> x0, other arithmetic: 57.2 us -> none  [the longest x3 30.9 us: body(): jax.ops.segment_sum(partial_value, tile_col, num_segments=column_blocks)]
    all_to_all x2 -> x0, blocking collectives: 56.2 us -> none  [body(): lax.all_to_all(local_sums, 'row', split_axis=0, concat_axis=0, tiled=True)]
    ppermute x0 -> x34, waiting for transfers between devices: none -> 37.7 us  [swap(): lax.ppermute(x, 'row', [(i, i ^ mask) for i in range(lax.axis_size('row'))])]
    dot_general x6 -> x0, local copies, waits for them, and re-layouts: 33.6 us -> none  [the longest x3 16.8 us: body(): jnp.einsum('tij,tjs->tis', tile_values, chosen, preferred_element_type=jn...]
    ppermute x0 -> x34, starting transfers between devices: none -> 31.9 us  [swap(): lax.ppermute(x, 'row', [(i, i ^ mask) for i in range(lax.axis_size('row'))])]
    dot_general x6 -> x0, matrix products: 29.3 us -> none  [the longest x3 15.9 us: body(): jnp.einsum('tij,tjs->tis', tile_values, chosen, preferred_element_type=jn...]
    all_to_all x1 -> x0, waiting for transfers between devices: 22.9 us -> none  [body(): lax.all_to_all(local_sums, 'row', split_axis=0, concat_axis=0, tiled=True)]
  transfers between devices with their start and end apart: 1 -> 34, of which waited for: 1 -> 22; matrix products, arithmetic and copies ran while one was open for 0% -> 0% of each run, Pallas kernels for 0% -> 6%
where the time goes in v3:
time: 83.2 us; the launch traced here: 83 us
  waiting for transfers between devices  37.7 us (45%)
  starting transfers between devices  31.9 us (38%)
  Pallas kernels  10.6 us (13%)
  other arithmetic  1.03 us (1%)
  local copies, waits for them, and re-layouts  0.92 us (1%)
  between operations  0.84 us (1%)
    ppermute x34, waiting for transfers between devices, swap(): lax.ppermute(x, 'row', [(i, i ^ mask) for i in range(lax.axis_size('row'))])  37.7 us
    ppermute x34, starting transfers between devices, swap(): lax.ppermute(x, 'row', [(i, i ^ mask) for i in range(lax.axis_size('row'))])  31.9 us
    pallas_call x14, Pallas kernels, call(): pl.pallas_call(kernel, out_shape=out_shape, in_specs=[VMEM] * len(operand...  8.05 us
    pallas_call x1, Pallas kernels, first_columns(): pl.pallas_call(functools.partial(first_kernel, span, chunks), out_shape=(...  2.57 us
  transfers between devices with their start and end apart: 34, of which 22 were waited for; matrix products, arithmetic and copies ran while one was open for 0% of the time, Pallas kernels for 6%

profile of v3, /device:TPU:0, one launch (start us, length us, event | category | flops | bytes accessed | tf_op | source)
XLA Modules:
  0.0 83.0 jit_solution(9592237626739343090)
XLA Ops:
  2.2 2.6 %shard_map.95 = (bf16[4,256,512]{2,1,0:T(8,128)(2,1)S(1)}, bf16[4,256,512]{2,1,0:T(8,128)(2,1)S(1)}, f32[64,512]{1,0:T(8,128)S(1)}, f32[64,512]{1,0:T(8,128)S(1)...) custom-call(s32[64]{0:T(128)S(1)} %multiply_add_fusion.at_hbm, ...), custom_call_target="tpu_custom_call" | custom-call | tf_op jit(solution)/shard_map/pallas_call | solution.py:91
  5.3 3.7 %collective-permute-start.1 = (f32[136,128]{1,0:T(8,128)S(1)}, f32[136,128]{1,0:T(8,128)S(1)}, u32[]{:S(2)}, u32[]{:S(2)}) collective-permute-start(f32[136,128]{1,0:T(8,128)S(1)} %pad_maximum_fusion.refs_0_), channel_id=1, source_target_pairs={{0,8},{1,9},{2,10},{3,11},{4,12},{5,13},{6,14},{7,15},{8,0},{9,1},... | collective-permute-start | bytes 208904 | tf_op jit(solution)/shard_map/ppermute | solution.py:29
  9.6 1.6 %collective-permute-start.3 = (bf16[64,512]{1,0:T(8,128)(2,1)S(1)}, bf16[64,512]{1,0:T(8,128)(2,1)S(1)}, u32[]{:S(2)}, u32[]{:S(2)}) collective-permute-start(bf16[64,512]{1,0:T(8,128)(2,1)S(1)} %add_convert_fusion.2), channel_id=1, source_target_pairs={{0,2},{1,3},{2,0},{3,1},{4,6},{5,7},{6,4},{7,5},{8,10},{9,11},{10,... | collective-permute-start | bytes 196616 | tf_op jit(solution)/shard_map/ppermute | solution.py:29
  11.2 1.6 %collective-permute-start.5 = (bf16[64,512]{1,0:T(8,128)(2,1)S(1)}, bf16[64,512]{1,0:T(8,128)(2,1)S(1)}, u32[]{:S(2)}, u32[]{:S(2)}) collective-permute-start(bf16[64,512]{1,0:T(8,128)(2,1)S(1)} %add_convert_fusion.1), channel_id=1, source_target_pairs={{0,4},{1,5},{2,6},{3,7},{4,0},{5,1},{6,2},{7,3},{8,12},{9,13},{10,... | collective-permute-start | bytes 196616 | tf_op jit(solution)/shard_map/ppermute | solution.py:29
  14.1 1.5 %collective-permute-done.5 = bf16[64,512]{1,0:T(8,128)(2,1)S(1)} collective-permute-done((bf16[64,512]{1,0:T(8,128)(2,1)S(1)}, bf16[64,512]{1,0:T(8,128)(2,1)S(1)}, u32[]{:S(2)}, u32[]{:S(2)}) %collective-permute-start.5) | collective-permute-done | bytes 65568 | tf_op jit(solution)/shard_map/ppermute | solution.py:29
  15.5 2.6 %collective-permute-done.7 = bf16[64,512]{1,0:T(8,128)(2,1)S(1)} collective-permute-done((bf16[64,512]{1,0:T(8,128)(2,1)S(1)}, bf16[64,512]{1,0:T(8,128)(2,1)S(1)}, u32[]{:S(2)}, u32[]{:S(2)}) %collective-permute-start.7) | collective-permute-done | bytes 65568 | tf_op jit(solution)/shard_map/ppermute | solution.py:29
  21.3 5.6 %collective-permute-done.11 = bf16[64,512]{1,0:T(8,128)(2,1)S(1)} collective-permute-done((bf16[64,512]{1,0:T(8,128)(2,1)S(1)}, bf16[64,512]{1,0:T(8,128)(2,1)S(1)}, u32[]{:S(2)}, u32[]{:S(2)}) %collective-permute-start.11) | collective-permute-done | bytes 65568 | tf_op jit(solution)/shard_map/ppermute | solution.py:29
  28.0 3.3 %collective-permute-done.15.refs_6_ = bf16[64,512]{1,0:T(8,128)(2,1)S(1)} collective-permute-done((bf16[64,512]{1,0:T(8,128)(2,1)S(1)}, bf16[64,512]{1,0:T(8,128)(2,1)S(1)}, u32[]{:S(2)}, u32[]{:S(2)}) %collective-permute-start.15) | collective-permute-done | bytes 65568 | tf_op jit(solution)/shard_map/ppermute | solution.py:29
  32.6 3.9 %collective-permute-done.16.refs_6_ = bf16[64,512]{1,0:T(8,128)(2,1)S(1)} collective-permute-done((bf16[64,512]{1,0:T(8,128)(2,1)S(1)}, bf16[64,512]{1,0:T(8,128)(2,1)S(1)}, u32[]{:S(2)}, u32[]{:S(2)}) %collective-permute-start.16) | collective-permute-done | bytes 65568 | tf_op jit(solution)/shard_map/ppermute | solution.py:29
  38.4 2.7 %collective-permute-start.20 = (bf16[64,512]{1,0:T(8,128)(2,1)S(1)}, bf16[64,512]{1,0:T(8,128)(2,1)S(1)}, u32[]{:S(2)}, u32[]{:S(2)}) collective-permute-start(bf16[64,512]{1,0:T(8,128)(2,1)S(1)} %get-tuple-element.70), channel_id=1, source_target_pairs={{0,6},{1,7},{2,4},{3,5},{4,2},{5,3},{6,0},{7,1},{8,14},{9,15},{10,... | collective-permute-start | bytes 196616 | tf_op jit(solution)/shard_map/ppermute | solution.py:29
  42.9 1.1 %collective-permute-done.20 = bf16[64,512]{1,0:T(8,128)(2,1)S(1)} collective-permute-done((bf16[64,512]{1,0:T(8,128)(2,1)S(1)}, bf16[64,512]{1,0:T(8,128)(2,1)S(1)}, u32[]{:S(2)}, u32[]{:S(2)}) %collective-permute-start.20) | collective-permute-done | bytes 65568 | tf_op jit(solution)/shard_map/ppermute | solution.py:29
  44.0 1.5 %collective-permute-start.21 = (bf16[64,512]{1,0:T(8,128)(2,1)S(1)}, bf16[64,512]{1,0:T(8,128)(2,1)S(1)}, u32[]{:S(2)}, u32[]{:S(2)}) collective-permute-start(bf16[64,512]{1,0:T(8,128)(2,1)S(1)} %fusion), channel_id=1, source_target_pairs={{0,8},{1,9},{2,10},{3,11},{4,12},{5,13},{6,14},{7,15},{8,0},{9,1},... | collective-permute-start | bytes 196616 | tf_op jit(solution)/shard_map/ppermute | solution.py:29
  45.6 3.7 %collective-permute-done.21 = bf16[64,512]{1,0:T(8,128)(2,1)S(1)} collective-permute-done((bf16[64,512]{1,0:T(8,128)(2,1)S(1)}, bf16[64,512]{1,0:T(8,128)(2,1)S(1)}, u32[]{:S(2)}, u32[]{:S(2)}) %collective-permute-start.21) | collective-permute-done | bytes 65568 | tf_op jit(solution)/shard_map/ppermute | solution.py:29
  49.3 2.3 %collective-permute-start.23 = (bf16[64,512]{1,0:T(8,128)(2,1)S(1)}, bf16[64,512]{1,0:T(8,128)(2,1)S(1)}, u32[]{:S(2)}, u32[]{:S(2)}) collective-permute-start(bf16[64,512]{1,0:T(8,128)(2,1)S(1)} %get-tuple-element.88.refs_4_), channel_id=1, source_target_pairs={{0,4},{1,5},{2,6},{3,7},{4,0},{5,1},{6,2},{7,3},{8,12},{9,13},{10,... | collective-permute-start | bytes 196616 | tf_op jit(solution)/shard_map/ppermute | solution.py:29
  51.7 1.4 %collective-permute-start.22 = (bf16[64,512]{1,0:T(8,128)(2,1)S(1)}, bf16[64,512]{1,0:T(8,128)(2,1)S(1)}, u32[]{:S(2)}, u32[]{:S(2)}) collective-permute-start(bf16[64,512]{1,0:T(8,128)(2,1)S(1)} %get-tuple-element.88.refs_4_), channel_id=1, source_target_pairs={{0,2},{1,3},{2,0},{3,1},{4,6},{5,7},{6,4},{7,5},{8,10},{9,11},{10,... | collective-permute-start | bytes 196616 | tf_op jit(solution)/shard_map/ppermute | solution.py:29
  53.9 2.0 %collective-permute-done.22.refs_5_ = bf16[64,512]{1,0:T(8,128)(2,1)S(1)} collective-permute-done((bf16[64,512]{1,0:T(8,128)(2,1)S(1)}, bf16[64,512]{1,0:T(8,128)(2,1)S(1)}, u32[]{:S(2)}, u32[]{:S(2)}) %collective-permute-start.22) | collective-permute-done | bytes 65568 | tf_op jit(solution)/shard_map/ppermute | solution.py:29
  56.9 1.3 %collective-permute-done.24.refs_6_ = bf16[64,512]{1,0:T(8,128)(2,1)S(1)} collective-permute-done((bf16[64,512]{1,0:T(8,128)(2,1)S(1)}, bf16[64,512]{1,0:T(8,128)(2,1)S(1)}, u32[]{:S(2)}, u32[]{:S(2)}) %collective-permute-start.24) | collective-permute-done | bytes 65568 | tf_op jit(solution)/shard_map/ppermute | solution.py:29
  59.3 1.2 %collective-permute-start.25 = (bf16[64,512]{1,0:T(8,128)(2,1)S(1)}, bf16[64,512]{1,0:T(8,128)(2,1)S(1)}, u32[]{:S(2)}, u32[]{:S(2)}) collective-permute-start(bf16[64,512]{1,0:T(8,128)(2,1)S(1)} %get-tuple-element.77), channel_id=1, source_target_pairs={{0,2},{1,3},{2,0},{3,1},{4,6},{5,7},{6,4},{7,5},{8,10},{9,11},{10,... | collective-permute-start | bytes 196616 | tf_op jit(solution)/shard_map/ppermute | solution.py:29
  60.5 2.4 %collective-permute-start.27 = (bf16[64,512]{1,0:T(8,128)(2,1)S(1)}, bf16[64,512]{1,0:T(8,128)(2,1)S(1)}, u32[]{:S(2)}, u32[]{:S(2)}) collective-permute-start(bf16[64,512]{1,0:T(8,128)(2,1)S(1)} %get-tuple-element.79), channel_id=1, source_target_pairs={{0,6},{1,7},{2,4},{3,5},{4,2},{5,3},{6,0},{7,1},{8,14},{9,15},{10,... | collective-permute-start | bytes 196616 | tf_op jit(solution)/shard_map/ppermute | solution.py:29
  63.6 1.8 %collective-permute-done.26.refs_7_ = bf16[64,512]{1,0:T(8,128)(2,1)S(1)} collective-permute-done((bf16[64,512]{1,0:T(8,128)(2,1)S(1)}, bf16[64,512]{1,0:T(8,128)(2,1)S(1)}, u32[]{:S(2)}, u32[]{:S(2)}) %collective-permute-start.26) | collective-permute-done | bytes 65568 | tf_op jit(solution)/shard_map/ppermute | solution.py:29
  65.8 2.5 %collective-permute-start.28 = (bf16[64,512]{1,0:T(8,128)(2,1)S(1)}, bf16[64,512]{1,0:T(8,128)(2,1)S(1)}, u32[]{:S(2)}, u32[]{:S(2)}) collective-permute-start(bf16[64,512]{1,0:T(8,128)(2,1)S(1)} %fusion.1), channel_id=1, source_target_pairs={{0,8},{1,9},{2,10},{3,11},{4,12},{5,13},{6,14},{7,15},{8,0},{9,1},... | collective-permute-start | bytes 196616 | tf_op jit(solution)/shard_map/ppermute | solution.py:29
  68.3 2.8 %collective-permute-done.28 = bf16[64,512]{1,0:T(8,128)(2,1)S(1)} collective-permute-done((bf16[64,512]{1,0:T(8,128)(2,1)S(1)}, bf16[64,512]{1,0:T(8,128)(2,1)S(1)}, u32[]{:S(2)}, u32[]{:S(2)}) %collective-permute-start.28) | collective-permute-done | bytes 65568 | tf_op jit(solution)/shard_map/ppermute | solution.py:29
  71.1 2.0 %collective-permute-start.31 = (bf16[64,512]{1,0:T(8,128)(2,1)S(1)}, bf16[64,512]{1,0:T(8,128)(2,1)S(1)}, u32[]{:S(2)}, u32[]{:S(2)}) collective-permute-start(bf16[64,512]{1,0:T(8,128)(2,1)S(1)} %get-tuple-element.86.refs_4_), channel_id=1, source_target_pairs={{0,4},{1,5},{2,6},{3,7},{4,0},{5,1},{6,2},{7,3},{8,12},{9,13},{10,... | collective-permute-start | bytes 196616 | tf_op jit(solution)/shard_map/ppermute | solution.py:29
  75.4 2.0 %collective-permute-done.30.refs_5_ = bf16[64,512]{1,0:T(8,128)(2,1)S(1)} collective-permute-done((bf16[64,512]{1,0:T(8,128)(2,1)S(1)}, bf16[64,512]{1,0:T(8,128)(2,1)S(1)}, u32[]{:S(2)}, u32[]{:S(2)}) %collective-permute-start.30) | collective-permute-done | bytes 65568 | tf_op jit(solution)/shard_map/ppermute | solution.py:29
  (81 shorter events, 25.2 us)
Async XLA Ops:
  4.8 4.7 %collective-permute-start.2 = (f32[64,512]{1,0:T(8,128)S(1)}, f32[64,512]{1,0:T(8,128)S(1)}, u32[]{:S(2)}, u32[]{:S(2)}) collective-permute-start(f32[64,512]{1,0:T(8,128)S(1)} %get-tuple-element.45), channel_id=1, source_target_pairs={{0,1},{1,0},{2,3},{3,2},{4,5},{5,4},{6,7},{7,6},{8,9},{9,8},{10,11... | collective-permute-start | bytes 393224 | tf_op jit(solution)/shard_map/ppermute | solution.py:29
  5.3 8.2 %collective-permute-start.1 = (f32[136,128]{1,0:T(8,128)S(1)}, f32[136,128]{1,0:T(8,128)S(1)}, u32[]{:S(2)}, u32[]{:S(2)}) collective-permute-start(f32[136,128]{1,0:T(8,128)S(1)} %pad_maximum_fusion.refs_0_), channel_id=1, source_target_pairs={{0,8},{1,9},{2,10},{3,11},{4,12},{5,13},{6,14},{7,15},{8,0},{9,1},... | collective-permute-start | bytes 208904 | tf_op jit(solution)/shard_map/ppermute | solution.py:29
  9.6 4.5 %collective-permute-start.3 = (bf16[64,512]{1,0:T(8,128)(2,1)S(1)}, bf16[64,512]{1,0:T(8,128)(2,1)S(1)}, u32[]{:S(2)}, u32[]{:S(2)}) collective-permute-start(bf16[64,512]{1,0:T(8,128)(2,1)S(1)} %add_convert_fusion.2), channel_id=1, source_target_pairs={{0,2},{1,3},{2,0},{3,1},{4,6},{5,7},{6,4},{7,5},{8,10},{9,11},{10,... | collective-permute-start | bytes 196616 | tf_op jit(solution)/shard_map/ppermute | solution.py:29
  11.2 4.3 %collective-permute-start.5 = (bf16[64,512]{1,0:T(8,128)(2,1)S(1)}, bf16[64,512]{1,0:T(8,128)(2,1)S(1)}, u32[]{:S(2)}, u32[]{:S(2)}) collective-permute-start(bf16[64,512]{1,0:T(8,128)(2,1)S(1)} %add_convert_fusion.1), channel_id=1, source_target_pairs={{0,4},{1,5},{2,6},{3,7},{4,0},{5,1},{6,2},{7,3},{8,12},{9,13},{10,... | collective-permute-start | bytes 196616 | tf_op jit(solution)/shard_map/ppermute | solution.py:29
  12.9 5.2 %collective-permute-start.7 = (bf16[64,512]{1,0:T(8,128)(2,1)S(1)}, bf16[64,512]{1,0:T(8,128)(2,1)S(1)}, u32[]{:S(2)}, u32[]{:S(2)}) collective-permute-start(bf16[64,512]{1,0:T(8,128)(2,1)S(1)} %add_convert_fusion), channel_id=1, source_target_pairs={{0,6},{1,7},{2,4},{3,5},{4,2},{5,3},{6,0},{7,1},{8,14},{9,15},{10,... | collective-permute-start | bytes 196616 | tf_op jit(solution)/shard_map/ppermute | solution.py:29
  13.5 6.1 %collective-permute-start.10 = (f32[64,512]{1,0:T(8,128)S(1)}, f32[64,512]{1,0:T(8,128)S(1)}, u32[]{:S(2)}, u32[]{:S(2)}) collective-permute-start(f32[64,512]{1,0:T(8,128)S(1)} %get-tuple-element.54), channel_id=1, source_target_pairs={{0,1},{1,0},{2,3},{3,2},{4,5},{5,4},{6,7},{7,6},{8,9},{9,8},{10,11... | collective-permute-start | bytes 393224 | tf_op jit(solution)/shard_map/ppermute | solution.py:29
  13.6 6.0 %collective-permute-start = (f32[136,128]{1,0:T(8,128)S(1)}, f32[136,128]{1,0:T(8,128)S(1)}, u32[]{:S(2)}, u32[]{:S(2)}) collective-permute-start(f32[136,128]{1,0:T(8,128)S(1)} %pad_maximum_fusion.refs_0_), channel_id=1, source_target_pairs={{0,1},{1,0},{2,3},{3,2},{4,5},{5,4},{6,7},{7,6},{8,9},{9,8},{10,11... | collective-permute-start | bytes 208904 | tf_op jit(solution)/shard_map/ppermute | solution.py:29
  19.8 11.9 %collective-permute-start.12 = (bf16[4,256,512]{2,1,0:T(8,128)(2,1)S(1)}, bf16[4,256,512]{2,1,0:T(8,128)(2,1)S(1)}, u32[]{:S(2)}, u32[]{:S(2)}) collective-permute-start(bf16[4,256,512]{2,1,0:T(8,128)(2,1)S(1)} %get-tuple-element.58.refs_0_.high), channel_id=1, source_target_pairs={{0,1},{1,0},{2,3},{3,2},{4,5},{5,4},{6,7},{7,6},{8,9},{9,8},{10,11... | collective-permute-start | bytes 3145736 | tf_op jit(solution)/shard_map/ppermute | solution.py:29
  20.2 11.5 %collective-permute-start.13 = (bf16[4,256,512]{2,1,0:T(8,128)(2,1)S(1)}, bf16[4,256,512]{2,1,0:T(8,128)(2,1)S(1)}, u32[]{:S(2)}, u32[]{:S(2)}) collective-permute-start(bf16[4,256,512]{2,1,0:T(8,128)(2,1)S(1)} %get-tuple-element.59.refs_1_.low), channel_id=1, source_target_pairs={{0,1},{1,0},{2,3},{3,2},{4,5},{5,4},{6,7},{7,6},{8,9},{9,8},{10,11... | collective-permute-start | bytes 3145736 | tf_op jit(solution)/shard_map/ppermute | solution.py:29
  20.3 6.6 %collective-permute-start.11 = (bf16[64,512]{1,0:T(8,128)(2,1)S(1)}, bf16[64,512]{1,0:T(8,128)(2,1)S(1)}, u32[]{:S(2)}, u32[]{:S(2)}) collective-permute-start(bf16[64,512]{1,0:T(8,128)(2,1)S(1)} %get-tuple-element.92), channel_id=1, source_target_pairs={{0,8},{1,9},{2,10},{3,11},{4,12},{5,13},{6,14},{7,15},{8,0},{9,1},... | collective-permute-start | bytes 196616 | tf_op jit(solution)/shard_map/ppermute | solution.py:29
  27.0 4.3 %collective-permute-start.15 = (bf16[64,512]{1,0:T(8,128)(2,1)S(1)}, bf16[64,512]{1,0:T(8,128)(2,1)S(1)}, u32[]{:S(2)}, u32[]{:S(2)}) collective-permute-start(bf16[64,512]{1,0:T(8,128)(2,1)S(1)} %get-tuple-element.90.refs_4_), channel_id=1, source_target_pairs={{0,4},{1,5},{2,6},{3,7},{4,0},{5,1},{6,2},{7,3},{8,12},{9,13},{10,... | collective-permute-start | bytes 196616 | tf_op jit(solution)/shard_map/ppermute | solution.py:29
  27.1 5.6 %collective-permute-start.17 = (f32[2,256,64]{2,1,0:T(8,128)S(1)}, f32[2,256,64]{2,1,0:T(8,128)S(1)}, u32[]{:S(2)}, u32[]{:S(2)}) collective-permute-start(f32[2,256,64]{2,1,0:T(8,128)S(1)} %get-tuple-element.65), channel_id=1, source_target_pairs={{0,1},{1,0},{2,3},{3,2},{4,5},{5,4},{6,7},{7,6},{8,9},{9,8},{10,11... | collective-permute-start | bytes 393224 | tf_op jit(solution)/shard_map/ppermute | solution.py:29
  27.2 4.5 %collective-permute-start.14 = (bf16[64,512]{1,0:T(8,128)(2,1)S(1)}, bf16[64,512]{1,0:T(8,128)(2,1)S(1)}, u32[]{:S(2)}, u32[]{:S(2)}) collective-permute-start(bf16[64,512]{1,0:T(8,128)(2,1)S(1)} %get-tuple-element.90.refs_4_), channel_id=1, source_target_pairs={{0,2},{1,3},{2,0},{3,1},{4,6},{5,7},{6,4},{7,5},{8,10},{9,11},{10,... | collective-permute-start | bytes 196616 | tf_op jit(solution)/shard_map/ppermute | solution.py:29
  31.3 5.2 %collective-permute-start.16 = (bf16[64,512]{1,0:T(8,128)(2,1)S(1)}, bf16[64,512]{1,0:T(8,128)(2,1)S(1)}, u32[]{:S(2)}, u32[]{:S(2)}) collective-permute-start(bf16[64,512]{1,0:T(8,128)(2,1)S(1)} %get-tuple-element.90.refs_4_), channel_id=1, source_target_pairs={{0,6},{1,7},{2,4},{3,5},{4,2},{5,3},{6,0},{7,1},{8,14},{9,15},{10,... | collective-permute-start | bytes 196616 | tf_op jit(solution)/shard_map/ppermute | solution.py:29
  38.4 5.6 %collective-permute-start.20 = (bf16[64,512]{1,0:T(8,128)(2,1)S(1)}, bf16[64,512]{1,0:T(8,128)(2,1)S(1)}, u32[]{:S(2)}, u32[]{:S(2)}) collective-permute-start(bf16[64,512]{1,0:T(8,128)(2,1)S(1)} %get-tuple-element.70), channel_id=1, source_target_pairs={{0,6},{1,7},{2,4},{3,5},{4,2},{5,3},{6,0},{7,1},{8,14},{9,15},{10,... | collective-permute-start | bytes 196616 | tf_op jit(solution)/shard_map/ppermute | solution.py:29
  44.0 5.2 %collective-permute-start.21 = (bf16[64,512]{1,0:T(8,128)(2,1)S(1)}, bf16[64,512]{1,0:T(8,128)(2,1)S(1)}, u32[]{:S(2)}, u32[]{:S(2)}) collective-permute-start(bf16[64,512]{1,0:T(8,128)(2,1)S(1)} %fusion), channel_id=1, source_target_pairs={{0,8},{1,9},{2,10},{3,11},{4,12},{5,13},{6,14},{7,15},{8,0},{9,1},... | collective-permute-start | bytes 196616 | tf_op jit(solution)/shard_map/ppermute | solution.py:29
  49.3 4.6 %collective-permute-start.23 = (bf16[64,512]{1,0:T(8,128)(2,1)S(1)}, bf16[64,512]{1,0:T(8,128)(2,1)S(1)}, u32[]{:S(2)}, u32[]{:S(2)}) collective-permute-start(bf16[64,512]{1,0:T(8,128)(2,1)S(1)} %get-tuple-element.88.refs_4_), channel_id=1, source_target_pairs={{0,4},{1,5},{2,6},{3,7},{4,0},{5,1},{6,2},{7,3},{8,12},{9,13},{10,... | collective-permute-start | bytes 196616 | tf_op jit(solution)/shard_map/ppermute | solution.py:29
  53.1 5.2 %collective-permute-start.24 = (bf16[64,512]{1,0:T(8,128)(2,1)S(1)}, bf16[64,512]{1,0:T(8,128)(2,1)S(1)}, u32[]{:S(2)}, u32[]{:S(2)}) collective-permute-start(bf16[64,512]{1,0:T(8,128)(2,1)S(1)} %get-tuple-element.88.refs_4_), channel_id=1, source_target_pairs={{0,6},{1,7},{2,4},{3,5},{4,2},{5,3},{6,0},{7,1},{8,14},{9,15},{10,... | collective-permute-start | bytes 196616 | tf_op jit(solution)/shard_map/ppermute | solution.py:29
  59.3 4.3 %collective-permute-start.25 = (bf16[64,512]{1,0:T(8,128)(2,1)S(1)}, bf16[64,512]{1,0:T(8,128)(2,1)S(1)}, u32[]{:S(2)}, u32[]{:S(2)}) collective-permute-start(bf16[64,512]{1,0:T(8,128)(2,1)S(1)} %get-tuple-element.77), channel_id=1, source_target_pairs={{0,2},{1,3},{2,0},{3,1},{4,6},{5,7},{6,4},{7,5},{8,10},{9,11},{10,... | collective-permute-start | bytes 196616 | tf_op jit(solution)/shard_map/ppermute | solution.py:29
  60.4 4.9 %collective-permute-start.26 = (bf16[64,512]{1,0:T(8,128)(2,1)S(1)}, bf16[64,512]{1,0:T(8,128)(2,1)S(1)}, u32[]{:S(2)}, u32[]{:S(2)}) collective-permute-start(bf16[64,512]{1,0:T(8,128)(2,1)S(1)} %get-tuple-element.78), channel_id=1, source_target_pairs={{0,4},{1,5},{2,6},{3,7},{4,0},{5,1},{6,2},{7,3},{8,12},{9,13},{10,... | collective-permute-start | bytes 196616 | tf_op jit(solution)/shard_map/ppermute | solution.py:29
  60.5 5.3 %collective-permute-start.27 = (bf16[64,512]{1,0:T(8,128)(2,1)S(1)}, bf16[64,512]{1,0:T(8,128)(2,1)S(1)}, u32[]{:S(2)}, u32[]{:S(2)}) collective-permute-start(bf16[64,512]{1,0:T(8,128)(2,1)S(1)} %get-tuple-element.79), channel_id=1, source_target_pairs={{0,6},{1,7},{2,4},{3,5},{4,2},{5,3},{6,0},{7,1},{8,14},{9,15},{10,... | collective-permute-start | bytes 196616 | tf_op jit(solution)/shard_map/ppermute | solution.py:29
  65.8 5.2 %collective-permute-start.28 = (bf16[64,512]{1,0:T(8,128)(2,1)S(1)}, bf16[64,512]{1,0:T(8,128)(2,1)S(1)}, u32[]{:S(2)}, u32[]{:S(2)}) collective-permute-start(bf16[64,512]{1,0:T(8,128)(2,1)S(1)} %fusion.1), channel_id=1, source_target_pairs={{0,8},{1,9},{2,10},{3,11},{4,12},{5,13},{6,14},{7,15},{8,0},{9,1},... | collective-permute-start | bytes 196616 | tf_op jit(solution)/shard_map/ppermute | solution.py:29
  71.1 4.3 %collective-permute-start.31 = (bf16[64,512]{1,0:T(8,128)(2,1)S(1)}, bf16[64,512]{1,0:T(8,128)(2,1)S(1)}, u32[]{:S(2)}, u32[]{:S(2)}) collective-permute-start(bf16[64,512]{1,0:T(8,128)(2,1)S(1)} %get-tuple-element.86.refs_4_), channel_id=1, source_target_pairs={{0,4},{1,5},{2,6},{3,7},{4,0},{5,1},{6,2},{7,3},{8,12},{9,13},{10,... | collective-permute-start | bytes 196616 | tf_op jit(solution)/shard_map/ppermute | solution.py:29
  74.2 5.2 %collective-permute-start.32 = (bf16[64,512]{1,0:T(8,128)(2,1)S(1)}, bf16[64,512]{1,0:T(8,128)(2,1)S(1)}, u32[]{:S(2)}, u32[]{:S(2)}) collective-permute-start(bf16[64,512]{1,0:T(8,128)(2,1)S(1)} %get-tuple-element.86.refs_4_), channel_id=1, source_target_pairs={{0,6},{1,7},{2,4},{3,5},{4,2},{5,3},{6,0},{7,1},{8,14},{9,15},{10,... | collective-permute-start | bytes 196616 | tf_op jit(solution)/shard_map/ppermute | solution.py:29
  (15 other events, 73.0 us)

commit v4 on v3

--- a/solution.py
+++ b/solution.py
@@ -35,12 +35,9 @@
     )
 
 
-def first_kernel(span, chunks, at_hbm, tile_hbm, dual_ref, *rest):
-    high_ref, low_ref = rest[:2]
-    keeps, sends = rest[2 : 2 + QUAD], rest[2 + QUAD : 2 + 2 * QUAD]
-    at_s, tile_s, acc, sems = rest[2 + 2 * QUAD :]
+def dense_kernel(span, chunks, at_hbm, tile_hbm, a_ref, at_s, tile_s, acc, sems):
     tiles, size, _ = tile_s.shape
-    row_blocks = high_ref.shape[1] // size
+    row_blocks = a_ref.shape[2] // size
     step = tiles // chunks
     index_copy = pltpu.make_async_copy(at_hbm, at_s, sems.at[0])
     tile_copies = [
@@ -52,7 +49,6 @@
     for copy in [index_copy] + tile_copies:
         copy.start()
     acc[...] = jnp.zeros_like(acc)
-    low = dual_ref[...].astype(BF16).T
 
     def add(t, _):
         at = at_s[t]
@@ -71,37 +67,44 @@
             block = acc[column * row_blocks + r]
             high = block.astype(BF16)
             rows = pl.ds(r * size, size)
-            high_ref[q, rows, cols] = high
-            low_ref[q, rows, cols] = (block - high.astype(F32)).astype(BF16)
-    _, me, core = place()
-    half = keeps[0].shape[0]
-    for k in range(QUAD):
-        total = dot(low, high_ref[me ^ k], 1, 0) + dot(low, low_ref[me ^ k], 1, 0)
-        keeps[k][...] = jnp.where(core == 0, total[:half], total[half:])
-        sends[k][...] = jnp.where(core == 0, total[half:], total[:half])
-
-
-def first_columns(tile_values, at, dual, span, columns, half):
+            a_ref[0, q, rows, cols] = high
+            a_ref[1, q, rows, cols] = (block - high.astype(F32)).astype(BF16)
+
+
+def dense(tile_values, at, span, columns, rows):
     tiles, size, _ = tile_values.shape
-    rows = dual.shape[0]
-    wide = columns * size // QUAD
     chunks = 4 if tiles % 16 == 0 else 1
     any_spec = pl.BlockSpec(memory_space=pltpu.HBM)
-    part = jax.ShapeDtypeStruct((half, wide), F32)
-    out = pl.pallas_call(
-        functools.partial(first_kernel, span, chunks),
-        out_shape=(jax.ShapeDtypeStruct((QUAD, rows, wide), BF16),) * 2 + (part,) * (2 * QUAD),
-        in_specs=[any_spec, any_spec, VMEM],
-        out_specs=(VMEM,) * (2 + 2 * QUAD),
+    return pl.pallas_call(
+        functools.partial(dense_kernel, span, chunks),
+        out_shape=jax.ShapeDtypeStruct((2, QUAD, rows, columns * size // QUAD), BF16),
+        in_specs=[any_spec, any_spec],
+        out_specs=VMEM,
         scratch_shapes=[
             pltpu.SMEM((tiles,), jnp.int32),
             pltpu.VMEM((tiles, size, size), BF16),
             pltpu.VMEM((columns * rows // size, size, size), F32),
             pltpu.SemaphoreType.DMA((1 + chunks,)),
         ],
-        compiler_params=pltpu.CompilerParams(vmem_limit_bytes=49 * 2**20),
-    )(at, tile_values, dual)
-    return out[:2], out[2 : 2 + QUAD], out[2 + QUAD :]
+        compiler_params=pltpu.CompilerParams(vmem_limit_bytes=50 * 2**20),
+    )(at, tile_values)
+
+
+def first_kernel(a_ref, dual_ref, primal_ref, cost_ref, limit_ref, mine_ref, other_ref, *rest):
+    keeps, sends = rest[:QUAD], rest[QUAD:]
+    _, me, core = place()
+    half = keeps[0].shape[0]
+    for at, ref in ((0, primal_ref), (half + 8, cost_ref)):
+        turned = ref[...].T
+        mine_ref[at : at + half] = jnp.where(core == 0, turned[:half], turned[half:])
+        other_ref[at : at + half] = jnp.where(core == 0, turned[half:], turned[:half])
+    for ref in (mine_ref, other_ref):
+        ref[half : half + 8] = jnp.broadcast_to(limit_ref[...], (8, limit_ref.shape[1]))
+    low = dual_ref[...].astype(BF16).T
+    for k in range(QUAD):
+        total = dot(low, a_ref[0, me ^ k], 1, 0) + dot(low, a_ref[1, me ^ k], 1, 0)
+        keeps[k][...] = jnp.where(core == 0, total[:half], total[half:])
+        sends[k][...] = jnp.where(core == 0, total[half:], total[:half])
 
 
 def prepare_kernel(dual, bound, mine, other):
@@ -139,31 +142,27 @@
     )
 
 
-def variables_kernel(*refs):
-    packs, costs, (primal_ref, cost_ref, limit_ref) = refs[:-5], refs[-5:-3], refs[-3:]
+def variables_kernel(mine, other, *refs):
+    fars, (primal_ref, cost_ref, limit_ref) = refs[:-3], refs[-3:]
     far, _, core = place()
-    width = costs[0].shape[0]
     half = primal_ref.shape[0]
-
-    def turn(block):
-        turned = block.T
-        return jnp.where(core == 0, turned[:half], turned[half:])
-
+    width = mine.shape[1]
     cost_ref[...] = jnp.zeros_like(cost_ref)
-    for j, ref in enumerate(packs):
+    blocks = [(mine, 0), (other, 0)] + [(f, at) for f in fars for at in (0, half + 8)]
+    for j, (ref, at) in enumerate(blocks):
         owner = (far * CORES + core) ^ j
         cols = pl.ds(pl.multiple_of(owner * width, width), width)
-        primal_ref[:, cols] = turn(ref[:width])
-        limit_ref[:, cols] = ref[width : width + 1]
+        primal_ref[:, cols] = ref[at : at + half]
+        limit_ref[:, cols] = ref[at + half : at + half + 1]
         if j < CORES:
-            cost_ref[:, cols] = turn(costs[j][...])
+            cost_ref[:, cols] = ref[half + 8 :]
 
 
 def row_product(a, pieces, members, me):
     total = None
     for piece, k in zip(pieces, members):
         for h in range(2):
-            part = dot(a[h][me ^ k], piece[...], 1, 1)
+            part = dot(a[h, me ^ k], piece[...], 1, 1)
             total = part if total is None else total + part
     return total
 
@@ -172,22 +171,22 @@
     total = None
     for i in range(2):
         for h in range(2):
-            part = dot(low[i], a[i][h][member], 1, 0)
+            part = dot(low[i], a[i][h, member], 1, 0)
             total = part if total is None else total + part
     return total
 
 
 def near_rows_kernel(*refs):
-    a, pieces, images = (refs[0:2], refs[2:4]), refs[4 : 3 + QUAD], refs[3 + QUAD :]
+    a, pieces, images = refs[0:2], refs[2 : 1 + QUAD], refs[1 + QUAD :]
     me = place()[1]
     for i in range(2):
         images[i][...] = row_product(a[i], pieces, range(QUAD - 1), me)
 
 
 def turn_kernel(first, *refs):
-    a, images, last, sides = (refs[0:2], refs[2:4]), refs[4:6], refs[6], refs[7:9]
-    at = 9 if first else 11
-    duals = [s.at[0] for s in sides] if first else refs[9:11]
+    a, images, last, sides = refs[0:2], refs[2:4], refs[4], refs[5:7]
+    at = 7 if first else 9
+    duals = [s.at[0] for s in sides] if first else refs[7:9]
     stepped, lows, pieces = refs[at : at + 2], refs[at + 2 : at + 4], refs[at + 4 :]
     me = place()[1]
     low = []
@@ -202,15 +201,15 @@
 
 
 def own_columns_kernel(*refs):
-    a, lows, got, out = (refs[0:2], refs[2:4]), refs[4:6], refs[6:-1], refs[-1]
+    a, lows, got, out = refs[0:2], refs[2:4], refs[4:-1], refs[-1]
     total = column_product([r[...] for r in lows], a, place()[1])
     for piece in got:
         total = total + piece[...].astype(F32)
     out[...] = total
 
 
-def finish_kernel(high, low, image, last, side, dual, out):
-    total = image[...] + row_product((high, low), (last,), (QUAD - 1,), place()[1])
+def finish_kernel(a, image, last, side, dual, out):
+    total = image[...] + row_product(a, (last,), (QUAD - 1,), place()[1])
     out[...] = jnp.maximum(dual[...] + STEP * (side[1] - total), 0.0)
 
 
@@ -243,33 +242,39 @@
             compiler_params=limits,
         )(*operands)
 
-    own, keeps, sends = first_columns(
-        tile_values, tile_col * (rows // size) + tile_row, dual_start, span, devices * span, half
-    )
+    own = dense(
+        tile_values, tile_col * (rows // size) + tile_row, span, devices * span, rows
+    )
+    packed = jax.ShapeDtypeStruct((2 * half + 8, width), F32)
+    out = call(
+        first_kernel,
+        (packed, packed) + (state,) * (2 * QUAD),
+        own,
+        dual_start,
+        primal_start,
+        objective,
+        upper_bound[None, :],
+    )
+    (pack, pack_out), keeps, sends = out[:2], out[2 : 2 + QUAD], out[2 + QUAD :]
+    pack_in = swap(pack_out, 1)
+    fars = [jnp.concatenate([pack[: half + 8], pack_in[: half + 8]], 0)]
+    for mask in far_masks:
+        fars = fars + [swap(f, mask) for f in fars]
     sums = [k + swap(s, 1) for k, s in zip(keeps, sends)]
     pieces = [s.astype(BF16) for s in sums[1:]]
     got = [swap(p, k * CORES) for k, p in enumerate(pieces, 1)]
 
-    pack = jnp.concatenate(
-        [primal_start, jnp.broadcast_to(upper_bound[None, :], (8, width))], 0
-    )
-    packs = [pack]
-    for mask in far_masks:
-        packs = packs + [swap(p, mask) for p in packs]
-    later, _ = lax.optimization_barrier((packs[1:], got[:]))
-    mates = [swap(p, 1) for p in [pack, *later]]
-    packs = [p for pair in zip(packs, mates) for p in pair]
     primal, cost, limit = call(
         variables_kernel,
         (state, state, jax.ShapeDtypeStruct((1, wide), F32)),
-        *packs,
-        objective,
-        swap(objective, 1),
+        pack,
+        pack_in,
+        *fars[1:],
     )
     sent, dual_start, row_bound, _, _ = lax.optimization_barrier(
         (own, dual_start, row_bound, pieces, sums[0])
     )
-    a = (*own, *[swap(s, 1) for s in sent])
+    a = (own, swap(sent, 1))
     halves = jax.ShapeDtypeStruct((2, rows, half), F32)
     mine, other = call(prepare_kernel, (halves, halves), dual_start, row_bound)
     sides = (mine, swap(other, 1))
@@ -290,6 +295,12 @@
         ahead = (2.0 * updated - primal).astype(BF16)
         primal = updated
         around = [ahead] + [swap(ahead, k * CORES) for k in range(1, QUAD)]
+        if iteration == ITERS - 1:
+            part = jax.ShapeDtypeStruct((half, width), F32)
+            mine, other = call(give_kernel, (part, part), primal)
+            near, mine, other = lax.optimization_barrier((around[:-1], mine, swap(other, 1)))
+            around = [*near, around[-1]]
+            held = (mine, other)
         images = call(near_rows_kernel, (side, side), *a, *around[:-1])
         if iteration < ITERS - 1:
             out = call(
@@ -305,18 +316,14 @@
             )
             duals, lows, pieces = out[0:2], out[2:4], out[4:]
 
-    part = jax.ShapeDtypeStruct((half, width), F32)
-    mine, other = call(give_kernel, (part, part), primal)
-    primal = call(
-        join_variables_kernel,
-        jax.ShapeDtypeStruct((width, scenarios), F32),
-        mine,
-        swap(other, 1),
-    )
     mine, other = [
-        call(finish_kernel, side, *a[2 * i : 2 * i + 2], images[i], around[-1], sides[i], duals[i])
+        call(finish_kernel, side, a[i], images[i], around[-1], sides[i], duals[i])
         for i in range(2)
     ]
+    first, second, _ = lax.optimization_barrier((*held, other))
+    primal = call(
+        join_variables_kernel, jax.ShapeDtypeStruct((width, scenarios), F32), first, second
+    )
     dual = call(
         join_rows_kernel, jax.ShapeDtypeStruct((rows, scenarios), F32), mine, swap(other, 1)
     )

time: 83.2 us -> 77.2 us (0.928)
  starting transfers between devices: 31.9 us -> 27.8 us
  waiting for transfers between devices: 37.7 us -> 36.7 us
  local copies, waits for them, and re-layouts: 0.92 us -> 0.03 us
    ppermute x34 -> x31, starting transfers between devices: 31.9 us -> 27.8 us  [swap(): lax.ppermute(x, 'row', [(i, i ^ mask) for i in range(lax.axis_size('row'))])]
    ppermute x34 -> x31, waiting for transfers between devices: 37.7 us -> 36.7 us  [swap(): lax.ppermute(x, 'row', [(i, i ^ mask) for i in range(lax.axis_size('row'))])]
    unnamed x10, local copies, waits for them, and re-layouts: 0.92 us -> 0.02 us
    pallas_call x14 -> x15, Pallas kernels: 8.05 us -> 8.36 us  [call(): pl.pallas_call(kernel, out_shape=out_shape, in_specs=[VMEM] * len(operand...]
  transfers between devices with their start and end apart: 34 -> 31, of which waited for: 22 -> 21; matrix products, arithmetic and copies ran while one was open for 0% -> 0% of each run, Pallas kernels for 6% -> 6%
where the time goes in v4:
time: 77.2 us; the launch traced here: 77 us
  waiting for transfers between devices  36.7 us (48%)
  starting transfers between devices  27.8 us (36%)
  Pallas kernels  10.4 us (13%)
  other arithmetic  1.02 us (1%)
  between operations  0.91 us (1%)
    ppermute x31, waiting for transfers between devices, swap(): lax.ppermute(x, 'row', [(i, i ^ mask) for i in range(lax.axis_size('row'))])  36.7 us
    ppermute x31, starting transfers between devices, swap(): lax.ppermute(x, 'row', [(i, i ^ mask) for i in range(lax.axis_size('row'))])  27.8 us
    pallas_call x15, Pallas kernels, call(): pl.pallas_call(kernel, out_shape=out_shape, in_specs=[VMEM] * len(operand...  8.36 us
    pallas_call x1, Pallas kernels, dense(): pl.pallas_call(functools.partial(dense_kernel, span, chunks), out_shape=j...  2.06 us
  transfers between devices with their start and end apart: 31, of which 21 were waited for; matrix products, arithmetic and copies ran while one was open for 0% of the time, Pallas kernels for 6%

profile of v4, /device:TPU:0, one launch (start us, length us, event | category | flops | bytes accessed | tf_op | source)
XLA Modules:
  0.0 77.0 jit_solution(7266320914143508403)
XLA Ops:
  1.3 2.1 %shard_map.95.a_ref.refs_0_.a = bf16[2,4,256,512]{3,2,1,0:T(8,128)(2,1)S(1)} custom-call(s32[64]{0:T(128)S(1)} %multiply_add_fusion.at_hbm, bf16[64,128,128]{2,1,0:T(8,128)(2,1)} %tile_hbm.1), custom_call_target="tpu_custom_call" | custom-call | tf_op jit(solution)/shard_map/pallas_call | solution.py:78
  5.5 3.9 %collective-permute-start.1 = (f32[144,128]{1,0:T(8,128)S(1)}, f32[144,128]{1,0:T(8,128)S(1)}, u32[]{:S(2)}, u32[]{:S(2)}) collective-permute-start(f32[144,128]{1,0:T(8,128)S(1)} %pad_maximum_fusion), channel_id=1, source_target_pairs={{0,8},{1,9},{2,10},{3,11},{4,12},{5,13},{6,14},{7,15},{8,0},{9,1},... | collective-permute-start | bytes 221192 | tf_op jit(solution)/shard_map/ppermute | solution.py:29
  9.4 1.6 %collective-permute-start.4 = (bf16[64,512]{1,0:T(8,128)(2,1)S(1)}, bf16[64,512]{1,0:T(8,128)(2,1)S(1)}, u32[]{:S(2)}, u32[]{:S(2)}) collective-permute-start(bf16[64,512]{1,0:T(8,128)(2,1)S(1)} %add_convert_fusion.2), channel_id=1, source_target_pairs={{0,2},{1,3},{2,0},{3,1},{4,6},{5,7},{6,4},{7,5},{8,10},{9,11},{10,... | collective-permute-start | bytes 196616 | tf_op jit(solution)/shard_map/ppermute | solution.py:29
  11.0 1.6 %collective-permute-start.6 = (bf16[64,512]{1,0:T(8,128)(2,1)S(1)}, bf16[64,512]{1,0:T(8,128)(2,1)S(1)}, u32[]{:S(2)}, u32[]{:S(2)}) collective-permute-start(bf16[64,512]{1,0:T(8,128)(2,1)S(1)} %add_convert_fusion.1), channel_id=1, source_target_pairs={{0,4},{1,5},{2,6},{3,7},{4,0},{5,1},{6,2},{7,3},{8,12},{9,13},{10,... | collective-permute-start | bytes 196616 | tf_op jit(solution)/shard_map/ppermute | solution.py:29
  13.7 2.2 %collective-permute-done.6 = bf16[64,512]{1,0:T(8,128)(2,1)S(1)} collective-permute-done((bf16[64,512]{1,0:T(8,128)(2,1)S(1)}, bf16[64,512]{1,0:T(8,128)(2,1)S(1)}, u32[]{:S(2)}, u32[]{:S(2)}) %collective-permute-start.6) | collective-permute-done | bytes 65568 | tf_op jit(solution)/shard_map/ppermute | solution.py:29
  15.9 2.0 %collective-permute-done.8 = bf16[64,512]{1,0:T(8,128)(2,1)S(1)} collective-permute-done((bf16[64,512]{1,0:T(8,128)(2,1)S(1)}, bf16[64,512]{1,0:T(8,128)(2,1)S(1)}, u32[]{:S(2)}, u32[]{:S(2)}) %collective-permute-start.8) | collective-permute-done | bytes 65568 | tf_op jit(solution)/shard_map/ppermute | solution.py:29
  18.9 5.8 %collective-permute-done.9 = bf16[64,512]{1,0:T(8,128)(2,1)S(1)} collective-permute-done((bf16[64,512]{1,0:T(8,128)(2,1)S(1)}, bf16[64,512]{1,0:T(8,128)(2,1)S(1)}, u32[]{:S(2)}, u32[]{:S(2)}) %collective-permute-start.9) | collective-permute-done | bytes 65568 | tf_op jit(solution)/shard_map/ppermute | solution.py:29
  25.5 2.8 %collective-permute-start.13 = (bf16[64,512]{1,0:T(8,128)(2,1)S(1)}, bf16[64,512]{1,0:T(8,128)(2,1)S(1)}, u32[]{:S(2)}, u32[]{:S(2)}) collective-permute-start(bf16[64,512]{1,0:T(8,128)(2,1)S(1)} %get-tuple-element.100.refs_2_), channel_id=1, source_target_pairs={{0,6},{1,7},{2,4},{3,5},{4,2},{5,3},{6,0},{7,1},{8,14},{9,15},{10,... | collective-permute-start | bytes 196616 | tf_op jit(solution)/shard_map/ppermute | solution.py:29
  28.3 1.2 %collective-permute-done.12.refs_4_ = bf16[64,512]{1,0:T(8,128)(2,1)S(1)} collective-permute-done((bf16[64,512]{1,0:T(8,128)(2,1)S(1)}, bf16[64,512]{1,0:T(8,128)(2,1)S(1)}, u32[]{:S(2)}, u32[]{:S(2)}) %collective-permute-start.12) | collective-permute-done | bytes 65568 | tf_op jit(solution)/shard_map/ppermute | solution.py:29
  31.7 1.5 %collective-permute-start.15 = (bf16[64,512]{1,0:T(8,128)(2,1)S(1)}, bf16[64,512]{1,0:T(8,128)(2,1)S(1)}, u32[]{:S(2)}, u32[]{:S(2)}) collective-permute-start(bf16[64,512]{1,0:T(8,128)(2,1)S(1)} %get-tuple-element.71), channel_id=1, source_target_pairs={{0,2},{1,3},{2,0},{3,1},{4,6},{5,7},{6,4},{7,5},{8,10},{9,11},{10,... | collective-permute-start | bytes 196616 | tf_op jit(solution)/shard_map/ppermute | solution.py:29
  33.2 1.9 %collective-permute-start.16 = (bf16[64,512]{1,0:T(8,128)(2,1)S(1)}, bf16[64,512]{1,0:T(8,128)(2,1)S(1)}, u32[]{:S(2)}, u32[]{:S(2)}) collective-permute-start(bf16[64,512]{1,0:T(8,128)(2,1)S(1)} %get-tuple-element.72), channel_id=1, source_target_pairs={{0,4},{1,5},{2,6},{3,7},{4,0},{5,1},{6,2},{7,3},{8,12},{9,13},{10,... | collective-permute-start | bytes 196616 | tf_op jit(solution)/shard_map/ppermute | solution.py:29
  36.1 1.4 %collective-permute-done.16.refs_5_ = bf16[64,512]{1,0:T(8,128)(2,1)S(1)} collective-permute-done((bf16[64,512]{1,0:T(8,128)(2,1)S(1)}, bf16[64,512]{1,0:T(8,128)(2,1)S(1)}, u32[]{:S(2)}, u32[]{:S(2)}) %collective-permute-start.16) | collective-permute-done | bytes 65568 | tf_op jit(solution)/shard_map/ppermute | solution.py:29
  37.8 2.5 %collective-permute-done.17 = bf16[64,512]{1,0:T(8,128)(2,1)S(1)} collective-permute-done((bf16[64,512]{1,0:T(8,128)(2,1)S(1)}, bf16[64,512]{1,0:T(8,128)(2,1)S(1)}, u32[]{:S(2)}, u32[]{:S(2)}) %collective-permute-start.17) | collective-permute-done | bytes 65568 | tf_op jit(solution)/shard_map/ppermute | solution.py:29
  40.4 5.6 %collective-permute-done.18 = bf16[64,512]{1,0:T(8,128)(2,1)S(1)} collective-permute-done((bf16[64,512]{1,0:T(8,128)(2,1)S(1)}, bf16[64,512]{1,0:T(8,128)(2,1)S(1)}, u32[]{:S(2)}, u32[]{:S(2)}) %collective-permute-start.18) | collective-permute-done | bytes 65568 | tf_op jit(solution)/shard_map/ppermute | solution.py:29
  47.2 2.5 %collective-permute-start.21 = (bf16[64,512]{1,0:T(8,128)(2,1)S(1)}, bf16[64,512]{1,0:T(8,128)(2,1)S(1)}, u32[]{:S(2)}, u32[]{:S(2)}) collective-permute-start(bf16[64,512]{1,0:T(8,128)(2,1)S(1)} %get-tuple-element.98.refs_2_), channel_id=1, source_target_pairs={{0,6},{1,7},{2,4},{3,5},{4,2},{5,3},{6,0},{7,1},{8,14},{9,15},{10,... | collective-permute-start | bytes 196616 | tf_op jit(solution)/shard_map/ppermute | solution.py:29
  51.7 1.0 %collective-permute-done.21.refs_4_ = bf16[64,512]{1,0:T(8,128)(2,1)S(1)} collective-permute-done((bf16[64,512]{1,0:T(8,128)(2,1)S(1)}, bf16[64,512]{1,0:T(8,128)(2,1)S(1)}, u32[]{:S(2)}, u32[]{:S(2)}) %collective-permute-start.21) | collective-permute-done | bytes 65568 | tf_op jit(solution)/shard_map/ppermute | solution.py:29
  53.8 1.7 %collective-permute-start.22 = (bf16[64,512]{1,0:T(8,128)(2,1)S(1)}, bf16[64,512]{1,0:T(8,128)(2,1)S(1)}, u32[]{:S(2)}, u32[]{:S(2)}) collective-permute-start(bf16[64,512]{1,0:T(8,128)(2,1)S(1)} %get-tuple-element.80), channel_id=1, source_target_pairs={{0,2},{1,3},{2,0},{3,1},{4,6},{5,7},{6,4},{7,5},{8,10},{9,11},{10,... | collective-permute-start | bytes 196616 | tf_op jit(solution)/shard_map/ppermute | solution.py:29
  55.5 1.8 %collective-permute-start.23 = (bf16[64,512]{1,0:T(8,128)(2,1)S(1)}, bf16[64,512]{1,0:T(8,128)(2,1)S(1)}, u32[]{:S(2)}, u32[]{:S(2)}) collective-permute-start(bf16[64,512]{1,0:T(8,128)(2,1)S(1)} %get-tuple-element.81), channel_id=1, source_target_pairs={{0,4},{1,5},{2,6},{3,7},{4,0},{5,1},{6,2},{7,3},{8,12},{9,13},{10,... | collective-permute-start | bytes 196616 | tf_op jit(solution)/shard_map/ppermute | solution.py:29
  58.1 1.8 %collective-permute-done.23.refs_5_ = bf16[64,512]{1,0:T(8,128)(2,1)S(1)} collective-permute-done((bf16[64,512]{1,0:T(8,128)(2,1)S(1)}, bf16[64,512]{1,0:T(8,128)(2,1)S(1)}, u32[]{:S(2)}, u32[]{:S(2)}) %collective-permute-start.23) | collective-permute-done | bytes 65568 | tf_op jit(solution)/shard_map/ppermute | solution.py:29
  60.2 2.5 %collective-permute-done.24 = bf16[64,512]{1,0:T(8,128)(2,1)S(1)} collective-permute-done((bf16[64,512]{1,0:T(8,128)(2,1)S(1)}, bf16[64,512]{1,0:T(8,128)(2,1)S(1)}, u32[]{:S(2)}, u32[]{:S(2)}) %collective-permute-start.24) | collective-permute-done | bytes 65568 | tf_op jit(solution)/shard_map/ppermute | solution.py:29
  62.8 5.3 %collective-permute-done.25 = bf16[64,512]{1,0:T(8,128)(2,1)S(1)} collective-permute-done((bf16[64,512]{1,0:T(8,128)(2,1)S(1)}, bf16[64,512]{1,0:T(8,128)(2,1)S(1)}, u32[]{:S(2)}, u32[]{:S(2)}) %collective-permute-start.25) | collective-permute-done | bytes 65568 | tf_op jit(solution)/shard_map/ppermute | solution.py:29
  68.2 1.1 %collective-permute-start.26 = (bf16[64,512]{1,0:T(8,128)(2,1)S(1)}, bf16[64,512]{1,0:T(8,128)(2,1)S(1)}, u32[]{:S(2)}, u32[]{:S(2)}) collective-permute-start(bf16[64,512]{1,0:T(8,128)(2,1)S(1)} %get-tuple-element.87.refs_2_), channel_id=1, source_target_pairs={{0,2},{1,3},{2,0},{3,1},{4,6},{5,7},{6,4},{7,5},{8,10},{9,11},{10,... | collective-permute-start | bytes 196616 | tf_op jit(solution)/shard_map/ppermute | solution.py:29
  69.3 2.4 %collective-permute-start.29 = (bf16[64,512]{1,0:T(8,128)(2,1)S(1)}, bf16[64,512]{1,0:T(8,128)(2,1)S(1)}, u32[]{:S(2)}, u32[]{:S(2)}) collective-permute-start(bf16[64,512]{1,0:T(8,128)(2,1)S(1)} %get-tuple-element.87.refs_2_), channel_id=1, source_target_pairs={{0,6},{1,7},{2,4},{3,5},{4,2},{5,3},{6,0},{7,1},{8,14},{9,15},{10,... | collective-permute-start | bytes 196616 | tf_op jit(solution)/shard_map/ppermute | solution.py:29
  71.8 1.2 %collective-permute-done.28.other = f32[64,128]{1,0:T(8,128)S(1)} collective-permute-done((f32[64,128]{1,0:T(8,128)S(1)}, f32[64,128]{1,0:T(8,128)S(1)}, u32[]{:S(2)}, u32[]{:S(2)}) %collective-permute-start.28) | collective-permute-done | bytes 32800 | tf_op jit(solution)/shard_map/ppermute | solution.py:29
  (77 shorter events, 18.7 us)
Async XLA Ops:
  4.4 4.9 %collective-permute-start.3 = (f32[64,512]{1,0:T(8,128)S(1)}, f32[64,512]{1,0:T(8,128)S(1)}, u32[]{:S(2)}, u32[]{:S(2)}) collective-permute-start(f32[64,512]{1,0:T(8,128)S(1)} %get-tuple-element.57), channel_id=1, source_target_pairs={{0,1},{1,0},{2,3},{3,2},{4,5},{5,4},{6,7},{7,6},{8,9},{9,8},{10,11... | collective-permute-start | bytes 393224 | tf_op jit(solution)/shard_map/ppermute | solution.py:29
  4.5 9.2 %collective-permute-start.2 = (f32[64,512]{1,0:T(8,128)S(1)}, f32[64,512]{1,0:T(8,128)S(1)}, u32[]{:S(2)}, u32[]{:S(2)}) collective-permute-start(f32[64,512]{1,0:T(8,128)S(1)} %get-tuple-element.54), channel_id=1, source_target_pairs={{0,1},{1,0},{2,3},{3,2},{4,5},{5,4},{6,7},{7,6},{8,9},{9,8},{10,11... | collective-permute-start | bytes 393224 | tf_op jit(solution)/shard_map/ppermute | solution.py:29
  4.9 6.0 %collective-permute-start.5 = (f32[64,512]{1,0:T(8,128)S(1)}, f32[64,512]{1,0:T(8,128)S(1)}, u32[]{:S(2)}, u32[]{:S(2)}) collective-permute-start(f32[64,512]{1,0:T(8,128)S(1)} %get-tuple-element.59), channel_id=1, source_target_pairs={{0,1},{1,0},{2,3},{3,2},{4,5},{5,4},{6,7},{7,6},{8,9},{9,8},{10,11... | collective-permute-start | bytes 393224 | tf_op jit(solution)/shard_map/ppermute | solution.py:29
  5.0 7.6 %collective-permute-start.7 = (f32[64,512]{1,0:T(8,128)S(1)}, f32[64,512]{1,0:T(8,128)S(1)}, u32[]{:S(2)}, u32[]{:S(2)}) collective-permute-start(f32[64,512]{1,0:T(8,128)S(1)} %get-tuple-element.61), channel_id=1, source_target_pairs={{0,1},{1,0},{2,3},{3,2},{4,5},{5,4},{6,7},{7,6},{8,9},{9,8},{10,11... | collective-permute-start | bytes 393224 | tf_op jit(solution)/shard_map/ppermute | solution.py:29
  5.5 8.2 %collective-permute-start.1 = (f32[144,128]{1,0:T(8,128)S(1)}, f32[144,128]{1,0:T(8,128)S(1)}, u32[]{:S(2)}, u32[]{:S(2)}) collective-permute-start(f32[144,128]{1,0:T(8,128)S(1)} %pad_maximum_fusion), channel_id=1, source_target_pairs={{0,8},{1,9},{2,10},{3,11},{4,12},{5,13},{6,14},{7,15},{8,0},{9,1},... | collective-permute-start | bytes 221192 | tf_op jit(solution)/shard_map/ppermute | solution.py:29
  9.4 4.3 %collective-permute-start.4 = (bf16[64,512]{1,0:T(8,128)(2,1)S(1)}, bf16[64,512]{1,0:T(8,128)(2,1)S(1)}, u32[]{:S(2)}, u32[]{:S(2)}) collective-permute-start(bf16[64,512]{1,0:T(8,128)(2,1)S(1)} %add_convert_fusion.2), channel_id=1, source_target_pairs={{0,2},{1,3},{2,0},{3,1},{4,6},{5,7},{6,4},{7,5},{8,10},{9,11},{10,... | collective-permute-start | bytes 196616 | tf_op jit(solution)/shard_map/ppermute | solution.py:29
  11.0 4.9 %collective-permute-start.6 = (bf16[64,512]{1,0:T(8,128)(2,1)S(1)}, bf16[64,512]{1,0:T(8,128)(2,1)S(1)}, u32[]{:S(2)}, u32[]{:S(2)}) collective-permute-start(bf16[64,512]{1,0:T(8,128)(2,1)S(1)} %add_convert_fusion.1), channel_id=1, source_target_pairs={{0,4},{1,5},{2,6},{3,7},{4,0},{5,1},{6,2},{7,3},{8,12},{9,13},{10,... | collective-permute-start | bytes 196616 | tf_op jit(solution)/shard_map/ppermute | solution.py:29
  12.7 5.2 %collective-permute-start.8 = (bf16[64,512]{1,0:T(8,128)(2,1)S(1)}, bf16[64,512]{1,0:T(8,128)(2,1)S(1)}, u32[]{:S(2)}, u32[]{:S(2)}) collective-permute-start(bf16[64,512]{1,0:T(8,128)(2,1)S(1)} %add_convert_fusion), channel_id=1, source_target_pairs={{0,6},{1,7},{2,4},{3,5},{4,2},{5,3},{6,0},{7,1},{8,14},{9,15},{10,... | collective-permute-start | bytes 196616 | tf_op jit(solution)/shard_map/ppermute | solution.py:29
  18.0 11.7 %collective-permute-start.10 = (bf16[2,4,256,512]{3,2,1,0:T(8,128)(2,1)S(1)}, bf16[2,4,256,512]{3,2,1,0:T(8,128)(2,1)S(1)}, u32[]{:S(2)}, u32[]{:S(2)}) collective-permute-start(bf16[2,4,256,512]{3,2,1,0:T(8,128)(2,1)S(1)} %shard_map.95.a_ref.refs_0_.a), channel_id=1, source_target_pairs={{0,1},{1,0},{2,3},{3,2},{4,5},{5,4},{6,7},{7,6},{8,9},{9,8},{10,11... | collective-permute-start | bytes 6291464 | tf_op jit(solution)/shard_map/ppermute | solution.py:29
  18.0 6.7 %collective-permute-start.9 = (bf16[64,512]{1,0:T(8,128)(2,1)S(1)}, bf16[64,512]{1,0:T(8,128)(2,1)S(1)}, u32[]{:S(2)}, u32[]{:S(2)}) collective-permute-start(bf16[64,512]{1,0:T(8,128)(2,1)S(1)} %get-tuple-element.102), channel_id=1, source_target_pairs={{0,8},{1,9},{2,10},{3,11},{4,12},{5,13},{6,14},{7,15},{8,0},{9,1},... | collective-permute-start | bytes 196616 | tf_op jit(solution)/shard_map/ppermute | solution.py:29
  18.7 12.0 %collective-permute-start.14 = (f32[2,256,64]{2,1,0:T(8,128)S(1)}, f32[2,256,64]{2,1,0:T(8,128)S(1)}, u32[]{:S(2)}, u32[]{:S(2)}) collective-permute-start(f32[2,256,64]{2,1,0:T(8,128)S(1)} %get-tuple-element.68), channel_id=1, source_target_pairs={{0,1},{1,0},{2,3},{3,2},{4,5},{5,4},{6,7},{7,6},{8,9},{9,8},{10,11... | collective-permute-start | bytes 393224 | tf_op jit(solution)/shard_map/ppermute | solution.py:29
  24.8 4.8 %collective-permute-start.12 = (bf16[64,512]{1,0:T(8,128)(2,1)S(1)}, bf16[64,512]{1,0:T(8,128)(2,1)S(1)}, u32[]{:S(2)}, u32[]{:S(2)}) collective-permute-start(bf16[64,512]{1,0:T(8,128)(2,1)S(1)} %get-tuple-element.100.refs_2_), channel_id=1, source_target_pairs={{0,4},{1,5},{2,6},{3,7},{4,0},{5,1},{6,2},{7,3},{8,12},{9,13},{10,... | collective-permute-start | bytes 196616 | tf_op jit(solution)/shard_map/ppermute | solution.py:29
  24.9 4.8 %collective-permute-start.11 = (bf16[64,512]{1,0:T(8,128)(2,1)S(1)}, bf16[64,512]{1,0:T(8,128)(2,1)S(1)}, u32[]{:S(2)}, u32[]{:S(2)}) collective-permute-start(bf16[64,512]{1,0:T(8,128)(2,1)S(1)} %get-tuple-element.100.refs_2_), channel_id=1, source_target_pairs={{0,2},{1,3},{2,0},{3,1},{4,6},{5,7},{6,4},{7,5},{8,10},{9,11},{10,... | collective-permute-start | bytes 196616 | tf_op jit(solution)/shard_map/ppermute | solution.py:29
  25.5 5.2 %collective-permute-start.13 = (bf16[64,512]{1,0:T(8,128)(2,1)S(1)}, bf16[64,512]{1,0:T(8,128)(2,1)S(1)}, u32[]{:S(2)}, u32[]{:S(2)}) collective-permute-start(bf16[64,512]{1,0:T(8,128)(2,1)S(1)} %get-tuple-element.100.refs_2_), channel_id=1, source_target_pairs={{0,6},{1,7},{2,4},{3,5},{4,2},{5,3},{6,0},{7,1},{8,14},{9,15},{10,... | collective-permute-start | bytes 196616 | tf_op jit(solution)/shard_map/ppermute | solution.py:29
  31.7 4.3 %collective-permute-start.15 = (bf16[64,512]{1,0:T(8,128)(2,1)S(1)}, bf16[64,512]{1,0:T(8,128)(2,1)S(1)}, u32[]{:S(2)}, u32[]{:S(2)}) collective-permute-start(bf16[64,512]{1,0:T(8,128)(2,1)S(1)} %get-tuple-element.71), channel_id=1, source_target_pairs={{0,2},{1,3},{2,0},{3,1},{4,6},{5,7},{6,4},{7,5},{8,10},{9,11},{10,... | collective-permute-start | bytes 196616 | tf_op jit(solution)/shard_map/ppermute | solution.py:29
  35.2 5.2 %collective-permute-start.17 = (bf16[64,512]{1,0:T(8,128)(2,1)S(1)}, bf16[64,512]{1,0:T(8,128)(2,1)S(1)}, u32[]{:S(2)}, u32[]{:S(2)}) collective-permute-start(bf16[64,512]{1,0:T(8,128)(2,1)S(1)} %get-tuple-element.73), channel_id=1, source_target_pairs={{0,6},{1,7},{2,4},{3,5},{4,2},{5,3},{6,0},{7,1},{8,14},{9,15},{10,... | collective-permute-start | bytes 196616 | tf_op jit(solution)/shard_map/ppermute | solution.py:29
  40.4 5.7 %collective-permute-start.18 = (bf16[64,512]{1,0:T(8,128)(2,1)S(1)}, bf16[64,512]{1,0:T(8,128)(2,1)S(1)}, u32[]{:S(2)}, u32[]{:S(2)}) collective-permute-start(bf16[64,512]{1,0:T(8,128)(2,1)S(1)} %fusion), channel_id=1, source_target_pairs={{0,8},{1,9},{2,10},{3,11},{4,12},{5,13},{6,14},{7,15},{8,0},{9,1},... | collective-permute-start | bytes 196616 | tf_op jit(solution)/shard_map/ppermute | solution.py:29
  47.2 5.6 %collective-permute-start.21 = (bf16[64,512]{1,0:T(8,128)(2,1)S(1)}, bf16[64,512]{1,0:T(8,128)(2,1)S(1)}, u32[]{:S(2)}, u32[]{:S(2)}) collective-permute-start(bf16[64,512]{1,0:T(8,128)(2,1)S(1)} %get-tuple-element.98.refs_2_), channel_id=1, source_target_pairs={{0,6},{1,7},{2,4},{3,5},{4,2},{5,3},{6,0},{7,1},{8,14},{9,15},{10,... | collective-permute-start | bytes 196616 | tf_op jit(solution)/shard_map/ppermute | solution.py:29
  55.5 4.4 %collective-permute-start.23 = (bf16[64,512]{1,0:T(8,128)(2,1)S(1)}, bf16[64,512]{1,0:T(8,128)(2,1)S(1)}, u32[]{:S(2)}, u32[]{:S(2)}) collective-permute-start(bf16[64,512]{1,0:T(8,128)(2,1)S(1)} %get-tuple-element.81), channel_id=1, source_target_pairs={{0,4},{1,5},{2,6},{3,7},{4,0},{5,1},{6,2},{7,3},{8,12},{9,13},{10,... | collective-permute-start | bytes 196616 | tf_op jit(solution)/shard_map/ppermute | solution.py:29
  57.2 5.5 %collective-permute-start.24 = (bf16[64,512]{1,0:T(8,128)(2,1)S(1)}, bf16[64,512]{1,0:T(8,128)(2,1)S(1)}, u32[]{:S(2)}, u32[]{:S(2)}) collective-permute-start(bf16[64,512]{1,0:T(8,128)(2,1)S(1)} %get-tuple-element.82), channel_id=1, source_target_pairs={{0,6},{1,7},{2,4},{3,5},{4,2},{5,3},{6,0},{7,1},{8,14},{9,15},{10,... | collective-permute-start | bytes 196616 | tf_op jit(solution)/shard_map/ppermute | solution.py:29
  62.7 5.3 %collective-permute-start.25 = (bf16[64,512]{1,0:T(8,128)(2,1)S(1)}, bf16[64,512]{1,0:T(8,128)(2,1)S(1)}, u32[]{:S(2)}, u32[]{:S(2)}) collective-permute-start(bf16[64,512]{1,0:T(8,128)(2,1)S(1)} %fusion.1), channel_id=1, source_target_pairs={{0,8},{1,9},{2,10},{3,11},{4,12},{5,13},{6,14},{7,15},{8,0},{9,1},... | collective-permute-start | bytes 196616 | tf_op jit(solution)/shard_map/ppermute | solution.py:29
  68.1 4.8 %collective-permute-start.27 = (bf16[64,512]{1,0:T(8,128)(2,1)S(1)}, bf16[64,512]{1,0:T(8,128)(2,1)S(1)}, u32[]{:S(2)}, u32[]{:S(2)}) collective-permute-start(bf16[64,512]{1,0:T(8,128)(2,1)S(1)} %get-tuple-element.87.refs_2_), channel_id=1, source_target_pairs={{0,4},{1,5},{2,6},{3,7},{4,0},{5,1},{6,2},{7,3},{8,12},{9,13},{10,... | collective-permute-start | bytes 196616 | tf_op jit(solution)/shard_map/ppermute | solution.py:29
  68.2 4.8 %collective-permute-start.26 = (bf16[64,512]{1,0:T(8,128)(2,1)S(1)}, bf16[64,512]{1,0:T(8,128)(2,1)S(1)}, u32[]{:S(2)}, u32[]{:S(2)}) collective-permute-start(bf16[64,512]{1,0:T(8,128)(2,1)S(1)} %get-tuple-element.87.refs_2_), channel_id=1, source_target_pairs={{0,2},{1,3},{2,0},{3,1},{4,6},{5,7},{6,4},{7,5},{8,10},{9,11},{10,... | collective-permute-start | bytes 196616 | tf_op jit(solution)/shard_map/ppermute | solution.py:29
  69.3 5.2 %collective-permute-start.29 = (bf16[64,512]{1,0:T(8,128)(2,1)S(1)}, bf16[64,512]{1,0:T(8,128)(2,1)S(1)}, u32[]{:S(2)}, u32[]{:S(2)}) collective-permute-start(bf16[64,512]{1,0:T(8,128)(2,1)S(1)} %get-tuple-element.87.refs_2_), channel_id=1, source_target_pairs={{0,6},{1,7},{2,4},{3,5},{4,2},{5,3},{6,0},{7,1},{8,14},{9,15},{10,... | collective-permute-start | bytes 196616 | tf_op jit(solution)/shard_map/ppermute | solution.py:29
  (12 other events, 44.8 us)

commit v5 on v4

--- a/solution.py
+++ b/solution.py
@@ -9,6 +9,7 @@
 
 ITERS = 3
 STEP = 0.4
+SUM_LAST, VALUE_LAST = 2, 1
 CORES = 2
 QUAD = 4
 UNIT = CORES * QUAD
@@ -180,7 +181,7 @@
     a, pieces, images = refs[0:2], refs[2 : 1 + QUAD], refs[1 + QUAD :]
     me = place()[1]
     for i in range(2):
-        images[i][...] = row_product(a[i], pieces, range(QUAD - 1), me)
+        images[i][...] = row_product(a[i], pieces, [k for k in range(QUAD) if k != VALUE_LAST], me)
 
 
 def turn_kernel(first, *refs):
@@ -191,7 +192,7 @@
     me = place()[1]
     low = []
     for i in range(2):
-        image = images[i][...] + row_product(a[i], (last,), (QUAD - 1,), me)
+        image = images[i][...] + row_product(a[i], (last,), (VALUE_LAST,), me)
         new = jnp.maximum(duals[i][...] + STEP * (sides[i][1] - image), 0.0)
         stepped[i][...] = new
         low.append(new.astype(BF16).T)
@@ -209,7 +210,7 @@
 
 
 def finish_kernel(a, image, last, side, dual, out):
-    total = image[...] + row_product(a, (last,), (QUAD - 1,), place()[1])
+    total = image[...] + row_product(a, (last,), (VALUE_LAST,), place()[1])
     out[...] = jnp.maximum(dual[...] + STEP * (side[1] - total), 0.0)
 
 
@@ -262,7 +263,12 @@
         fars = fars + [swap(f, mask) for f in fars]
     sums = [k + swap(s, 1) for k, s in zip(keeps, sends)]
     pieces = [s.astype(BF16) for s in sums[1:]]
-    got = [swap(p, k * CORES) for k, p in enumerate(pieces, 1)]
+    def send(pieces, last):
+        order = [k for k in range(1, QUAD) if k != last] + [last]
+        moved = {k: swap(pieces[k], k * CORES) for k in order}
+        return [moved[k] for k in range(1, QUAD) if k != last] + [moved[last]]
+
+    got = send([None, *pieces], SUM_LAST)
 
     primal, cost, limit = call(
         variables_kernel,
@@ -286,7 +292,7 @@
             for g in got[:-1]:
                 total = total + g.astype(F32)
         else:
-            got = [swap(p, k * CORES) for k, p in enumerate(pieces, 1)]
+            got = send([None, *pieces], SUM_LAST)
             total = call(own_columns_kernel, state, *a, *lows, *got[:-1]) - cost
         total = total + got[-1].astype(F32)
         for mask in far_masks:
@@ -294,7 +300,7 @@
         updated = jnp.clip(primal + STEP * total, 0.0, limit)
         ahead = (2.0 * updated - primal).astype(BF16)
         primal = updated
-        around = [ahead] + [swap(ahead, k * CORES) for k in range(1, QUAD)]
+        around = [ahead] + send([ahead] * QUAD, VALUE_LAST)
         if iteration == ITERS - 1:
             part = jax.ShapeDtypeStruct((half, width), F32)
             mine, other = call(give_kernel, (part, part), primal)

time: 77.2 us -> 75.2 us (0.974)
  waiting for transfers between devices: 36.7 us -> 32.6 us
  starting transfers between devices: 27.8 us -> 30.1 us
    ppermute x31, waiting for transfers between devices: 36.7 us -> 32.6 us  [swap(): lax.ppermute(x, 'row', [(i, i ^ mask) for i in range(lax.axis_size('row'))])]
    ppermute x31, starting transfers between devices: 27.8 us -> 30.1 us  [swap(): lax.ppermute(x, 'row', [(i, i ^ mask) for i in range(lax.axis_size('row'))])]
  transfers between devices with their start and end apart: 31 -> 31, of which waited for: 21 -> 22; matrix products, arithmetic and copies ran while one was open for 0% -> 0% of each run, Pallas kernels for 6% -> 6%
where the time goes in v5:
time: 75.2 us; the launch traced here: 75 us
  waiting for transfers between devices  32.6 us (43%)
  starting transfers between devices  30.1 us (40%)
  Pallas kernels  10.4 us (14%)
  other arithmetic  1.02 us (1%)
  between operations  0.89 us (1%)
    ppermute x31, waiting for transfers between devices, swap(): lax.ppermute(x, 'row', [(i, i ^ mask) for i in range(lax.axis_size('row'))])  32.6 us
    ppermute x31, starting transfers between devices, swap(): lax.ppermute(x, 'row', [(i, i ^ mask) for i in range(lax.axis_size('row'))])  30.1 us
    pallas_call x15, Pallas kernels, call(): pl.pallas_call(kernel, out_shape=out_shape, in_specs=[VMEM] * len(operand...  8.36 us
    pallas_call x1, Pallas kernels, dense(): pl.pallas_call(functools.partial(dense_kernel, span, chunks), out_shape=j...  2.06 us
  transfers between devices with their start and end apart: 31, of which 22 were waited for; matrix products, arithmetic and copies ran while one was open for 0% of the time, Pallas kernels for 6%

profile of v5, /device:TPU:0, one launch (start us, length us, event | category | flops | bytes accessed | tf_op | source)
XLA Modules:
  0.0 75.0 jit_solution(299552486253379896)
XLA Ops:
  1.3 2.1 %shard_map.95.a_ref.refs_0_.a = bf16[2,4,256,512]{3,2,1,0:T(8,128)(2,1)S(1)} custom-call(s32[64]{0:T(128)S(1)} %multiply_add_fusion.at_hbm, bf16[64,128,128]{2,1,0:T(8,128)(2,1)} %tile_hbm.1), custom_call_target="tpu_custom_call" | custom-call | tf_op jit(solution)/shard_map/pallas_call | solution.py:79
  5.5 3.9 %collective-permute-start.1 = (f32[144,128]{1,0:T(8,128)S(1)}, f32[144,128]{1,0:T(8,128)S(1)}, u32[]{:S(2)}, u32[]{:S(2)}) collective-permute-start(f32[144,128]{1,0:T(8,128)S(1)} %pad_maximum_fusion), channel_id=1, source_target_pairs={{0,8},{1,9},{2,10},{3,11},{4,12},{5,13},{6,14},{7,15},{8,0},{9,1},... | collective-permute-start | bytes 221192 | tf_op jit(solution)/shard_map/ppermute | solution.py:30
  9.4 1.6 %collective-permute-start.4 = (bf16[64,512]{1,0:T(8,128)(2,1)S(1)}, bf16[64,512]{1,0:T(8,128)(2,1)S(1)}, u32[]{:S(2)}, u32[]{:S(2)}) collective-permute-start(bf16[64,512]{1,0:T(8,128)(2,1)S(1)} %add_convert_fusion.2), channel_id=1, source_target_pairs={{0,2},{1,3},{2,0},{3,1},{4,6},{5,7},{6,4},{7,5},{8,10},{9,11},{10,... | collective-permute-start | bytes 196616 | tf_op jit(solution)/shard_map/ppermute | solution.py:30
  11.0 1.6 %collective-permute-start.6 = (bf16[64,512]{1,0:T(8,128)(2,1)S(1)}, bf16[64,512]{1,0:T(8,128)(2,1)S(1)}, u32[]{:S(2)}, u32[]{:S(2)}) collective-permute-start(bf16[64,512]{1,0:T(8,128)(2,1)S(1)} %add_convert_fusion.1), channel_id=1, source_target_pairs={{0,6},{1,7},{2,4},{3,5},{4,2},{5,3},{6,0},{7,1},{8,14},{9,15},{10,... | collective-permute-start | bytes 196616 | tf_op jit(solution)/shard_map/ppermute | solution.py:30
  13.8 3.0 %collective-permute-done.6 = bf16[64,512]{1,0:T(8,128)(2,1)S(1)} collective-permute-done((bf16[64,512]{1,0:T(8,128)(2,1)S(1)}, bf16[64,512]{1,0:T(8,128)(2,1)S(1)}, u32[]{:S(2)}, u32[]{:S(2)}) %collective-permute-start.6) | collective-permute-done | bytes 65568 | tf_op jit(solution)/shard_map/ppermute | solution.py:30
  18.1 5.8 %collective-permute-done.9 = bf16[64,512]{1,0:T(8,128)(2,1)S(1)} collective-permute-done((bf16[64,512]{1,0:T(8,128)(2,1)S(1)}, bf16[64,512]{1,0:T(8,128)(2,1)S(1)}, u32[]{:S(2)}, u32[]{:S(2)}) %collective-permute-start.9) | collective-permute-done | bytes 65568 | tf_op jit(solution)/shard_map/ppermute | solution.py:30
  24.4 2.6 %collective-permute-start.11 = (bf16[64,512]{1,0:T(8,128)(2,1)S(1)}, bf16[64,512]{1,0:T(8,128)(2,1)S(1)}, u32[]{:S(2)}, u32[]{:S(2)}) collective-permute-start(bf16[64,512]{1,0:T(8,128)(2,1)S(1)} %get-tuple-element.100.refs_2_), channel_id=1, source_target_pairs={{0,4},{1,5},{2,6},{3,7},{4,0},{5,1},{6,2},{7,3},{8,12},{9,13},{10,... | collective-permute-start | bytes 196616 | tf_op jit(solution)/shard_map/ppermute | solution.py:30
  27.5 1.8 %collective-permute-done.12.refs_4_ = bf16[64,512]{1,0:T(8,128)(2,1)S(1)} collective-permute-done((bf16[64,512]{1,0:T(8,128)(2,1)S(1)}, bf16[64,512]{1,0:T(8,128)(2,1)S(1)}, u32[]{:S(2)}, u32[]{:S(2)}) %collective-permute-start.12) | collective-permute-done | bytes 65568 | tf_op jit(solution)/shard_map/ppermute | solution.py:30
  33.0 1.8 %collective-permute-start.16 = (bf16[64,512]{1,0:T(8,128)(2,1)S(1)}, bf16[64,512]{1,0:T(8,128)(2,1)S(1)}, u32[]{:S(2)}, u32[]{:S(2)}) collective-permute-start(bf16[64,512]{1,0:T(8,128)(2,1)S(1)} %get-tuple-element.72), channel_id=1, source_target_pairs={{0,6},{1,7},{2,4},{3,5},{4,2},{5,3},{6,0},{7,1},{8,14},{9,15},{10,... | collective-permute-start | bytes 196616 | tf_op jit(solution)/shard_map/ppermute | solution.py:30
  34.8 1.0 %collective-permute-start.17 = (bf16[64,512]{1,0:T(8,128)(2,1)S(1)}, bf16[64,512]{1,0:T(8,128)(2,1)S(1)}, u32[]{:S(2)}, u32[]{:S(2)}) collective-permute-start(bf16[64,512]{1,0:T(8,128)(2,1)S(1)} %get-tuple-element.73), channel_id=1, source_target_pairs={{0,4},{1,5},{2,6},{3,7},{4,0},{5,1},{6,2},{7,3},{8,12},{9,13},{10,... | collective-permute-start | bytes 196616 | tf_op jit(solution)/shard_map/ppermute | solution.py:30
  36.6 1.6 %collective-permute-done.16.refs_5_ = bf16[64,512]{1,0:T(8,128)(2,1)S(1)} collective-permute-done((bf16[64,512]{1,0:T(8,128)(2,1)S(1)}, bf16[64,512]{1,0:T(8,128)(2,1)S(1)}, u32[]{:S(2)}, u32[]{:S(2)}) %collective-permute-start.16) | collective-permute-done | bytes 65568 | tf_op jit(solution)/shard_map/ppermute | solution.py:30
  40.1 4.5 %collective-permute-done.18 = bf16[64,512]{1,0:T(8,128)(2,1)S(1)} collective-permute-done((bf16[64,512]{1,0:T(8,128)(2,1)S(1)}, bf16[64,512]{1,0:T(8,128)(2,1)S(1)}, u32[]{:S(2)}, u32[]{:S(2)}) %collective-permute-start.18) | collective-permute-done | bytes 65568 | tf_op jit(solution)/shard_map/ppermute | solution.py:30
  44.6 1.4 %collective-permute-start.20 = (bf16[64,512]{1,0:T(8,128)(2,1)S(1)}, bf16[64,512]{1,0:T(8,128)(2,1)S(1)}, u32[]{:S(2)}, u32[]{:S(2)}) collective-permute-start(bf16[64,512]{1,0:T(8,128)(2,1)S(1)} %get-tuple-element.98.refs_2_), channel_id=1, source_target_pairs={{0,6},{1,7},{2,4},{3,5},{4,2},{5,3},{6,0},{7,1},{8,14},{9,15},{10,... | collective-permute-start | bytes 196616 | tf_op jit(solution)/shard_map/ppermute | solution.py:30
  46.0 1.4 %collective-permute-start.19 = (bf16[64,512]{1,0:T(8,128)(2,1)S(1)}, bf16[64,512]{1,0:T(8,128)(2,1)S(1)}, u32[]{:S(2)}, u32[]{:S(2)}) collective-permute-start(bf16[64,512]{1,0:T(8,128)(2,1)S(1)} %get-tuple-element.98.refs_2_), channel_id=1, source_target_pairs={{0,4},{1,5},{2,6},{3,7},{4,0},{5,1},{6,2},{7,3},{8,12},{9,13},{10,... | collective-permute-start | bytes 196616 | tf_op jit(solution)/shard_map/ppermute | solution.py:30
  48.2 1.7 %collective-permute-done.20.refs_4_ = bf16[64,512]{1,0:T(8,128)(2,1)S(1)} collective-permute-done((bf16[64,512]{1,0:T(8,128)(2,1)S(1)}, bf16[64,512]{1,0:T(8,128)(2,1)S(1)}, u32[]{:S(2)}, u32[]{:S(2)}) %collective-permute-start.20) | collective-permute-done | bytes 65568 | tf_op jit(solution)/shard_map/ppermute | solution.py:30
  52.8 1.3 %collective-permute-start.22 = (bf16[64,512]{1,0:T(8,128)(2,1)S(1)}, bf16[64,512]{1,0:T(8,128)(2,1)S(1)}, u32[]{:S(2)}, u32[]{:S(2)}) collective-permute-start(bf16[64,512]{1,0:T(8,128)(2,1)S(1)} %get-tuple-element.80), channel_id=1, source_target_pairs={{0,2},{1,3},{2,0},{3,1},{4,6},{5,7},{6,4},{7,5},{8,10},{9,11},{10,... | collective-permute-start | bytes 196616 | tf_op jit(solution)/shard_map/ppermute | solution.py:30
  54.0 1.2 %collective-permute-start.23 = (bf16[64,512]{1,0:T(8,128)(2,1)S(1)}, bf16[64,512]{1,0:T(8,128)(2,1)S(1)}, u32[]{:S(2)}, u32[]{:S(2)}) collective-permute-start(bf16[64,512]{1,0:T(8,128)(2,1)S(1)} %get-tuple-element.81), channel_id=1, source_target_pairs={{0,6},{1,7},{2,4},{3,5},{4,2},{5,3},{6,0},{7,1},{8,14},{9,15},{10,... | collective-permute-start | bytes 196616 | tf_op jit(solution)/shard_map/ppermute | solution.py:30
  55.2 1.1 %collective-permute-start.24 = (bf16[64,512]{1,0:T(8,128)(2,1)S(1)}, bf16[64,512]{1,0:T(8,128)(2,1)S(1)}, u32[]{:S(2)}, u32[]{:S(2)}) collective-permute-start(bf16[64,512]{1,0:T(8,128)(2,1)S(1)} %get-tuple-element.82), channel_id=1, source_target_pairs={{0,4},{1,5},{2,6},{3,7},{4,0},{5,1},{6,2},{7,3},{8,12},{9,13},{10,... | collective-permute-start | bytes 196616 | tf_op jit(solution)/shard_map/ppermute | solution.py:30
  57.1 2.1 %collective-permute-done.23.refs_5_ = bf16[64,512]{1,0:T(8,128)(2,1)S(1)} collective-permute-done((bf16[64,512]{1,0:T(8,128)(2,1)S(1)}, bf16[64,512]{1,0:T(8,128)(2,1)S(1)}, u32[]{:S(2)}, u32[]{:S(2)}) %collective-permute-start.23) | collective-permute-done | bytes 65568 | tf_op jit(solution)/shard_map/ppermute | solution.py:30
  59.6 1.2 %collective-permute-start.25 = (bf16[64,512]{1,0:T(8,128)(2,1)S(1)}, bf16[64,512]{1,0:T(8,128)(2,1)S(1)}, u32[]{:S(2)}, u32[]{:S(2)}) collective-permute-start(bf16[64,512]{1,0:T(8,128)(2,1)S(1)} %fusion.1), channel_id=1, source_target_pairs={{0,8},{1,9},{2,10},{3,11},{4,12},{5,13},{6,14},{7,15},{8,0},{9,1},... | collective-permute-start | bytes 196616 | tf_op jit(solution)/shard_map/ppermute | solution.py:30
  60.8 4.7 %collective-permute-done.25 = bf16[64,512]{1,0:T(8,128)(2,1)S(1)} collective-permute-done((bf16[64,512]{1,0:T(8,128)(2,1)S(1)}, bf16[64,512]{1,0:T(8,128)(2,1)S(1)}, u32[]{:S(2)}, u32[]{:S(2)}) %collective-permute-start.25) | collective-permute-done | bytes 65568 | tf_op jit(solution)/shard_map/ppermute | solution.py:30
  65.6 1.2 %collective-permute-start.27 = (bf16[64,512]{1,0:T(8,128)(2,1)S(1)}, bf16[64,512]{1,0:T(8,128)(2,1)S(1)}, u32[]{:S(2)}, u32[]{:S(2)}) collective-permute-start(bf16[64,512]{1,0:T(8,128)(2,1)S(1)} %get-tuple-element.87.refs_2_), channel_id=1, source_target_pairs={{0,6},{1,7},{2,4},{3,5},{4,2},{5,3},{6,0},{7,1},{8,14},{9,15},{10,... | collective-permute-start | bytes 196616 | tf_op jit(solution)/shard_map/ppermute | solution.py:30
  66.7 1.5 %collective-permute-start.26 = (bf16[64,512]{1,0:T(8,128)(2,1)S(1)}, bf16[64,512]{1,0:T(8,128)(2,1)S(1)}, u32[]{:S(2)}, u32[]{:S(2)}) collective-permute-start(bf16[64,512]{1,0:T(8,128)(2,1)S(1)} %get-tuple-element.87.refs_2_), channel_id=1, source_target_pairs={{0,4},{1,5},{2,6},{3,7},{4,0},{5,1},{6,2},{7,3},{8,12},{9,13},{10,... | collective-permute-start | bytes 196616 | tf_op jit(solution)/shard_map/ppermute | solution.py:30
  69.2 1.2 %collective-permute-done.28.other = f32[64,128]{1,0:T(8,128)S(1)} collective-permute-done((f32[64,128]{1,0:T(8,128)S(1)}, f32[64,128]{1,0:T(8,128)S(1)}, u32[]{:S(2)}, u32[]{:S(2)}) %collective-permute-start.28) | collective-permute-done | bytes 32800 | tf_op jit(solution)/shard_map/ppermute | solution.py:30
  (77 shorter events, 23.0 us)
Async XLA Ops:
  4.4 4.9 %collective-permute-start.3 = (f32[64,512]{1,0:T(8,128)S(1)}, f32[64,512]{1,0:T(8,128)S(1)}, u32[]{:S(2)}, u32[]{:S(2)}) collective-permute-start(f32[64,512]{1,0:T(8,128)S(1)} %get-tuple-element.57), channel_id=1, source_target_pairs={{0,1},{1,0},{2,3},{3,2},{4,5},{5,4},{6,7},{7,6},{8,9},{9,8},{10,11... | collective-permute-start | bytes 393224 | tf_op jit(solution)/shard_map/ppermute | solution.py:30
  4.5 9.2 %collective-permute-start.2 = (f32[64,512]{1,0:T(8,128)S(1)}, f32[64,512]{1,0:T(8,128)S(1)}, u32[]{:S(2)}, u32[]{:S(2)}) collective-permute-start(f32[64,512]{1,0:T(8,128)S(1)} %get-tuple-element.54), channel_id=1, source_target_pairs={{0,1},{1,0},{2,3},{3,2},{4,5},{5,4},{6,7},{7,6},{8,9},{9,8},{10,11... | collective-permute-start | bytes 393224 | tf_op jit(solution)/shard_map/ppermute | solution.py:30
  4.9 6.0 %collective-permute-start.5 = (f32[64,512]{1,0:T(8,128)S(1)}, f32[64,512]{1,0:T(8,128)S(1)}, u32[]{:S(2)}, u32[]{:S(2)}) collective-permute-start(f32[64,512]{1,0:T(8,128)S(1)} %get-tuple-element.59), channel_id=1, source_target_pairs={{0,1},{1,0},{2,3},{3,2},{4,5},{5,4},{6,7},{7,6},{8,9},{9,8},{10,11... | collective-permute-start | bytes 393224 | tf_op jit(solution)/shard_map/ppermute | solution.py:30
  5.0 7.6 %collective-permute-start.7 = (f32[64,512]{1,0:T(8,128)S(1)}, f32[64,512]{1,0:T(8,128)S(1)}, u32[]{:S(2)}, u32[]{:S(2)}) collective-permute-start(f32[64,512]{1,0:T(8,128)S(1)} %get-tuple-element.61), channel_id=1, source_target_pairs={{0,1},{1,0},{2,3},{3,2},{4,5},{5,4},{6,7},{7,6},{8,9},{9,8},{10,11... | collective-permute-start | bytes 393224 | tf_op jit(solution)/shard_map/ppermute | solution.py:30
  5.5 8.2 %collective-permute-start.1 = (f32[144,128]{1,0:T(8,128)S(1)}, f32[144,128]{1,0:T(8,128)S(1)}, u32[]{:S(2)}, u32[]{:S(2)}) collective-permute-start(f32[144,128]{1,0:T(8,128)S(1)} %pad_maximum_fusion), channel_id=1, source_target_pairs={{0,8},{1,9},{2,10},{3,11},{4,12},{5,13},{6,14},{7,15},{8,0},{9,1},... | collective-permute-start | bytes 221192 | tf_op jit(solution)/shard_map/ppermute | solution.py:30
  9.4 4.4 %collective-permute-start.4 = (bf16[64,512]{1,0:T(8,128)(2,1)S(1)}, bf16[64,512]{1,0:T(8,128)(2,1)S(1)}, u32[]{:S(2)}, u32[]{:S(2)}) collective-permute-start(bf16[64,512]{1,0:T(8,128)(2,1)S(1)} %add_convert_fusion.2), channel_id=1, source_target_pairs={{0,2},{1,3},{2,0},{3,1},{4,6},{5,7},{6,4},{7,5},{8,10},{9,11},{10,... | collective-permute-start | bytes 196616 | tf_op jit(solution)/shard_map/ppermute | solution.py:30
  11.0 5.8 %collective-permute-start.6 = (bf16[64,512]{1,0:T(8,128)(2,1)S(1)}, bf16[64,512]{1,0:T(8,128)(2,1)S(1)}, u32[]{:S(2)}, u32[]{:S(2)}) collective-permute-start(bf16[64,512]{1,0:T(8,128)(2,1)S(1)} %add_convert_fusion.1), channel_id=1, source_target_pairs={{0,6},{1,7},{2,4},{3,5},{4,2},{5,3},{6,0},{7,1},{8,14},{9,15},{10,... | collective-permute-start | bytes 196616 | tf_op jit(solution)/shard_map/ppermute | solution.py:30
  12.6 4.3 %collective-permute-start.8 = (bf16[64,512]{1,0:T(8,128)(2,1)S(1)}, bf16[64,512]{1,0:T(8,128)(2,1)S(1)}, u32[]{:S(2)}, u32[]{:S(2)}) collective-permute-start(bf16[64,512]{1,0:T(8,128)(2,1)S(1)} %add_convert_fusion), channel_id=1, source_target_pairs={{0,4},{1,5},{2,6},{3,7},{4,0},{5,1},{6,2},{7,3},{8,12},{9,13},{10,... | collective-permute-start | bytes 196616 | tf_op jit(solution)/shard_map/ppermute | solution.py:30
  17.0 13.2 %collective-permute-start.10 = (bf16[2,4,256,512]{3,2,1,0:T(8,128)(2,1)S(1)}, bf16[2,4,256,512]{3,2,1,0:T(8,128)(2,1)S(1)}, u32[]{:S(2)}, u32[]{:S(2)}) collective-permute-start(bf16[2,4,256,512]{3,2,1,0:T(8,128)(2,1)S(1)} %shard_map.95.a_ref.refs_0_.a), channel_id=1, source_target_pairs={{0,1},{1,0},{2,3},{3,2},{4,5},{5,4},{6,7},{7,6},{8,9},{9,8},{10,11... | collective-permute-start | bytes 6291464 | tf_op jit(solution)/shard_map/ppermute | solution.py:30
  17.1 6.8 %collective-permute-start.9 = (bf16[64,512]{1,0:T(8,128)(2,1)S(1)}, bf16[64,512]{1,0:T(8,128)(2,1)S(1)}, u32[]{:S(2)}, u32[]{:S(2)}) collective-permute-start(bf16[64,512]{1,0:T(8,128)(2,1)S(1)} %get-tuple-element.102), channel_id=1, source_target_pairs={{0,8},{1,9},{2,10},{3,11},{4,12},{5,13},{6,14},{7,15},{8,0},{9,1},... | collective-permute-start | bytes 196616 | tf_op jit(solution)/shard_map/ppermute | solution.py:30
  17.9 13.4 %collective-permute-start.14 = (f32[2,256,64]{2,1,0:T(8,128)S(1)}, f32[2,256,64]{2,1,0:T(8,128)S(1)}, u32[]{:S(2)}, u32[]{:S(2)}) collective-permute-start(f32[2,256,64]{2,1,0:T(8,128)S(1)} %get-tuple-element.68), channel_id=1, source_target_pairs={{0,1},{1,0},{2,3},{3,2},{4,5},{5,4},{6,7},{7,6},{8,9},{9,8},{10,11... | collective-permute-start | bytes 393224 | tf_op jit(solution)/shard_map/ppermute | solution.py:30
  23.9 5.4 %collective-permute-start.12 = (bf16[64,512]{1,0:T(8,128)(2,1)S(1)}, bf16[64,512]{1,0:T(8,128)(2,1)S(1)}, u32[]{:S(2)}, u32[]{:S(2)}) collective-permute-start(bf16[64,512]{1,0:T(8,128)(2,1)S(1)} %get-tuple-element.100.refs_2_), channel_id=1, source_target_pairs={{0,6},{1,7},{2,4},{3,5},{4,2},{5,3},{6,0},{7,1},{8,14},{9,15},{10,... | collective-permute-start | bytes 196616 | tf_op jit(solution)/shard_map/ppermute | solution.py:30
  24.4 5.7 %collective-permute-start.11 = (bf16[64,512]{1,0:T(8,128)(2,1)S(1)}, bf16[64,512]{1,0:T(8,128)(2,1)S(1)}, u32[]{:S(2)}, u32[]{:S(2)}) collective-permute-start(bf16[64,512]{1,0:T(8,128)(2,1)S(1)} %get-tuple-element.100.refs_2_), channel_id=1, source_target_pairs={{0,4},{1,5},{2,6},{3,7},{4,0},{5,1},{6,2},{7,3},{8,12},{9,13},{10,... | collective-permute-start | bytes 196616 | tf_op jit(solution)/shard_map/ppermute | solution.py:30
  32.3 4.3 %collective-permute-start.15 = (bf16[64,512]{1,0:T(8,128)(2,1)S(1)}, bf16[64,512]{1,0:T(8,128)(2,1)S(1)}, u32[]{:S(2)}, u32[]{:S(2)}) collective-permute-start(bf16[64,512]{1,0:T(8,128)(2,1)S(1)} %get-tuple-element.71), channel_id=1, source_target_pairs={{0,2},{1,3},{2,0},{3,1},{4,6},{5,7},{6,4},{7,5},{8,10},{9,11},{10,... | collective-permute-start | bytes 196616 | tf_op jit(solution)/shard_map/ppermute | solution.py:30
  33.0 5.2 %collective-permute-start.16 = (bf16[64,512]{1,0:T(8,128)(2,1)S(1)}, bf16[64,512]{1,0:T(8,128)(2,1)S(1)}, u32[]{:S(2)}, u32[]{:S(2)}) collective-permute-start(bf16[64,512]{1,0:T(8,128)(2,1)S(1)} %get-tuple-element.72), channel_id=1, source_target_pairs={{0,6},{1,7},{2,4},{3,5},{4,2},{5,3},{6,0},{7,1},{8,14},{9,15},{10,... | collective-permute-start | bytes 196616 | tf_op jit(solution)/shard_map/ppermute | solution.py:30
  39.1 5.4 %collective-permute-start.18 = (bf16[64,512]{1,0:T(8,128)(2,1)S(1)}, bf16[64,512]{1,0:T(8,128)(2,1)S(1)}, u32[]{:S(2)}, u32[]{:S(2)}) collective-permute-start(bf16[64,512]{1,0:T(8,128)(2,1)S(1)} %fusion), channel_id=1, source_target_pairs={{0,8},{1,9},{2,10},{3,11},{4,12},{5,13},{6,14},{7,15},{8,0},{9,1},... | collective-permute-start | bytes 196616 | tf_op jit(solution)/shard_map/ppermute | solution.py:30
  44.6 5.2 %collective-permute-start.20 = (bf16[64,512]{1,0:T(8,128)(2,1)S(1)}, bf16[64,512]{1,0:T(8,128)(2,1)S(1)}, u32[]{:S(2)}, u32[]{:S(2)}) collective-permute-start(bf16[64,512]{1,0:T(8,128)(2,1)S(1)} %get-tuple-element.98.refs_2_), channel_id=1, source_target_pairs={{0,6},{1,7},{2,4},{3,5},{4,2},{5,3},{6,0},{7,1},{8,14},{9,15},{10,... | collective-permute-start | bytes 196616 | tf_op jit(solution)/shard_map/ppermute | solution.py:30
  46.0 4.4 %collective-permute-start.19 = (bf16[64,512]{1,0:T(8,128)(2,1)S(1)}, bf16[64,512]{1,0:T(8,128)(2,1)S(1)}, u32[]{:S(2)}, u32[]{:S(2)}) collective-permute-start(bf16[64,512]{1,0:T(8,128)(2,1)S(1)} %get-tuple-element.98.refs_2_), channel_id=1, source_target_pairs={{0,4},{1,5},{2,6},{3,7},{4,0},{5,1},{6,2},{7,3},{8,12},{9,13},{10,... | collective-permute-start | bytes 196616 | tf_op jit(solution)/shard_map/ppermute | solution.py:30
  47.4 4.3 %collective-permute-start.21 = (bf16[64,512]{1,0:T(8,128)(2,1)S(1)}, bf16[64,512]{1,0:T(8,128)(2,1)S(1)}, u32[]{:S(2)}, u32[]{:S(2)}) collective-permute-start(bf16[64,512]{1,0:T(8,128)(2,1)S(1)} %get-tuple-element.98.refs_2_), channel_id=1, source_target_pairs={{0,2},{1,3},{2,0},{3,1},{4,6},{5,7},{6,4},{7,5},{8,10},{9,11},{10,... | collective-permute-start | bytes 196616 | tf_op jit(solution)/shard_map/ppermute | solution.py:30
  52.8 4.3 %collective-permute-start.22 = (bf16[64,512]{1,0:T(8,128)(2,1)S(1)}, bf16[64,512]{1,0:T(8,128)(2,1)S(1)}, u32[]{:S(2)}, u32[]{:S(2)}) collective-permute-start(bf16[64,512]{1,0:T(8,128)(2,1)S(1)} %get-tuple-element.80), channel_id=1, source_target_pairs={{0,2},{1,3},{2,0},{3,1},{4,6},{5,7},{6,4},{7,5},{8,10},{9,11},{10,... | collective-permute-start | bytes 196616 | tf_op jit(solution)/shard_map/ppermute | solution.py:30
  54.0 5.2 %collective-permute-start.23 = (bf16[64,512]{1,0:T(8,128)(2,1)S(1)}, bf16[64,512]{1,0:T(8,128)(2,1)S(1)}, u32[]{:S(2)}, u32[]{:S(2)}) collective-permute-start(bf16[64,512]{1,0:T(8,128)(2,1)S(1)} %get-tuple-element.81), channel_id=1, source_target_pairs={{0,6},{1,7},{2,4},{3,5},{4,2},{5,3},{6,0},{7,1},{8,14},{9,15},{10,... | collective-permute-start | bytes 196616 | tf_op jit(solution)/shard_map/ppermute | solution.py:30
  59.6 5.9 %collective-permute-start.25 = (bf16[64,512]{1,0:T(8,128)(2,1)S(1)}, bf16[64,512]{1,0:T(8,128)(2,1)S(1)}, u32[]{:S(2)}, u32[]{:S(2)}) collective-permute-start(bf16[64,512]{1,0:T(8,128)(2,1)S(1)} %fusion.1), channel_id=1, source_target_pairs={{0,8},{1,9},{2,10},{3,11},{4,12},{5,13},{6,14},{7,15},{8,0},{9,1},... | collective-permute-start | bytes 196616 | tf_op jit(solution)/shard_map/ppermute | solution.py:30
  65.6 5.2 %collective-permute-start.27 = (bf16[64,512]{1,0:T(8,128)(2,1)S(1)}, bf16[64,512]{1,0:T(8,128)(2,1)S(1)}, u32[]{:S(2)}, u32[]{:S(2)}) collective-permute-start(bf16[64,512]{1,0:T(8,128)(2,1)S(1)} %get-tuple-element.87.refs_2_), channel_id=1, source_target_pairs={{0,6},{1,7},{2,4},{3,5},{4,2},{5,3},{6,0},{7,1},{8,14},{9,15},{10,... | collective-permute-start | bytes 196616 | tf_op jit(solution)/shard_map/ppermute | solution.py:30
  66.7 4.4 %collective-permute-start.26 = (bf16[64,512]{1,0:T(8,128)(2,1)S(1)}, bf16[64,512]{1,0:T(8,128)(2,1)S(1)}, u32[]{:S(2)}, u32[]{:S(2)}) collective-permute-start(bf16[64,512]{1,0:T(8,128)(2,1)S(1)} %get-tuple-element.87.refs_2_), channel_id=1, source_target_pairs={{0,4},{1,5},{2,6},{3,7},{4,0},{5,1},{6,2},{7,3},{8,12},{9,13},{10,... | collective-permute-start | bytes 196616 | tf_op jit(solution)/shard_map/ppermute | solution.py:30
  (12 other events, 43.9 us)

commit v6 on v5

--- a/solution.py
+++ b/solution.py
@@ -15,6 +15,7 @@
 UNIT = CORES * QUAD
 VMEM = pl.BlockSpec(memory_space=pltpu.VMEM)
 F32, BF16 = jnp.float32, jnp.bfloat16
+SUM = F32
 
 
 def params(a_bytes):
@@ -198,7 +199,7 @@
         low.append(new.astype(BF16).T)
         lows[i][...] = low[i]
     for k in range(1, QUAD):
-        pieces[k - 1][...] = column_product(low, a, me ^ k).astype(BF16)
+        pieces[k - 1][...] = column_product(low, a, me ^ k).astype(SUM)
 
 
 def own_columns_kernel(*refs):
@@ -230,7 +231,7 @@
     core = place()[2]
     limits = params(4 * QUAD * rows * wide)
     state = jax.ShapeDtypeStruct((half, wide), F32)
-    piece = jax.ShapeDtypeStruct((half, wide), BF16)
+    piece = jax.ShapeDtypeStruct((half, wide), SUM)
     side = jax.ShapeDtypeStruct((rows, half), F32)
 
     def call(kernel, out_shape, *operands):
@@ -262,7 +263,7 @@
     for mask in far_masks:
         fars = fars + [swap(f, mask) for f in fars]
     sums = [k + swap(s, 1) for k, s in zip(keeps, sends)]
-    pieces = [s.astype(BF16) for s in sums[1:]]
+    pieces = [s.astype(SUM) for s in sums[1:]]
     def send(pieces, last):
         order = [k for k in range(1, QUAD) if k != last] + [last]
         moved = {k: swap(pieces[k], k * CORES) for k in order}
@@ -296,7 +297,7 @@
             total = call(own_columns_kernel, state, *a, *lows, *got[:-1]) - cost
         total = total + got[-1].astype(F32)
         for mask in far_masks:
-            total = total + swap(total.astype(BF16), mask).astype(F32)
+            total = total + swap(total.astype(SUM), mask).astype(F32)
         updated = jnp.clip(primal + STEP * total, 0.0, limit)
         ahead = (2.0 * updated - primal).astype(BF16)
         primal = updated

time: 75.2 us -> 88.1 us (1.17)
  waiting for transfers between devices: 32.6 us -> 40.5 us
  starting transfers between devices: 30.1 us -> 35.1 us
    ppermute x31, waiting for transfers between devices: 32.6 us -> 40.5 us  [swap(): lax.ppermute(x, 'row', [(i, i ^ mask) for i in range(lax.axis_size('row'))])]
    ppermute x31, starting transfers between devices: 30.1 us -> 35.1 us  [swap(): lax.ppermute(x, 'row', [(i, i ^ mask) for i in range(lax.axis_size('row'))])]
  transfers between devices with their start and end apart: 31 -> 31, of which waited for: 22 -> 21; matrix products, arithmetic and copies ran while one was open for 0% -> 0% of each run, Pallas kernels for 6% -> 5%
where the time goes in v6:
time: 88.1 us; the launch traced here: 87.9 us
  waiting for transfers between devices  40.5 us (46%)
  starting transfers between devices  35.1 us (40%)
  Pallas kernels  10.4 us (12%)
  other arithmetic  1 us (1%)
  between operations  0.9 us (1%)
    ppermute x31, waiting for transfers between devices, swap(): lax.ppermute(x, 'row', [(i, i ^ mask) for i in range(lax.axis_size('row'))])  40.5 us
    ppermute x31, starting transfers between devices, swap(): lax.ppermute(x, 'row', [(i, i ^ mask) for i in range(lax.axis_size('row'))])  35.1 us
    pallas_call x15, Pallas kernels, call(): pl.pallas_call(kernel, out_shape=out_shape, in_specs=[VMEM] * len(operand...  8.35 us
    pallas_call x1, Pallas kernels, dense(): pl.pallas_call(functools.partial(dense_kernel, span, chunks), out_shape=j...  2.06 us
  transfers between devices with their start and end apart: 31, of which 21 were waited for; matrix products, arithmetic and copies ran while one was open for 0% of the time, Pallas kernels for 5%

profile of v6, /device:TPU:0, one launch (start us, length us, event | category | flops | bytes accessed | tf_op | source)
XLA Modules:
  0.0 87.9 jit_solution(14693203117171117390)
XLA Ops:
  1.3 2.1 %shard_map.95.a_ref.refs_0_.a = bf16[2,4,256,512]{3,2,1,0:T(8,128)(2,1)S(1)} custom-call(s32[64]{0:T(128)S(1)} %multiply_add_fusion.at_hbm, bf16[64,128,128]{2,1,0:T(8,128)(2,1)} %tile_hbm.1), custom_call_target="tpu_custom_call" | custom-call | tf_op jit(solution)/shard_map/pallas_call | solution.py:80
  6.2 2.8 %collective-permute-start.4 = (f32[64,512]{1,0:T(8,128)S(1)}, f32[64,512]{1,0:T(8,128)S(1)}, u32[]{:S(2)}, u32[]{:S(2)}) collective-permute-start(f32[64,512]{1,0:T(8,128)S(1)} %add.50), channel_id=1, source_target_pairs={{0,2},{1,3},{2,0},{3,1},{4,6},{5,7},{6,4},{7,5},{8,10},{9,11},{10,... | collective-permute-start | bytes 393224 | tf_op jit(solution)/shard_map/ppermute | solution.py:31
  9.0 1.6 %collective-permute-start.6 = (f32[64,512]{1,0:T(8,128)S(1)}, f32[64,512]{1,0:T(8,128)S(1)}, u32[]{:S(2)}, u32[]{:S(2)}) collective-permute-start(f32[64,512]{1,0:T(8,128)S(1)} %add.52), channel_id=1, source_target_pairs={{0,6},{1,7},{2,4},{3,5},{4,2},{5,3},{6,0},{7,1},{8,14},{9,15},{10,... | collective-permute-start | bytes 393224 | tf_op jit(solution)/shard_map/ppermute | solution.py:31
  10.8 2.9 %collective-permute-start.1 = (f32[144,128]{1,0:T(8,128)S(1)}, f32[144,128]{1,0:T(8,128)S(1)}, u32[]{:S(2)}, u32[]{:S(2)}) collective-permute-start(f32[144,128]{1,0:T(8,128)S(1)} %pad_maximum_fusion), channel_id=1, source_target_pairs={{0,8},{1,9},{2,10},{3,11},{4,12},{5,13},{6,14},{7,15},{8,0},{9,1},... | collective-permute-start | bytes 221192 | tf_op jit(solution)/shard_map/ppermute | solution.py:31
  13.8 4.3 %collective-permute-done.1.refs_0_ = f32[144,128]{1,0:T(8,128)S(1)} collective-permute-done((f32[144,128]{1,0:T(8,128)S(1)}, f32[144,128]{1,0:T(8,128)S(1)}, u32[]{:S(2)}, u32[]{:S(2)}) %collective-permute-start.1) | collective-permute-done | bytes 73760 | tf_op jit(solution)/shard_map/ppermute | solution.py:31
  19.0 2.7 %collective-permute-start.9 = (f32[64,512]{1,0:T(8,128)S(1)}, f32[64,512]{1,0:T(8,128)S(1)}, u32[]{:S(2)}, u32[]{:S(2)}) collective-permute-start(f32[64,512]{1,0:T(8,128)S(1)} %add_add_fusion), channel_id=1, source_target_pairs={{0,8},{1,9},{2,10},{3,11},{4,12},{5,13},{6,14},{7,15},{8,0},{9,1},... | collective-permute-start | bytes 393224 | tf_op jit(solution)/shard_map/ppermute | solution.py:31
  22.2 6.4 %collective-permute-done.9 = f32[64,512]{1,0:T(8,128)S(1)} collective-permute-done((f32[64,512]{1,0:T(8,128)S(1)}, f32[64,512]{1,0:T(8,128)S(1)}, u32[]{:S(2)}, u32[]{:S(2)}) %collective-permute-start.9) | collective-permute-done | bytes 131104 | tf_op jit(solution)/shard_map/ppermute | solution.py:31
  28.6 1.8 %collective-permute-start.12 = (bf16[64,512]{1,0:T(8,128)(2,1)S(1)}, bf16[64,512]{1,0:T(8,128)(2,1)S(1)}, u32[]{:S(2)}, u32[]{:S(2)}) collective-permute-start(bf16[64,512]{1,0:T(8,128)(2,1)S(1)} %get-tuple-element.100.refs_2_), channel_id=1, source_target_pairs={{0,6},{1,7},{2,4},{3,5},{4,2},{5,3},{6,0},{7,1},{8,14},{9,15},{10,... | collective-permute-start | bytes 196616 | tf_op jit(solution)/shard_map/ppermute | solution.py:31
  30.4 1.4 %collective-permute-start.11 = (bf16[64,512]{1,0:T(8,128)(2,1)S(1)}, bf16[64,512]{1,0:T(8,128)(2,1)S(1)}, u32[]{:S(2)}, u32[]{:S(2)}) collective-permute-start(bf16[64,512]{1,0:T(8,128)(2,1)S(1)} %get-tuple-element.100.refs_2_), channel_id=1, source_target_pairs={{0,4},{1,5},{2,6},{3,7},{4,0},{5,1},{6,2},{7,3},{8,12},{9,13},{10,... | collective-permute-start | bytes 196616 | tf_op jit(solution)/shard_map/ppermute | solution.py:31
  32.2 2.0 %collective-permute-done.12.refs_4_ = bf16[64,512]{1,0:T(8,128)(2,1)S(1)} collective-permute-done((bf16[64,512]{1,0:T(8,128)(2,1)S(1)}, bf16[64,512]{1,0:T(8,128)(2,1)S(1)}, u32[]{:S(2)}, u32[]{:S(2)}) %collective-permute-start.12) | collective-permute-done | bytes 65568 | tf_op jit(solution)/shard_map/ppermute | solution.py:31
  37.7 1.9 %collective-permute-start.16 = (f32[64,512]{1,0:T(8,128)S(1)}, f32[64,512]{1,0:T(8,128)S(1)}, u32[]{:S(2)}, u32[]{:S(2)}) collective-permute-start(f32[64,512]{1,0:T(8,128)S(1)} %get-tuple-element.72), channel_id=1, source_target_pairs={{0,6},{1,7},{2,4},{3,5},{4,2},{5,3},{6,0},{7,1},{8,14},{9,15},{10,... | collective-permute-start | bytes 393224 | tf_op jit(solution)/shard_map/ppermute | solution.py:31
  40.6 3.5 %collective-permute-done.15.refs_4_ = f32[64,512]{1,0:T(8,128)S(1)} collective-permute-done((f32[64,512]{1,0:T(8,128)S(1)}, f32[64,512]{1,0:T(8,128)S(1)}, u32[]{:S(2)}, u32[]{:S(2)}) %collective-permute-start.15) | collective-permute-done | bytes 131104 | tf_op jit(solution)/shard_map/ppermute | solution.py:31
  45.4 3.0 %collective-permute-start.18 = (f32[64,512]{1,0:T(8,128)S(1)}, f32[64,512]{1,0:T(8,128)S(1)}, u32[]{:S(2)}, u32[]{:S(2)}) collective-permute-start(f32[64,512]{1,0:T(8,128)S(1)} %subtract_add_fusion.1), channel_id=1, source_target_pairs={{0,8},{1,9},{2,10},{3,11},{4,12},{5,13},{6,14},{7,15},{8,0},{9,1},... | collective-permute-start | bytes 393224 | tf_op jit(solution)/shard_map/ppermute | solution.py:31
  48.4 4.4 %collective-permute-done.18 = f32[64,512]{1,0:T(8,128)S(1)} collective-permute-done((f32[64,512]{1,0:T(8,128)S(1)}, f32[64,512]{1,0:T(8,128)S(1)}, u32[]{:S(2)}, u32[]{:S(2)}) %collective-permute-start.18) | collective-permute-done | bytes 131104 | tf_op jit(solution)/shard_map/ppermute | solution.py:31
  52.8 1.1 %collective-permute-start.20 = (bf16[64,512]{1,0:T(8,128)(2,1)S(1)}, bf16[64,512]{1,0:T(8,128)(2,1)S(1)}, u32[]{:S(2)}, u32[]{:S(2)}) collective-permute-start(bf16[64,512]{1,0:T(8,128)(2,1)S(1)} %get-tuple-element.98.refs_2_), channel_id=1, source_target_pairs={{0,6},{1,7},{2,4},{3,5},{4,2},{5,3},{6,0},{7,1},{8,14},{9,15},{10,... | collective-permute-start | bytes 196616 | tf_op jit(solution)/shard_map/ppermute | solution.py:31
  54.9 1.4 %collective-permute-start.21 = (bf16[64,512]{1,0:T(8,128)(2,1)S(1)}, bf16[64,512]{1,0:T(8,128)(2,1)S(1)}, u32[]{:S(2)}, u32[]{:S(2)}) collective-permute-start(bf16[64,512]{1,0:T(8,128)(2,1)S(1)} %get-tuple-element.98.refs_2_), channel_id=1, source_target_pairs={{0,2},{1,3},{2,0},{3,1},{4,6},{5,7},{6,4},{7,5},{8,10},{9,11},{10,... | collective-permute-start | bytes 196616 | tf_op jit(solution)/shard_map/ppermute | solution.py:31
  56.3 1.7 %collective-permute-done.20.refs_4_ = bf16[64,512]{1,0:T(8,128)(2,1)S(1)} collective-permute-done((bf16[64,512]{1,0:T(8,128)(2,1)S(1)}, bf16[64,512]{1,0:T(8,128)(2,1)S(1)}, u32[]{:S(2)}, u32[]{:S(2)}) %collective-permute-start.20) | collective-permute-done | bytes 65568 | tf_op jit(solution)/shard_map/ppermute | solution.py:31
  61.0 2.7 %collective-permute-start.22 = (f32[64,512]{1,0:T(8,128)S(1)}, f32[64,512]{1,0:T(8,128)S(1)}, u32[]{:S(2)}, u32[]{:S(2)}) collective-permute-start(f32[64,512]{1,0:T(8,128)S(1)} %get-tuple-element.80), channel_id=1, source_target_pairs={{0,2},{1,3},{2,0},{3,1},{4,6},{5,7},{6,4},{7,5},{8,10},{9,11},{10,... | collective-permute-start | bytes 393224 | tf_op jit(solution)/shard_map/ppermute | solution.py:31
  65.2 1.4 %collective-permute-done.22.refs_4_ = f32[64,512]{1,0:T(8,128)S(1)} collective-permute-done((f32[64,512]{1,0:T(8,128)S(1)}, f32[64,512]{1,0:T(8,128)S(1)}, u32[]{:S(2)}, u32[]{:S(2)}) %collective-permute-start.22) | collective-permute-done | bytes 131104 | tf_op jit(solution)/shard_map/ppermute | solution.py:31
  66.6 3.6 %collective-permute-done.23.refs_5_ = f32[64,512]{1,0:T(8,128)S(1)} collective-permute-done((f32[64,512]{1,0:T(8,128)S(1)}, f32[64,512]{1,0:T(8,128)S(1)}, u32[]{:S(2)}, u32[]{:S(2)}) %collective-permute-start.23) | collective-permute-done | bytes 131104 | tf_op jit(solution)/shard_map/ppermute | solution.py:31
  70.6 1.5 %collective-permute-start.25 = (f32[64,512]{1,0:T(8,128)S(1)}, f32[64,512]{1,0:T(8,128)S(1)}, u32[]{:S(2)}, u32[]{:S(2)}) collective-permute-start(f32[64,512]{1,0:T(8,128)S(1)} %subtract_add_fusion), channel_id=1, source_target_pairs={{0,8},{1,9},{2,10},{3,11},{4,12},{5,13},{6,14},{7,15},{8,0},{9,1},... | collective-permute-start | bytes 393224 | tf_op jit(solution)/shard_map/ppermute | solution.py:31
  72.1 5.8 %collective-permute-done.25 = f32[64,512]{1,0:T(8,128)S(1)} collective-permute-done((f32[64,512]{1,0:T(8,128)S(1)}, f32[64,512]{1,0:T(8,128)S(1)}, u32[]{:S(2)}, u32[]{:S(2)}) %collective-permute-start.25) | collective-permute-done | bytes 131104 | tf_op jit(solution)/shard_map/ppermute | solution.py:31
  79.0 2.2 %collective-permute-start.26 = (bf16[64,512]{1,0:T(8,128)(2,1)S(1)}, bf16[64,512]{1,0:T(8,128)(2,1)S(1)}, u32[]{:S(2)}, u32[]{:S(2)}) collective-permute-start(bf16[64,512]{1,0:T(8,128)(2,1)S(1)} %get-tuple-element.87.refs_2_), channel_id=1, source_target_pairs={{0,4},{1,5},{2,6},{3,7},{4,0},{5,1},{6,2},{7,3},{8,12},{9,13},{10,... | collective-permute-start | bytes 196616 | tf_op jit(solution)/shard_map/ppermute | solution.py:31
  81.6 1.2 %collective-permute-done.28.other = f32[64,128]{1,0:T(8,128)S(1)} collective-permute-done((f32[64,128]{1,0:T(8,128)S(1)}, f32[64,128]{1,0:T(8,128)S(1)}, u32[]{:S(2)}, u32[]{:S(2)}) %collective-permute-start.28) | collective-permute-done | bytes 32800 | tf_op jit(solution)/shard_map/ppermute | solution.py:31
  (77 shorter events, 23.7 us)
Async XLA Ops:
  4.4 4.6 %collective-permute-start.5 = (f32[64,512]{1,0:T(8,128)S(1)}, f32[64,512]{1,0:T(8,128)S(1)}, u32[]{:S(2)}, u32[]{:S(2)}) collective-permute-start(f32[64,512]{1,0:T(8,128)S(1)} %get-tuple-element.59), channel_id=1, source_target_pairs={{0,1},{1,0},{2,3},{3,2},{4,5},{5,4},{6,7},{7,6},{8,9},{9,8},{10,11... | collective-permute-start | bytes 393224 | tf_op jit(solution)/shard_map/ppermute | solution.py:31
  4.5 6.1 %collective-permute-start.7 = (f32[64,512]{1,0:T(8,128)S(1)}, f32[64,512]{1,0:T(8,128)S(1)}, u32[]{:S(2)}, u32[]{:S(2)}) collective-permute-start(f32[64,512]{1,0:T(8,128)S(1)} %get-tuple-element.61), channel_id=1, source_target_pairs={{0,1},{1,0},{2,3},{3,2},{4,5},{5,4},{6,7},{7,6},{8,9},{9,8},{10,11... | collective-permute-start | bytes 393224 | tf_op jit(solution)/shard_map/ppermute | solution.py:31
  5.0 13.0 %collective-permute-start.2 = (f32[64,512]{1,0:T(8,128)S(1)}, f32[64,512]{1,0:T(8,128)S(1)}, u32[]{:S(2)}, u32[]{:S(2)}) collective-permute-start(f32[64,512]{1,0:T(8,128)S(1)} %get-tuple-element.54), channel_id=1, source_target_pairs={{0,1},{1,0},{2,3},{3,2},{4,5},{5,4},{6,7},{7,6},{8,9},{9,8},{10,11... | collective-permute-start | bytes 393224 | tf_op jit(solution)/shard_map/ppermute | solution.py:31
  6.2 11.8 %collective-permute-start.4 = (f32[64,512]{1,0:T(8,128)S(1)}, f32[64,512]{1,0:T(8,128)S(1)}, u32[]{:S(2)}, u32[]{:S(2)}) collective-permute-start(f32[64,512]{1,0:T(8,128)S(1)} %add.50), channel_id=1, source_target_pairs={{0,2},{1,3},{2,0},{3,1},{4,6},{5,7},{6,4},{7,5},{8,10},{9,11},{10,... | collective-permute-start | bytes 393224 | tf_op jit(solution)/shard_map/ppermute | solution.py:31
  9.0 9.0 %collective-permute-start.6 = (f32[64,512]{1,0:T(8,128)S(1)}, f32[64,512]{1,0:T(8,128)S(1)}, u32[]{:S(2)}, u32[]{:S(2)}) collective-permute-start(f32[64,512]{1,0:T(8,128)S(1)} %add.52), channel_id=1, source_target_pairs={{0,6},{1,7},{2,4},{3,5},{4,2},{5,3},{6,0},{7,1},{8,14},{9,15},{10,... | collective-permute-start | bytes 393224 | tf_op jit(solution)/shard_map/ppermute | solution.py:31
  10.7 8.2 %collective-permute-start.8 = (f32[64,512]{1,0:T(8,128)S(1)}, f32[64,512]{1,0:T(8,128)S(1)}, u32[]{:S(2)}, u32[]{:S(2)}) collective-permute-start(f32[64,512]{1,0:T(8,128)S(1)} %add.54), channel_id=1, source_target_pairs={{0,4},{1,5},{2,6},{3,7},{4,0},{5,1},{6,2},{7,3},{8,12},{9,13},{10,... | collective-permute-start | bytes 393224 | tf_op jit(solution)/shard_map/ppermute | solution.py:31
  10.8 7.2 %collective-permute-start.1 = (f32[144,128]{1,0:T(8,128)S(1)}, f32[144,128]{1,0:T(8,128)S(1)}, u32[]{:S(2)}, u32[]{:S(2)}) collective-permute-start(f32[144,128]{1,0:T(8,128)S(1)} %pad_maximum_fusion), channel_id=1, source_target_pairs={{0,8},{1,9},{2,10},{3,11},{4,12},{5,13},{6,14},{7,15},{8,0},{9,1},... | collective-permute-start | bytes 221192 | tf_op jit(solution)/shard_map/ppermute | solution.py:31
  18.9 16.0 %collective-permute-start.10 = (bf16[2,4,256,512]{3,2,1,0:T(8,128)(2,1)S(1)}, bf16[2,4,256,512]{3,2,1,0:T(8,128)(2,1)S(1)}, u32[]{:S(2)}, u32[]{:S(2)}) collective-permute-start(bf16[2,4,256,512]{3,2,1,0:T(8,128)(2,1)S(1)} %shard_map.95.a_ref.refs_0_.a), channel_id=1, source_target_pairs={{0,1},{1,0},{2,3},{3,2},{4,5},{5,4},{6,7},{7,6},{8,9},{9,8},{10,11... | collective-permute-start | bytes 6291464 | tf_op jit(solution)/shard_map/ppermute | solution.py:31
  19.0 9.6 %collective-permute-start.9 = (f32[64,512]{1,0:T(8,128)S(1)}, f32[64,512]{1,0:T(8,128)S(1)}, u32[]{:S(2)}, u32[]{:S(2)}) collective-permute-start(f32[64,512]{1,0:T(8,128)S(1)} %add_add_fusion), channel_id=1, source_target_pairs={{0,8},{1,9},{2,10},{3,11},{4,12},{5,13},{6,14},{7,15},{8,0},{9,1},... | collective-permute-start | bytes 393224 | tf_op jit(solution)/shard_map/ppermute | solution.py:31
  22.0 13.9 %collective-permute-start.14 = (f32[2,256,64]{2,1,0:T(8,128)S(1)}, f32[2,256,64]{2,1,0:T(8,128)S(1)}, u32[]{:S(2)}, u32[]{:S(2)}) collective-permute-start(f32[2,256,64]{2,1,0:T(8,128)S(1)} %get-tuple-element.68), channel_id=1, source_target_pairs={{0,1},{1,0},{2,3},{3,2},{4,5},{5,4},{6,7},{7,6},{8,9},{9,8},{10,11... | collective-permute-start | bytes 393224 | tf_op jit(solution)/shard_map/ppermute | solution.py:31
  28.6 5.6 %collective-permute-start.12 = (bf16[64,512]{1,0:T(8,128)(2,1)S(1)}, bf16[64,512]{1,0:T(8,128)(2,1)S(1)}, u32[]{:S(2)}, u32[]{:S(2)}) collective-permute-start(bf16[64,512]{1,0:T(8,128)(2,1)S(1)} %get-tuple-element.100.refs_2_), channel_id=1, source_target_pairs={{0,6},{1,7},{2,4},{3,5},{4,2},{5,3},{6,0},{7,1},{8,14},{9,15},{10,... | collective-permute-start | bytes 196616 | tf_op jit(solution)/shard_map/ppermute | solution.py:31
  30.4 4.5 %collective-permute-start.11 = (bf16[64,512]{1,0:T(8,128)(2,1)S(1)}, bf16[64,512]{1,0:T(8,128)(2,1)S(1)}, u32[]{:S(2)}, u32[]{:S(2)}) collective-permute-start(bf16[64,512]{1,0:T(8,128)(2,1)S(1)} %get-tuple-element.100.refs_2_), channel_id=1, source_target_pairs={{0,4},{1,5},{2,6},{3,7},{4,0},{5,1},{6,2},{7,3},{8,12},{9,13},{10,... | collective-permute-start | bytes 196616 | tf_op jit(solution)/shard_map/ppermute | solution.py:31
  37.1 7.1 %collective-permute-start.15 = (f32[64,512]{1,0:T(8,128)S(1)}, f32[64,512]{1,0:T(8,128)S(1)}, u32[]{:S(2)}, u32[]{:S(2)}) collective-permute-start(f32[64,512]{1,0:T(8,128)S(1)} %get-tuple-element.71), channel_id=1, source_target_pairs={{0,2},{1,3},{2,0},{3,1},{4,6},{5,7},{6,4},{7,5},{8,10},{9,11},{10,... | collective-permute-start | bytes 393224 | tf_op jit(solution)/shard_map/ppermute | solution.py:31
  37.7 6.4 %collective-permute-start.16 = (f32[64,512]{1,0:T(8,128)S(1)}, f32[64,512]{1,0:T(8,128)S(1)}, u32[]{:S(2)}, u32[]{:S(2)}) collective-permute-start(f32[64,512]{1,0:T(8,128)S(1)} %get-tuple-element.72), channel_id=1, source_target_pairs={{0,6},{1,7},{2,4},{3,5},{4,2},{5,3},{6,0},{7,1},{8,14},{9,15},{10,... | collective-permute-start | bytes 393224 | tf_op jit(solution)/shard_map/ppermute | solution.py:31
  39.6 5.7 %collective-permute-start.17 = (f32[64,512]{1,0:T(8,128)S(1)}, f32[64,512]{1,0:T(8,128)S(1)}, u32[]{:S(2)}, u32[]{:S(2)}) collective-permute-start(f32[64,512]{1,0:T(8,128)S(1)} %get-tuple-element.73), channel_id=1, source_target_pairs={{0,4},{1,5},{2,6},{3,7},{4,0},{5,1},{6,2},{7,3},{8,12},{9,13},{10,... | collective-permute-start | bytes 393224 | tf_op jit(solution)/shard_map/ppermute | solution.py:31
  45.4 7.4 %collective-permute-start.18 = (f32[64,512]{1,0:T(8,128)S(1)}, f32[64,512]{1,0:T(8,128)S(1)}, u32[]{:S(2)}, u32[]{:S(2)}) collective-permute-start(f32[64,512]{1,0:T(8,128)S(1)} %subtract_add_fusion.1), channel_id=1, source_target_pairs={{0,8},{1,9},{2,10},{3,11},{4,12},{5,13},{6,14},{7,15},{8,0},{9,1},... | collective-permute-start | bytes 393224 | tf_op jit(solution)/shard_map/ppermute | solution.py:31
  52.8 5.2 %collective-permute-start.20 = (bf16[64,512]{1,0:T(8,128)(2,1)S(1)}, bf16[64,512]{1,0:T(8,128)(2,1)S(1)}, u32[]{:S(2)}, u32[]{:S(2)}) collective-permute-start(bf16[64,512]{1,0:T(8,128)(2,1)S(1)} %get-tuple-element.98.refs_2_), channel_id=1, source_target_pairs={{0,6},{1,7},{2,4},{3,5},{4,2},{5,3},{6,0},{7,1},{8,14},{9,15},{10,... | collective-permute-start | bytes 196616 | tf_op jit(solution)/shard_map/ppermute | solution.py:31
  54.9 5.1 %collective-permute-start.21 = (bf16[64,512]{1,0:T(8,128)(2,1)S(1)}, bf16[64,512]{1,0:T(8,128)(2,1)S(1)}, u32[]{:S(2)}, u32[]{:S(2)}) collective-permute-start(bf16[64,512]{1,0:T(8,128)(2,1)S(1)} %get-tuple-element.98.refs_2_), channel_id=1, source_target_pairs={{0,2},{1,3},{2,0},{3,1},{4,6},{5,7},{6,4},{7,5},{8,10},{9,11},{10,... | collective-permute-start | bytes 196616 | tf_op jit(solution)/shard_map/ppermute | solution.py:31
  61.0 5.6 %collective-permute-start.22 = (f32[64,512]{1,0:T(8,128)S(1)}, f32[64,512]{1,0:T(8,128)S(1)}, u32[]{:S(2)}, u32[]{:S(2)}) collective-permute-start(f32[64,512]{1,0:T(8,128)S(1)} %get-tuple-element.80), channel_id=1, source_target_pairs={{0,2},{1,3},{2,0},{3,1},{4,6},{5,7},{6,4},{7,5},{8,10},{9,11},{10,... | collective-permute-start | bytes 393224 | tf_op jit(solution)/shard_map/ppermute | solution.py:31
  63.7 6.6 %collective-permute-start.23 = (f32[64,512]{1,0:T(8,128)S(1)}, f32[64,512]{1,0:T(8,128)S(1)}, u32[]{:S(2)}, u32[]{:S(2)}) collective-permute-start(f32[64,512]{1,0:T(8,128)S(1)} %get-tuple-element.81), channel_id=1, source_target_pairs={{0,6},{1,7},{2,4},{3,5},{4,2},{5,3},{6,0},{7,1},{8,14},{9,15},{10,... | collective-permute-start | bytes 393224 | tf_op jit(solution)/shard_map/ppermute | solution.py:31
  64.2 6.3 %collective-permute-start.24 = (f32[64,512]{1,0:T(8,128)S(1)}, f32[64,512]{1,0:T(8,128)S(1)}, u32[]{:S(2)}, u32[]{:S(2)}) collective-permute-start(f32[64,512]{1,0:T(8,128)S(1)} %get-tuple-element.82), channel_id=1, source_target_pairs={{0,4},{1,5},{2,6},{3,7},{4,0},{5,1},{6,2},{7,3},{8,12},{9,13},{10,... | collective-permute-start | bytes 393224 | tf_op jit(solution)/shard_map/ppermute | solution.py:31
  70.6 7.3 %collective-permute-start.25 = (f32[64,512]{1,0:T(8,128)S(1)}, f32[64,512]{1,0:T(8,128)S(1)}, u32[]{:S(2)}, u32[]{:S(2)}) collective-permute-start(f32[64,512]{1,0:T(8,128)S(1)} %subtract_add_fusion), channel_id=1, source_target_pairs={{0,8},{1,9},{2,10},{3,11},{4,12},{5,13},{6,14},{7,15},{8,0},{9,1},... | collective-permute-start | bytes 393224 | tf_op jit(solution)/shard_map/ppermute | solution.py:31
  78.0 5.2 %collective-permute-start.27 = (bf16[64,512]{1,0:T(8,128)(2,1)S(1)}, bf16[64,512]{1,0:T(8,128)(2,1)S(1)}, u32[]{:S(2)}, u32[]{:S(2)}) collective-permute-start(bf16[64,512]{1,0:T(8,128)(2,1)S(1)} %get-tuple-element.87.refs_2_), channel_id=1, source_target_pairs={{0,6},{1,7},{2,4},{3,5},{4,2},{5,3},{6,0},{7,1},{8,14},{9,15},{10,... | collective-permute-start | bytes 196616 | tf_op jit(solution)/shard_map/ppermute | solution.py:31
  79.0 5.1 %collective-permute-start.26 = (bf16[64,512]{1,0:T(8,128)(2,1)S(1)}, bf16[64,512]{1,0:T(8,128)(2,1)S(1)}, u32[]{:S(2)}, u32[]{:S(2)}) collective-permute-start(bf16[64,512]{1,0:T(8,128)(2,1)S(1)} %get-tuple-element.87.refs_2_), channel_id=1, source_target_pairs={{0,4},{1,5},{2,6},{3,7},{4,0},{5,1},{6,2},{7,3},{8,12},{9,13},{10,... | collective-permute-start | bytes 196616 | tf_op jit(solution)/shard_map/ppermute | solution.py:31
  (12 other events, 45.7 us)

commit v7 on v5

--- a/solution.py
+++ b/solution.py
@@ -24,6 +24,11 @@
 def place():
     me = lax.axis_index("row")
     return me // UNIT, (me // CORES) % QUAD, me % CORES
+
+
+def group():
+    _, q, core = place()
+    return core ^ (q & 1) ^ (q >> 1)
 
 
 def swap(x, mask):
@@ -93,28 +98,28 @@
 
 def first_kernel(a_ref, dual_ref, primal_ref, cost_ref, limit_ref, mine_ref, other_ref, *rest):
     keeps, sends = rest[:QUAD], rest[QUAD:]
-    _, me, core = place()
+    me, first = place()[1], group() == 0
     half = keeps[0].shape[0]
     for at, ref in ((0, primal_ref), (half + 8, cost_ref)):
         turned = ref[...].T
-        mine_ref[at : at + half] = jnp.where(core == 0, turned[:half], turned[half:])
-        other_ref[at : at + half] = jnp.where(core == 0, turned[half:], turned[:half])
+        mine_ref[at : at + half] = jnp.where(first, turned[:half], turned[half:])
+        other_ref[at : at + half] = jnp.where(first, turned[half:], turned[:half])
     for ref in (mine_ref, other_ref):
         ref[half : half + 8] = jnp.broadcast_to(limit_ref[...], (8, limit_ref.shape[1]))
     low = dual_ref[...].astype(BF16).T
     for k in range(QUAD):
         total = dot(low, a_ref[0, me ^ k], 1, 0) + dot(low, a_ref[1, me ^ k], 1, 0)
-        keeps[k][...] = jnp.where(core == 0, total[:half], total[half:])
-        sends[k][...] = jnp.where(core == 0, total[half:], total[:half])
+        keeps[k][...] = jnp.where(first, total[:half], total[half:])
+        sends[k][...] = jnp.where(first, total[half:], total[:half])
 
 
 def prepare_kernel(dual, bound, mine, other):
-    core = place()[2]
+    first = group() == 0
     half = mine.shape[2]
     for i, ref in enumerate((dual, bound)):
         left, right = ref[:, :half], ref[:, half:]
-        mine[i] = jnp.where(core == 0, left, right)
-        other[i] = jnp.where(core == 0, right, left)
+        mine[i] = jnp.where(first, left, right)
+        other[i] = jnp.where(first, right, left)
 
 
 def give_kernel(primal, mine, other):
@@ -125,9 +130,9 @@
 
 
 def join_variables_kernel(mine, other, out):
-    core = place()[2]
+    first = group() == 0
     both = jnp.where(
-        core == 0,
+        first,
         jnp.concatenate([mine[...], other[...]], 0),
         jnp.concatenate([other[...], mine[...]], 0),
     )
@@ -135,9 +140,9 @@
 
 
 def join_rows_kernel(mine, other, out):
-    core = place()[2]
+    first = group() == 0
     out[...] = jnp.where(
-        core == 0,
+        first,
         jnp.concatenate([mine[...], other[...]], 1),
         jnp.concatenate([other[...], mine[...]], 1),
     )
@@ -227,7 +232,6 @@
     while UNIT << len(far_masks) < devices:
         far_masks.append(UNIT << len(far_masks))
     wide = devices * width // QUAD
-    core = place()[2]
     limits = params(4 * QUAD * rows * wide)
     state = jax.ShapeDtypeStruct((half, wide), F32)
     piece = jax.ShapeDtypeStruct((half, wide), BF16)
@@ -265,7 +269,7 @@
     pieces = [s.astype(BF16) for s in sums[1:]]
     def send(pieces, last):
         order = [k for k in range(1, QUAD) if k != last] + [last]
-        moved = {k: swap(pieces[k], k * CORES) for k in order}
+        moved = {k: swap(pieces[k], k * CORES ^ (k & 1) ^ (k >> 1)) for k in order}
         return [moved[k] for k in range(1, QUAD) if k != last] + [moved[last]]
 
     got = send([None, *pieces], SUM_LAST)

time: 75.2 us -> 74.6 us (level)
  transfers between devices with their start and end apart: 31 -> 31, of which waited for: 22 -> 14; matrix products, arithmetic and copies ran while one was open for 0% -> 0% of each run, Pallas kernels for 6% -> 6%
where the time goes in v7:
time: 74.6 us; the launch traced here: 74.4 us
  waiting for transfers between devices  32 us (43%)
  starting transfers between devices  30 us (40%)
  Pallas kernels  10.4 us (14%)
  other arithmetic  1.03 us (1%)
  between operations  0.91 us (1%)
    ppermute x31, waiting for transfers between devices, swap(): lax.ppermute(x, 'row', [(i, i ^ mask) for i in range(lax.axis_size('row'))])  32 us
    ppermute x31, starting transfers between devices, swap(): lax.ppermute(x, 'row', [(i, i ^ mask) for i in range(lax.axis_size('row'))])  30 us
    pallas_call x15, Pallas kernels, call(): pl.pallas_call(kernel, out_shape=out_shape, in_specs=[VMEM] * len(operand...  8.37 us
    pallas_call x1, Pallas kernels, dense(): pl.pallas_call(functools.partial(dense_kernel, span, chunks), out_shape=j...  2.06 us
  transfers between devices with their start and end apart: 31, of which 14 were waited for; matrix products, arithmetic and copies ran while one was open for 0% of the time, Pallas kernels for 6%

profile of v7, /device:TPU:0, one launch (start us, length us, event | category | flops | bytes accessed | tf_op | source)
XLA Modules:
  0.0 74.4 jit_solution(10879395319313559310)
XLA Ops:
  1.3 2.1 %shard_map.95.a_ref.refs_0_.a = bf16[2,4,256,512]{3,2,1,0:T(8,128)(2,1)S(1)} custom-call(s32[64]{0:T(128)S(1)} %multiply_add_fusion.at_hbm, bf16[64,128,128]{2,1,0:T(8,128)(2,1)} %tile_hbm.1), custom_call_target="tpu_custom_call" | custom-call | tf_op jit(solution)/shard_map/pallas_call | solution.py:84
  5.5 3.9 %collective-permute-start.1 = (f32[144,128]{1,0:T(8,128)S(1)}, f32[144,128]{1,0:T(8,128)S(1)}, u32[]{:S(2)}, u32[]{:S(2)}) collective-permute-start(f32[144,128]{1,0:T(8,128)S(1)} %pad_maximum_fusion), channel_id=1, source_target_pairs={{0,8},{1,9},{2,10},{3,11},{4,12},{5,13},{6,14},{7,15},{8,0},{9,1},... | collective-permute-start | bytes 221192 | tf_op jit(solution)/shard_map/ppermute | solution.py:35
  9.4 1.2 %collective-permute-start.4 = (bf16[64,512]{1,0:T(8,128)(2,1)S(1)}, bf16[64,512]{1,0:T(8,128)(2,1)S(1)}, u32[]{:S(2)}, u32[]{:S(2)}) collective-permute-start(bf16[64,512]{1,0:T(8,128)(2,1)S(1)} %add_convert_fusion.2), channel_id=1, source_target_pairs={{0,3},{1,2},{2,1},{3,0},{4,7},{5,6},{6,5},{7,4},{8,11},{9,10},{10,... | collective-permute-start | bytes 196616 | tf_op jit(solution)/shard_map/ppermute | solution.py:35
  10.6 1.6 %collective-permute-start.6 = (bf16[64,512]{1,0:T(8,128)(2,1)S(1)}, bf16[64,512]{1,0:T(8,128)(2,1)S(1)}, u32[]{:S(2)}, u32[]{:S(2)}) collective-permute-start(bf16[64,512]{1,0:T(8,128)(2,1)S(1)} %add_convert_fusion.1), channel_id=1, source_target_pairs={{0,6},{1,7},{2,4},{3,5},{4,2},{5,3},{6,0},{7,1},{8,14},{9,15},{10,... | collective-permute-start | bytes 196616 | tf_op jit(solution)/shard_map/ppermute | solution.py:35
  12.6 1.1 %collective-permute-done.1.refs_0_ = f32[144,128]{1,0:T(8,128)S(1)} collective-permute-done((f32[144,128]{1,0:T(8,128)S(1)}, f32[144,128]{1,0:T(8,128)S(1)}, u32[]{:S(2)}, u32[]{:S(2)}) %collective-permute-start.1) | collective-permute-done | bytes 73760 | tf_op jit(solution)/shard_map/ppermute | solution.py:35
  13.7 2.4 %collective-permute-done.6 = bf16[64,512]{1,0:T(8,128)(2,1)S(1)} collective-permute-done((bf16[64,512]{1,0:T(8,128)(2,1)S(1)}, bf16[64,512]{1,0:T(8,128)(2,1)S(1)}, u32[]{:S(2)}, u32[]{:S(2)}) %collective-permute-start.6) | collective-permute-done | bytes 65568 | tf_op jit(solution)/shard_map/ppermute | solution.py:35
  18.1 5.2 %collective-permute-done.9 = bf16[64,512]{1,0:T(8,128)(2,1)S(1)} collective-permute-done((bf16[64,512]{1,0:T(8,128)(2,1)S(1)}, bf16[64,512]{1,0:T(8,128)(2,1)S(1)}, u32[]{:S(2)}, u32[]{:S(2)}) %collective-permute-start.9) | collective-permute-done | bytes 65568 | tf_op jit(solution)/shard_map/ppermute | solution.py:35
  24.4 2.2 %collective-permute-start.13 = (bf16[64,512]{1,0:T(8,128)(2,1)S(1)}, bf16[64,512]{1,0:T(8,128)(2,1)S(1)}, u32[]{:S(2)}, u32[]{:S(2)}) collective-permute-start(bf16[64,512]{1,0:T(8,128)(2,1)S(1)} %get-tuple-element.100.refs_2_), channel_id=1, source_target_pairs={{0,3},{1,2},{2,1},{3,0},{4,7},{5,6},{6,5},{7,4},{8,11},{9,10},{10,... | collective-permute-start | bytes 196616 | tf_op jit(solution)/shard_map/ppermute | solution.py:35
  26.6 2.6 %collective-permute-done.12.refs_4_ = bf16[64,512]{1,0:T(8,128)(2,1)S(1)} collective-permute-done((bf16[64,512]{1,0:T(8,128)(2,1)S(1)}, bf16[64,512]{1,0:T(8,128)(2,1)S(1)}, u32[]{:S(2)}, u32[]{:S(2)}) %collective-permute-start.12) | collective-permute-done | bytes 65568 | tf_op jit(solution)/shard_map/ppermute | solution.py:35
  32.8 1.5 %collective-permute-start.17 = (bf16[64,512]{1,0:T(8,128)(2,1)S(1)}, bf16[64,512]{1,0:T(8,128)(2,1)S(1)}, u32[]{:S(2)}, u32[]{:S(2)}) collective-permute-start(bf16[64,512]{1,0:T(8,128)(2,1)S(1)} %get-tuple-element.73), channel_id=1, source_target_pairs={{0,5},{1,4},{2,7},{3,6},{4,1},{5,0},{6,3},{7,2},{8,13},{9,12},{10,... | collective-permute-start | bytes 196616 | tf_op jit(solution)/shard_map/ppermute | solution.py:35
  34.2 1.1 %collective-permute-done.15.refs_4_ = bf16[64,512]{1,0:T(8,128)(2,1)S(1)} collective-permute-done((bf16[64,512]{1,0:T(8,128)(2,1)S(1)}, bf16[64,512]{1,0:T(8,128)(2,1)S(1)}, u32[]{:S(2)}, u32[]{:S(2)}) %collective-permute-start.15) | collective-permute-done | bytes 65568 | tf_op jit(solution)/shard_map/ppermute | solution.py:35
  35.4 2.6 %collective-permute-done.16.refs_5_ = bf16[64,512]{1,0:T(8,128)(2,1)S(1)} collective-permute-done((bf16[64,512]{1,0:T(8,128)(2,1)S(1)}, bf16[64,512]{1,0:T(8,128)(2,1)S(1)}, u32[]{:S(2)}, u32[]{:S(2)}) %collective-permute-start.16) | collective-permute-done | bytes 65568 | tf_op jit(solution)/shard_map/ppermute | solution.py:35
  38.3 1.6 %collective-permute-start.18 = (bf16[64,512]{1,0:T(8,128)(2,1)S(1)}, bf16[64,512]{1,0:T(8,128)(2,1)S(1)}, u32[]{:S(2)}, u32[]{:S(2)}) collective-permute-start(bf16[64,512]{1,0:T(8,128)(2,1)S(1)} %fusion), channel_id=1, source_target_pairs={{0,8},{1,9},{2,10},{3,11},{4,12},{5,13},{6,14},{7,15},{8,0},{9,1},... | collective-permute-start | bytes 196616 | tf_op jit(solution)/shard_map/ppermute | solution.py:35
  40.0 4.5 %collective-permute-done.18 = bf16[64,512]{1,0:T(8,128)(2,1)S(1)} collective-permute-done((bf16[64,512]{1,0:T(8,128)(2,1)S(1)}, bf16[64,512]{1,0:T(8,128)(2,1)S(1)}, u32[]{:S(2)}, u32[]{:S(2)}) %collective-permute-start.18) | collective-permute-done | bytes 65568 | tf_op jit(solution)/shard_map/ppermute | solution.py:35
  44.7 1.6 %collective-permute-start.19 = (bf16[64,512]{1,0:T(8,128)(2,1)S(1)}, bf16[64,512]{1,0:T(8,128)(2,1)S(1)}, u32[]{:S(2)}, u32[]{:S(2)}) collective-permute-start(bf16[64,512]{1,0:T(8,128)(2,1)S(1)} %get-tuple-element.98.refs_2_), channel_id=1, source_target_pairs={{0,5},{1,4},{2,7},{3,6},{4,1},{5,0},{6,3},{7,2},{8,13},{9,12},{10,... | collective-permute-start | bytes 196616 | tf_op jit(solution)/shard_map/ppermute | solution.py:35
  46.3 1.5 %collective-permute-start.21 = (bf16[64,512]{1,0:T(8,128)(2,1)S(1)}, bf16[64,512]{1,0:T(8,128)(2,1)S(1)}, u32[]{:S(2)}, u32[]{:S(2)}) collective-permute-start(bf16[64,512]{1,0:T(8,128)(2,1)S(1)} %get-tuple-element.98.refs_2_), channel_id=1, source_target_pairs={{0,3},{1,2},{2,1},{3,0},{4,7},{5,6},{6,5},{7,4},{8,11},{9,10},{10,... | collective-permute-start | bytes 196616 | tf_op jit(solution)/shard_map/ppermute | solution.py:35
  47.8 2.0 %collective-permute-done.20.refs_4_ = bf16[64,512]{1,0:T(8,128)(2,1)S(1)} collective-permute-done((bf16[64,512]{1,0:T(8,128)(2,1)S(1)}, bf16[64,512]{1,0:T(8,128)(2,1)S(1)}, u32[]{:S(2)}, u32[]{:S(2)}) %collective-permute-start.20) | collective-permute-done | bytes 65568 | tf_op jit(solution)/shard_map/ppermute | solution.py:35
  52.9 1.4 %collective-permute-start.23 = (bf16[64,512]{1,0:T(8,128)(2,1)S(1)}, bf16[64,512]{1,0:T(8,128)(2,1)S(1)}, u32[]{:S(2)}, u32[]{:S(2)}) collective-permute-start(bf16[64,512]{1,0:T(8,128)(2,1)S(1)} %get-tuple-element.81), channel_id=1, source_target_pairs={{0,6},{1,7},{2,4},{3,5},{4,2},{5,3},{6,0},{7,1},{8,14},{9,15},{10,... | collective-permute-start | bytes 196616 | tf_op jit(solution)/shard_map/ppermute | solution.py:35
  55.6 3.0 %collective-permute-done.23.refs_5_ = bf16[64,512]{1,0:T(8,128)(2,1)S(1)} collective-permute-done((bf16[64,512]{1,0:T(8,128)(2,1)S(1)}, bf16[64,512]{1,0:T(8,128)(2,1)S(1)}, u32[]{:S(2)}, u32[]{:S(2)}) %collective-permute-start.23) | collective-permute-done | bytes 65568 | tf_op jit(solution)/shard_map/ppermute | solution.py:35
  59.0 2.2 %collective-permute-start.25 = (bf16[64,512]{1,0:T(8,128)(2,1)S(1)}, bf16[64,512]{1,0:T(8,128)(2,1)S(1)}, u32[]{:S(2)}, u32[]{:S(2)}) collective-permute-start(bf16[64,512]{1,0:T(8,128)(2,1)S(1)} %fusion.1), channel_id=1, source_target_pairs={{0,8},{1,9},{2,10},{3,11},{4,12},{5,13},{6,14},{7,15},{8,0},{9,1},... | collective-permute-start | bytes 196616 | tf_op jit(solution)/shard_map/ppermute | solution.py:35
  61.2 4.4 %collective-permute-done.25 = bf16[64,512]{1,0:T(8,128)(2,1)S(1)} collective-permute-done((bf16[64,512]{1,0:T(8,128)(2,1)S(1)}, bf16[64,512]{1,0:T(8,128)(2,1)S(1)}, u32[]{:S(2)}, u32[]{:S(2)}) %collective-permute-start.25) | collective-permute-done | bytes 65568 | tf_op jit(solution)/shard_map/ppermute | solution.py:35
  65.8 1.2 %collective-permute-start.26 = (bf16[64,512]{1,0:T(8,128)(2,1)S(1)}, bf16[64,512]{1,0:T(8,128)(2,1)S(1)}, u32[]{:S(2)}, u32[]{:S(2)}) collective-permute-start(bf16[64,512]{1,0:T(8,128)(2,1)S(1)} %get-tuple-element.87.refs_2_), channel_id=1, source_target_pairs={{0,5},{1,4},{2,7},{3,6},{4,1},{5,0},{6,3},{7,2},{8,13},{9,12},{10,... | collective-permute-start | bytes 196616 | tf_op jit(solution)/shard_map/ppermute | solution.py:35
  67.1 1.8 %collective-permute-start.29 = (bf16[64,512]{1,0:T(8,128)(2,1)S(1)}, bf16[64,512]{1,0:T(8,128)(2,1)S(1)}, u32[]{:S(2)}, u32[]{:S(2)}) collective-permute-start(bf16[64,512]{1,0:T(8,128)(2,1)S(1)} %get-tuple-element.87.refs_2_), channel_id=1, source_target_pairs={{0,3},{1,2},{2,1},{3,0},{4,7},{5,6},{6,5},{7,4},{8,11},{9,10},{10,... | collective-permute-start | bytes 196616 | tf_op jit(solution)/shard_map/ppermute | solution.py:35
  69.0 1.2 %collective-permute-done.28.other = f32[64,128]{1,0:T(8,128)S(1)} collective-permute-done((f32[64,128]{1,0:T(8,128)S(1)}, f32[64,128]{1,0:T(8,128)S(1)}, u32[]{:S(2)}, u32[]{:S(2)}) %collective-permute-start.28) | collective-permute-done | bytes 32800 | tf_op jit(solution)/shard_map/ppermute | solution.py:35
  (77 shorter events, 19.7 us)
Async XLA Ops:
  4.4 4.9 %collective-permute-start.3 = (f32[64,512]{1,0:T(8,128)S(1)}, f32[64,512]{1,0:T(8,128)S(1)}, u32[]{:S(2)}, u32[]{:S(2)}) collective-permute-start(f32[64,512]{1,0:T(8,128)S(1)} %get-tuple-element.57), channel_id=1, source_target_pairs={{0,1},{1,0},{2,3},{3,2},{4,5},{5,4},{6,7},{7,6},{8,9},{9,8},{10,11... | collective-permute-start | bytes 393224 | tf_op jit(solution)/shard_map/ppermute | solution.py:35
  4.5 9.2 %collective-permute-start.2 = (f32[64,512]{1,0:T(8,128)S(1)}, f32[64,512]{1,0:T(8,128)S(1)}, u32[]{:S(2)}, u32[]{:S(2)}) collective-permute-start(f32[64,512]{1,0:T(8,128)S(1)} %get-tuple-element.54), channel_id=1, source_target_pairs={{0,1},{1,0},{2,3},{3,2},{4,5},{5,4},{6,7},{7,6},{8,9},{9,8},{10,11... | collective-permute-start | bytes 393224 | tf_op jit(solution)/shard_map/ppermute | solution.py:35
  5.0 5.6 %collective-permute-start.5 = (f32[64,512]{1,0:T(8,128)S(1)}, f32[64,512]{1,0:T(8,128)S(1)}, u32[]{:S(2)}, u32[]{:S(2)}) collective-permute-start(f32[64,512]{1,0:T(8,128)S(1)} %get-tuple-element.59), channel_id=1, source_target_pairs={{0,1},{1,0},{2,3},{3,2},{4,5},{5,4},{6,7},{7,6},{8,9},{9,8},{10,11... | collective-permute-start | bytes 393224 | tf_op jit(solution)/shard_map/ppermute | solution.py:35
  5.0 7.2 %collective-permute-start.7 = (f32[64,512]{1,0:T(8,128)S(1)}, f32[64,512]{1,0:T(8,128)S(1)}, u32[]{:S(2)}, u32[]{:S(2)}) collective-permute-start(f32[64,512]{1,0:T(8,128)S(1)} %get-tuple-element.61), channel_id=1, source_target_pairs={{0,1},{1,0},{2,3},{3,2},{4,5},{5,4},{6,7},{7,6},{8,9},{9,8},{10,11... | collective-permute-start | bytes 393224 | tf_op jit(solution)/shard_map/ppermute | solution.py:35
  5.5 8.2 %collective-permute-start.1 = (f32[144,128]{1,0:T(8,128)S(1)}, f32[144,128]{1,0:T(8,128)S(1)}, u32[]{:S(2)}, u32[]{:S(2)}) collective-permute-start(f32[144,128]{1,0:T(8,128)S(1)} %pad_maximum_fusion), channel_id=1, source_target_pairs={{0,8},{1,9},{2,10},{3,11},{4,12},{5,13},{6,14},{7,15},{8,0},{9,1},... | collective-permute-start | bytes 221192 | tf_op jit(solution)/shard_map/ppermute | solution.py:35
  10.6 5.5 %collective-permute-start.6 = (bf16[64,512]{1,0:T(8,128)(2,1)S(1)}, bf16[64,512]{1,0:T(8,128)(2,1)S(1)}, u32[]{:S(2)}, u32[]{:S(2)}) collective-permute-start(bf16[64,512]{1,0:T(8,128)(2,1)S(1)} %add_convert_fusion.1), channel_id=1, source_target_pairs={{0,6},{1,7},{2,4},{3,5},{4,2},{5,3},{6,0},{7,1},{8,14},{9,15},{10,... | collective-permute-start | bytes 196616 | tf_op jit(solution)/shard_map/ppermute | solution.py:35
  16.4 12.8 %collective-permute-start.10 = (bf16[2,4,256,512]{3,2,1,0:T(8,128)(2,1)S(1)}, bf16[2,4,256,512]{3,2,1,0:T(8,128)(2,1)S(1)}, u32[]{:S(2)}, u32[]{:S(2)}) collective-permute-start(bf16[2,4,256,512]{3,2,1,0:T(8,128)(2,1)S(1)} %shard_map.95.a_ref.refs_0_.a), channel_id=1, source_target_pairs={{0,1},{1,0},{2,3},{3,2},{4,5},{5,4},{6,7},{7,6},{8,9},{9,8},{10,11... | collective-permute-start | bytes 6291464 | tf_op jit(solution)/shard_map/ppermute | solution.py:35
  16.6 6.7 %collective-permute-start.9 = (bf16[64,512]{1,0:T(8,128)(2,1)S(1)}, bf16[64,512]{1,0:T(8,128)(2,1)S(1)}, u32[]{:S(2)}, u32[]{:S(2)}) collective-permute-start(bf16[64,512]{1,0:T(8,128)(2,1)S(1)} %get-tuple-element.102), channel_id=1, source_target_pairs={{0,8},{1,9},{2,10},{3,11},{4,12},{5,13},{6,14},{7,15},{8,0},{9,1},... | collective-permute-start | bytes 196616 | tf_op jit(solution)/shard_map/ppermute | solution.py:35
  17.9 12.3 %collective-permute-start.14 = (f32[2,256,64]{2,1,0:T(8,128)S(1)}, f32[2,256,64]{2,1,0:T(8,128)S(1)}, u32[]{:S(2)}, u32[]{:S(2)}) collective-permute-start(f32[2,256,64]{2,1,0:T(8,128)S(1)} %get-tuple-element.68), channel_id=1, source_target_pairs={{0,1},{1,0},{2,3},{3,2},{4,5},{5,4},{6,7},{7,6},{8,9},{9,8},{10,11... | collective-permute-start | bytes 393224 | tf_op jit(solution)/shard_map/ppermute | solution.py:35
  23.3 5.9 %collective-permute-start.12 = (bf16[64,512]{1,0:T(8,128)(2,1)S(1)}, bf16[64,512]{1,0:T(8,128)(2,1)S(1)}, u32[]{:S(2)}, u32[]{:S(2)}) collective-permute-start(bf16[64,512]{1,0:T(8,128)(2,1)S(1)} %get-tuple-element.100.refs_2_), channel_id=1, source_target_pairs={{0,6},{1,7},{2,4},{3,5},{4,2},{5,3},{6,0},{7,1},{8,14},{9,15},{10,... | collective-permute-start | bytes 196616 | tf_op jit(solution)/shard_map/ppermute | solution.py:35
  24.4 4.8 %collective-permute-start.11 = (bf16[64,512]{1,0:T(8,128)(2,1)S(1)}, bf16[64,512]{1,0:T(8,128)(2,1)S(1)}, u32[]{:S(2)}, u32[]{:S(2)}) collective-permute-start(bf16[64,512]{1,0:T(8,128)(2,1)S(1)} %get-tuple-element.100.refs_2_), channel_id=1, source_target_pairs={{0,5},{1,4},{2,7},{3,6},{4,1},{5,0},{6,3},{7,2},{8,13},{9,12},{10,... | collective-permute-start | bytes 196616 | tf_op jit(solution)/shard_map/ppermute | solution.py:35
  24.4 5.8 %collective-permute-start.13 = (bf16[64,512]{1,0:T(8,128)(2,1)S(1)}, bf16[64,512]{1,0:T(8,128)(2,1)S(1)}, u32[]{:S(2)}, u32[]{:S(2)}) collective-permute-start(bf16[64,512]{1,0:T(8,128)(2,1)S(1)} %get-tuple-element.100.refs_2_), channel_id=1, source_target_pairs={{0,3},{1,2},{2,1},{3,0},{4,7},{5,6},{6,5},{7,4},{8,11},{9,10},{10,... | collective-permute-start | bytes 196616 | tf_op jit(solution)/shard_map/ppermute | solution.py:35
  32.2 5.8 %collective-permute-start.16 = (bf16[64,512]{1,0:T(8,128)(2,1)S(1)}, bf16[64,512]{1,0:T(8,128)(2,1)S(1)}, u32[]{:S(2)}, u32[]{:S(2)}) collective-permute-start(bf16[64,512]{1,0:T(8,128)(2,1)S(1)} %get-tuple-element.72), channel_id=1, source_target_pairs={{0,6},{1,7},{2,4},{3,5},{4,2},{5,3},{6,0},{7,1},{8,14},{9,15},{10,... | collective-permute-start | bytes 196616 | tf_op jit(solution)/shard_map/ppermute | solution.py:35
  32.8 5.5 %collective-permute-start.17 = (bf16[64,512]{1,0:T(8,128)(2,1)S(1)}, bf16[64,512]{1,0:T(8,128)(2,1)S(1)}, u32[]{:S(2)}, u32[]{:S(2)}) collective-permute-start(bf16[64,512]{1,0:T(8,128)(2,1)S(1)} %get-tuple-element.73), channel_id=1, source_target_pairs={{0,5},{1,4},{2,7},{3,6},{4,1},{5,0},{6,3},{7,2},{8,13},{9,12},{10,... | collective-permute-start | bytes 196616 | tf_op jit(solution)/shard_map/ppermute | solution.py:35
  38.3 6.2 %collective-permute-start.18 = (bf16[64,512]{1,0:T(8,128)(2,1)S(1)}, bf16[64,512]{1,0:T(8,128)(2,1)S(1)}, u32[]{:S(2)}, u32[]{:S(2)}) collective-permute-start(bf16[64,512]{1,0:T(8,128)(2,1)S(1)} %fusion), channel_id=1, source_target_pairs={{0,8},{1,9},{2,10},{3,11},{4,12},{5,13},{6,14},{7,15},{8,0},{9,1},... | collective-permute-start | bytes 196616 | tf_op jit(solution)/shard_map/ppermute | solution.py:35
  44.6 5.3 %collective-permute-start.20 = (bf16[64,512]{1,0:T(8,128)(2,1)S(1)}, bf16[64,512]{1,0:T(8,128)(2,1)S(1)}, u32[]{:S(2)}, u32[]{:S(2)}) collective-permute-start(bf16[64,512]{1,0:T(8,128)(2,1)S(1)} %get-tuple-element.98.refs_2_), channel_id=1, source_target_pairs={{0,6},{1,7},{2,4},{3,5},{4,2},{5,3},{6,0},{7,1},{8,14},{9,15},{10,... | collective-permute-start | bytes 196616 | tf_op jit(solution)/shard_map/ppermute | solution.py:35
  44.7 5.1 %collective-permute-start.19 = (bf16[64,512]{1,0:T(8,128)(2,1)S(1)}, bf16[64,512]{1,0:T(8,128)(2,1)S(1)}, u32[]{:S(2)}, u32[]{:S(2)}) collective-permute-start(bf16[64,512]{1,0:T(8,128)(2,1)S(1)} %get-tuple-element.98.refs_2_), channel_id=1, source_target_pairs={{0,5},{1,4},{2,7},{3,6},{4,1},{5,0},{6,3},{7,2},{8,13},{9,12},{10,... | collective-permute-start | bytes 196616 | tf_op jit(solution)/shard_map/ppermute | solution.py:35
  46.3 4.5 %collective-permute-start.21 = (bf16[64,512]{1,0:T(8,128)(2,1)S(1)}, bf16[64,512]{1,0:T(8,128)(2,1)S(1)}, u32[]{:S(2)}, u32[]{:S(2)}) collective-permute-start(bf16[64,512]{1,0:T(8,128)(2,1)S(1)} %get-tuple-element.98.refs_2_), channel_id=1, source_target_pairs={{0,3},{1,2},{2,1},{3,0},{4,7},{5,6},{6,5},{7,4},{8,11},{9,10},{10,... | collective-permute-start | bytes 196616 | tf_op jit(solution)/shard_map/ppermute | solution.py:35
  52.9 5.8 %collective-permute-start.23 = (bf16[64,512]{1,0:T(8,128)(2,1)S(1)}, bf16[64,512]{1,0:T(8,128)(2,1)S(1)}, u32[]{:S(2)}, u32[]{:S(2)}) collective-permute-start(bf16[64,512]{1,0:T(8,128)(2,1)S(1)} %get-tuple-element.81), channel_id=1, source_target_pairs={{0,6},{1,7},{2,4},{3,5},{4,2},{5,3},{6,0},{7,1},{8,14},{9,15},{10,... | collective-permute-start | bytes 196616 | tf_op jit(solution)/shard_map/ppermute | solution.py:35
  54.3 4.7 %collective-permute-start.24 = (bf16[64,512]{1,0:T(8,128)(2,1)S(1)}, bf16[64,512]{1,0:T(8,128)(2,1)S(1)}, u32[]{:S(2)}, u32[]{:S(2)}) collective-permute-start(bf16[64,512]{1,0:T(8,128)(2,1)S(1)} %get-tuple-element.82), channel_id=1, source_target_pairs={{0,5},{1,4},{2,7},{3,6},{4,1},{5,0},{6,3},{7,2},{8,13},{9,12},{10,... | collective-permute-start | bytes 196616 | tf_op jit(solution)/shard_map/ppermute | solution.py:35
  59.0 6.5 %collective-permute-start.25 = (bf16[64,512]{1,0:T(8,128)(2,1)S(1)}, bf16[64,512]{1,0:T(8,128)(2,1)S(1)}, u32[]{:S(2)}, u32[]{:S(2)}) collective-permute-start(bf16[64,512]{1,0:T(8,128)(2,1)S(1)} %fusion.1), channel_id=1, source_target_pairs={{0,8},{1,9},{2,10},{3,11},{4,12},{5,13},{6,14},{7,15},{8,0},{9,1},... | collective-permute-start | bytes 196616 | tf_op jit(solution)/shard_map/ppermute | solution.py:35
  65.6 5.3 %collective-permute-start.27 = (bf16[64,512]{1,0:T(8,128)(2,1)S(1)}, bf16[64,512]{1,0:T(8,128)(2,1)S(1)}, u32[]{:S(2)}, u32[]{:S(2)}) collective-permute-start(bf16[64,512]{1,0:T(8,128)(2,1)S(1)} %get-tuple-element.87.refs_2_), channel_id=1, source_target_pairs={{0,6},{1,7},{2,4},{3,5},{4,2},{5,3},{6,0},{7,1},{8,14},{9,15},{10,... | collective-permute-start | bytes 196616 | tf_op jit(solution)/shard_map/ppermute | solution.py:35
  65.8 5.1 %collective-permute-start.26 = (bf16[64,512]{1,0:T(8,128)(2,1)S(1)}, bf16[64,512]{1,0:T(8,128)(2,1)S(1)}, u32[]{:S(2)}, u32[]{:S(2)}) collective-permute-start(bf16[64,512]{1,0:T(8,128)(2,1)S(1)} %get-tuple-element.87.refs_2_), channel_id=1, source_target_pairs={{0,5},{1,4},{2,7},{3,6},{4,1},{5,0},{6,3},{7,2},{8,13},{9,12},{10,... | collective-permute-start | bytes 196616 | tf_op jit(solution)/shard_map/ppermute | solution.py:35
  67.1 4.8 %collective-permute-start.29 = (bf16[64,512]{1,0:T(8,128)(2,1)S(1)}, bf16[64,512]{1,0:T(8,128)(2,1)S(1)}, u32[]{:S(2)}, u32[]{:S(2)}) collective-permute-start(bf16[64,512]{1,0:T(8,128)(2,1)S(1)} %get-tuple-element.87.refs_2_), channel_id=1, source_target_pairs={{0,3},{1,2},{2,1},{3,0},{4,7},{5,6},{6,5},{7,4},{8,11},{9,10},{10,... | collective-permute-start | bytes 196616 | tf_op jit(solution)/shard_map/ppermute | solution.py:35
  (12 other events, 43.2 us)

commit v8 on v7

--- a/solution.py
+++ b/solution.py
@@ -9,7 +9,8 @@
 
 ITERS = 3
 STEP = 0.4
-SUM_LAST, VALUE_LAST = 2, 1
+EARLY = (1, 3)
+SUM_LAST, VALUE_LAST = 2, 2
 CORES = 2
 QUAD = 4
 UNIT = CORES * QUAD
@@ -182,28 +183,41 @@
     return total
 
 
-def near_rows_kernel(*refs):
-    a, pieces, images = refs[0:2], refs[2 : 1 + QUAD], refs[1 + QUAD :]
+def near_rows_kernel(first, *refs):
+    a, pieces, sides = refs[0:2], refs[2 : 1 + QUAD], refs[1 + QUAD : 3 + QUAD]
+    duals = [s.at[0] for s in sides] if first else refs[3 + QUAD : 5 + QUAD]
+    bases = refs[-2:]
     me = place()[1]
     for i in range(2):
-        images[i][...] = row_product(a[i], pieces, [k for k in range(QUAD) if k != VALUE_LAST], me)
-
-
-def turn_kernel(first, *refs):
-    a, images, last, sides = refs[0:2], refs[2:4], refs[4], refs[5:7]
-    at = 7 if first else 9
-    duals = [s.at[0] for s in sides] if first else refs[7:9]
-    stepped, lows, pieces = refs[at : at + 2], refs[at + 2 : at + 4], refs[at + 4 :]
+        image = row_product(a[i], pieces, [k for k in range(QUAD) if k != VALUE_LAST], me)
+        bases[i][...] = duals[i][...] + STEP * (sides[i][1] - image)
+
+
+def stepped_dual(a, base, last, me):
+    image = row_product(a, (last,), (VALUE_LAST,), me)
+    return jnp.maximum(base[...] - STEP * image, 0.0)
+
+
+def turn_kernel(members, *refs):
+    a, bases, last = refs[0:2], refs[2:4], refs[4]
+    stepped, lows, pieces = refs[5:7], refs[7:9], refs[9:]
     me = place()[1]
     low = []
     for i in range(2):
-        image = images[i][...] + row_product(a[i], (last,), (VALUE_LAST,), me)
-        new = jnp.maximum(duals[i][...] + STEP * (sides[i][1] - image), 0.0)
+        new = stepped_dual(a[i], bases[i], last, me)
         stepped[i][...] = new
         low.append(new.astype(BF16).T)
         lows[i][...] = low[i]
-    for k in range(1, QUAD):
-        pieces[k - 1][...] = column_product(low, a, me ^ k).astype(BF16)
+    for k, piece in zip(members, pieces):
+        piece[...] = column_product(low, a, me ^ k).astype(BF16)
+
+
+def more_columns_kernel(members, *refs):
+    a, lows, pieces = refs[0:2], refs[2:4], refs[4:]
+    low = [r[...] for r in lows]
+    me = place()[1]
+    for k, piece in zip(members, pieces):
+        piece[...] = column_product(low, a, me ^ k).astype(BF16)
 
 
 def own_columns_kernel(*refs):
@@ -214,9 +228,8 @@
     out[...] = total
 
 
-def finish_kernel(a, image, last, side, dual, out):
-    total = image[...] + row_product(a, (last,), (VALUE_LAST,), place()[1])
-    out[...] = jnp.maximum(dual[...] + STEP * (side[1] - total), 0.0)
+def finish_kernel(a, base, last, out):
+    out[...] = stepped_dual(a, base, last, place()[1])
 
 
 def body(
@@ -311,23 +324,37 @@
             near, mine, other = lax.optimization_barrier((around[:-1], mine, swap(other, 1)))
             around = [*near, around[-1]]
             held = (mine, other)
-        images = call(near_rows_kernel, (side, side), *a, *around[:-1])
+        bases = call(
+            functools.partial(near_rows_kernel, iteration == 0),
+            (side, side),
+            *a,
+            *around[:-1],
+            *sides,
+            *duals,
+        )
         if iteration < ITERS - 1:
+            early = [k for k in range(1, QUAD) if k in EARLY]
+            late = [k for k in range(1, QUAD) if k not in EARLY]
             out = call(
-                functools.partial(turn_kernel, iteration == 0),
+                functools.partial(turn_kernel, early),
                 (side,) * 2
                 + (jax.ShapeDtypeStruct((half, rows), BF16),) * 2
-                + (piece,) * (QUAD - 1),
+                + (piece,) * len(early),
                 *a,
-                *images,
+                *bases,
                 around[-1],
-                *sides,
-                *duals,
             )
-            duals, lows, pieces = out[0:2], out[2:4], out[4:]
+            duals, lows = out[0:2], out[2:4]
+            made = dict(zip(early, out[4:]))
+            if late:
+                out = call(
+                    functools.partial(more_columns_kernel, late), (piece,) * len(late), *a, *lows
+                )
+                made.update(zip(late, out))
+            pieces = [made[k] for k in range(1, QUAD)]
 
     mine, other = [
-        call(finish_kernel, side, a[i], images[i], around[-1], sides[i], duals[i])
+        call(finish_kernel, side, a[i], bases[i], around[-1])
         for i in range(2)
     ]
     first, second, _ = lax.optimization_barrier((*held, other))

time: 74.6 us -> 74.2 us (level)
  waiting for transfers between devices: 32 us -> 30.2 us
  starting transfers between devices: 30 us -> 31 us
    ppermute x31, waiting for transfers between devices: 32 us -> 30.2 us  [swap(): lax.ppermute(x, 'row', [(i, i ^ mask) for i in range(lax.axis_size('row'))])]
    ppermute x31, starting transfers between devices: 30 us -> 31 us  [swap(): lax.ppermute(x, 'row', [(i, i ^ mask) for i in range(lax.axis_size('row'))])]
    pallas_call x15 -> x17, Pallas kernels: 8.37 us -> 8.76 us  [call(): pl.pallas_call(kernel, out_shape=out_shape, in_specs=[VMEM] * len(operand...]
  transfers between devices with their start and end apart: 31 -> 31, of which waited for: 14 -> 18; matrix products, arithmetic and copies ran while one was open for 0% -> 0% of each run, Pallas kernels for 6% -> 7%
where the time goes in v8:
time: 74.2 us; the launch traced here: 74 us
  starting transfers between devices  31 us (42%)
  waiting for transfers between devices  30.2 us (41%)
  Pallas kernels  10.8 us (15%)
  other arithmetic  1.01 us (1%)
  between operations  0.92 us (1%)
    ppermute x31, starting transfers between devices, swap(): lax.ppermute(x, 'row', [(i, i ^ mask) for i in range(lax.axis_size('row'))])  31 us
    ppermute x31, waiting for transfers between devices, swap(): lax.ppermute(x, 'row', [(i, i ^ mask) for i in range(lax.axis_size('row'))])  30.2 us
    pallas_call x17, Pallas kernels, call(): pl.pallas_call(kernel, out_shape=out_shape, in_specs=[VMEM] * len(operand...  8.76 us
    pallas_call x1, Pallas kernels, dense(): pl.pallas_call(functools.partial(dense_kernel, span, chunks), out_shape=j...  2.06 us
  transfers between devices with their start and end apart: 31, of which 18 were waited for; matrix products, arithmetic and copies ran while one was open for 0% of the time, Pallas kernels for 7%

profile of v8, /device:TPU:0, one launch (start us, length us, event | category | flops | bytes accessed | tf_op | source)
XLA Modules:
  0.0 74.0 jit_solution(12744433914063880326)
XLA Ops:
  1.3 2.1 %shard_map.95.a_ref.refs_0_.a = bf16[2,4,256,512]{3,2,1,0:T(8,128)(2,1)S(1)} custom-call(s32[64]{0:T(128)S(1)} %multiply_add_fusion.at_hbm, bf16[64,128,128]{2,1,0:T(8,128)(2,1)} %tile_hbm.1), custom_call_target="tpu_custom_call" | custom-call | tf_op jit(solution)/shard_map/pallas_call | solution.py:85
  5.5 3.9 %collective-permute-start.1 = (f32[144,128]{1,0:T(8,128)S(1)}, f32[144,128]{1,0:T(8,128)S(1)}, u32[]{:S(2)}, u32[]{:S(2)}) collective-permute-start(f32[144,128]{1,0:T(8,128)S(1)} %pad_maximum_fusion), channel_id=1, source_target_pairs={{0,8},{1,9},{2,10},{3,11},{4,12},{5,13},{6,14},{7,15},{8,0},{9,1},... | collective-permute-start | bytes 221192 | tf_op jit(solution)/shard_map/ppermute | solution.py:36
  9.4 1.2 %collective-permute-start.4 = (bf16[64,512]{1,0:T(8,128)(2,1)S(1)}, bf16[64,512]{1,0:T(8,128)(2,1)S(1)}, u32[]{:S(2)}, u32[]{:S(2)}) collective-permute-start(bf16[64,512]{1,0:T(8,128)(2,1)S(1)} %add_convert_fusion.2), channel_id=1, source_target_pairs={{0,3},{1,2},{2,1},{3,0},{4,7},{5,6},{6,5},{7,4},{8,11},{9,10},{10,... | collective-permute-start | bytes 196616 | tf_op jit(solution)/shard_map/ppermute | solution.py:36
  10.6 1.6 %collective-permute-start.6 = (bf16[64,512]{1,0:T(8,128)(2,1)S(1)}, bf16[64,512]{1,0:T(8,128)(2,1)S(1)}, u32[]{:S(2)}, u32[]{:S(2)}) collective-permute-start(bf16[64,512]{1,0:T(8,128)(2,1)S(1)} %add_convert_fusion.1), channel_id=1, source_target_pairs={{0,6},{1,7},{2,4},{3,5},{4,2},{5,3},{6,0},{7,1},{8,14},{9,15},{10,... | collective-permute-start | bytes 196616 | tf_op jit(solution)/shard_map/ppermute | solution.py:36
  12.6 1.1 %collective-permute-done.1.refs_0_ = f32[144,128]{1,0:T(8,128)S(1)} collective-permute-done((f32[144,128]{1,0:T(8,128)S(1)}, f32[144,128]{1,0:T(8,128)S(1)}, u32[]{:S(2)}, u32[]{:S(2)}) %collective-permute-start.1) | collective-permute-done | bytes 73760 | tf_op jit(solution)/shard_map/ppermute | solution.py:36
  13.7 2.4 %collective-permute-done.6 = bf16[64,512]{1,0:T(8,128)(2,1)S(1)} collective-permute-done((bf16[64,512]{1,0:T(8,128)(2,1)S(1)}, bf16[64,512]{1,0:T(8,128)(2,1)S(1)}, u32[]{:S(2)}, u32[]{:S(2)}) %collective-permute-start.6) | collective-permute-done | bytes 65568 | tf_op jit(solution)/shard_map/ppermute | solution.py:36
  16.6 1.0 %collective-permute-start.9 = (bf16[64,512]{1,0:T(8,128)(2,1)S(1)}, bf16[64,512]{1,0:T(8,128)(2,1)S(1)}, u32[]{:S(2)}, u32[]{:S(2)}) collective-permute-start(bf16[64,512]{1,0:T(8,128)(2,1)S(1)} %get-tuple-element.98), channel_id=1, source_target_pairs={{0,8},{1,9},{2,10},{3,11},{4,12},{5,13},{6,14},{7,15},{8,0},{9,1},... | collective-permute-start | bytes 196616 | tf_op jit(solution)/shard_map/ppermute | solution.py:36
  18.1 5.2 %collective-permute-done.9 = bf16[64,512]{1,0:T(8,128)(2,1)S(1)} collective-permute-done((bf16[64,512]{1,0:T(8,128)(2,1)S(1)}, bf16[64,512]{1,0:T(8,128)(2,1)S(1)}, u32[]{:S(2)}, u32[]{:S(2)}) %collective-permute-start.9) | collective-permute-done | bytes 65568 | tf_op jit(solution)/shard_map/ppermute | solution.py:36
  23.3 1.1 %collective-permute-start.12 = (bf16[64,512]{1,0:T(8,128)(2,1)S(1)}, bf16[64,512]{1,0:T(8,128)(2,1)S(1)}, u32[]{:S(2)}, u32[]{:S(2)}) collective-permute-start(bf16[64,512]{1,0:T(8,128)(2,1)S(1)} %get-tuple-element.96.refs_2_), channel_id=1, source_target_pairs={{0,6},{1,7},{2,4},{3,5},{4,2},{5,3},{6,0},{7,1},{8,14},{9,15},{10,... | collective-permute-start | bytes 196616 | tf_op jit(solution)/shard_map/ppermute | solution.py:36
  24.4 2.2 %collective-permute-start.14 = (bf16[64,512]{1,0:T(8,128)(2,1)S(1)}, bf16[64,512]{1,0:T(8,128)(2,1)S(1)}, u32[]{:S(2)}, u32[]{:S(2)}) collective-permute-start(bf16[64,512]{1,0:T(8,128)(2,1)S(1)} %get-tuple-element.96.refs_2_), channel_id=1, source_target_pairs={{0,5},{1,4},{2,7},{3,6},{4,1},{5,0},{6,3},{7,2},{8,13},{9,12},{10,... | collective-permute-start | bytes 196616 | tf_op jit(solution)/shard_map/ppermute | solution.py:36
  26.6 2.1 %collective-permute-done.12.refs_4_ = bf16[64,512]{1,0:T(8,128)(2,1)S(1)} collective-permute-done((bf16[64,512]{1,0:T(8,128)(2,1)S(1)}, bf16[64,512]{1,0:T(8,128)(2,1)S(1)}, u32[]{:S(2)}, u32[]{:S(2)}) %collective-permute-start.12) | collective-permute-done | bytes 65568 | tf_op jit(solution)/shard_map/ppermute | solution.py:36
  28.9 1.0 %shard_map.99 = (f32[256,64]{1,0:T(8,128)S(1)}, f32[256,64]{1,0:T(8,128)S(1)}) custom-call(bf16[2,4,256,512]{3,2,1,0:T(8,128)(2,1)S(1)} %shard_map.95.a_ref.refs_0_.a, bf16[2,4,256,512]{3,2,1,0:T(8,128)(2,1)S(1)} %collective-permute-done.10.refs_1_.a, bf16[64,512]{1,0:T(8,128)(2,1)S(1)} %get-tuple-element.96.refs_2_, ...), custom_call_target="tpu_custom_call" | custom-call | tf_op jit(solution)/shard_map/pallas_call | solution.py:255
  31.4 1.7 %collective-permute-start.16 = (bf16[64,512]{1,0:T(8,128)(2,1)S(1)}, bf16[64,512]{1,0:T(8,128)(2,1)S(1)}, u32[]{:S(2)}, u32[]{:S(2)}) collective-permute-start(bf16[64,512]{1,0:T(8,128)(2,1)S(1)} %get-tuple-element.70), channel_id=1, source_target_pairs={{0,6},{1,7},{2,4},{3,5},{4,2},{5,3},{6,0},{7,1},{8,14},{9,15},{10,... | collective-permute-start | bytes 196616 | tf_op jit(solution)/shard_map/ppermute | solution.py:36
  35.0 2.0 %collective-permute-done.16.refs_5_ = bf16[64,512]{1,0:T(8,128)(2,1)S(1)} collective-permute-done((bf16[64,512]{1,0:T(8,128)(2,1)S(1)}, bf16[64,512]{1,0:T(8,128)(2,1)S(1)}, u32[]{:S(2)}, u32[]{:S(2)}) %collective-permute-start.16) | collective-permute-done | bytes 65568 | tf_op jit(solution)/shard_map/ppermute | solution.py:36
  37.3 2.6 %collective-permute-start.18 = (bf16[64,512]{1,0:T(8,128)(2,1)S(1)}, bf16[64,512]{1,0:T(8,128)(2,1)S(1)}, u32[]{:S(2)}, u32[]{:S(2)}) collective-permute-start(bf16[64,512]{1,0:T(8,128)(2,1)S(1)} %fusion), channel_id=1, source_target_pairs={{0,8},{1,9},{2,10},{3,11},{4,12},{5,13},{6,14},{7,15},{8,0},{9,1},... | collective-permute-start | bytes 196616 | tf_op jit(solution)/shard_map/ppermute | solution.py:36
  39.9 4.3 %collective-permute-done.18 = bf16[64,512]{1,0:T(8,128)(2,1)S(1)} collective-permute-done((bf16[64,512]{1,0:T(8,128)(2,1)S(1)}, bf16[64,512]{1,0:T(8,128)(2,1)S(1)}, u32[]{:S(2)}, u32[]{:S(2)}) %collective-permute-start.18) | collective-permute-done | bytes 65568 | tf_op jit(solution)/shard_map/ppermute | solution.py:36
  45.0 2.5 %collective-permute-start.21 = (bf16[64,512]{1,0:T(8,128)(2,1)S(1)}, bf16[64,512]{1,0:T(8,128)(2,1)S(1)}, u32[]{:S(2)}, u32[]{:S(2)}) collective-permute-start(bf16[64,512]{1,0:T(8,128)(2,1)S(1)} %get-tuple-element.94.refs_2_), channel_id=1, source_target_pairs={{0,5},{1,4},{2,7},{3,6},{4,1},{5,0},{6,3},{7,2},{8,13},{9,12},{10,... | collective-permute-start | bytes 196616 | tf_op jit(solution)/shard_map/ppermute | solution.py:36
  47.5 2.1 %collective-permute-done.20.refs_4_ = bf16[64,512]{1,0:T(8,128)(2,1)S(1)} collective-permute-done((bf16[64,512]{1,0:T(8,128)(2,1)S(1)}, bf16[64,512]{1,0:T(8,128)(2,1)S(1)}, u32[]{:S(2)}, u32[]{:S(2)}) %collective-permute-start.20) | collective-permute-done | bytes 65568 | tf_op jit(solution)/shard_map/ppermute | solution.py:36
  52.3 1.8 %collective-permute-start.23 = (bf16[64,512]{1,0:T(8,128)(2,1)S(1)}, bf16[64,512]{1,0:T(8,128)(2,1)S(1)}, u32[]{:S(2)}, u32[]{:S(2)}) collective-permute-start(bf16[64,512]{1,0:T(8,128)(2,1)S(1)} %get-tuple-element.78), channel_id=1, source_target_pairs={{0,6},{1,7},{2,4},{3,5},{4,2},{5,3},{6,0},{7,1},{8,14},{9,15},{10,... | collective-permute-start | bytes 196616 | tf_op jit(solution)/shard_map/ppermute | solution.py:36
  55.9 1.9 %collective-permute-done.23.refs_5_ = bf16[64,512]{1,0:T(8,128)(2,1)S(1)} collective-permute-done((bf16[64,512]{1,0:T(8,128)(2,1)S(1)}, bf16[64,512]{1,0:T(8,128)(2,1)S(1)}, u32[]{:S(2)}, u32[]{:S(2)}) %collective-permute-start.23) | collective-permute-done | bytes 65568 | tf_op jit(solution)/shard_map/ppermute | solution.py:36
  58.3 2.4 %collective-permute-start.25 = (bf16[64,512]{1,0:T(8,128)(2,1)S(1)}, bf16[64,512]{1,0:T(8,128)(2,1)S(1)}, u32[]{:S(2)}, u32[]{:S(2)}) collective-permute-start(bf16[64,512]{1,0:T(8,128)(2,1)S(1)} %fusion.1), channel_id=1, source_target_pairs={{0,8},{1,9},{2,10},{3,11},{4,12},{5,13},{6,14},{7,15},{8,0},{9,1},... | collective-permute-start | bytes 196616 | tf_op jit(solution)/shard_map/ppermute | solution.py:36
  60.7 4.4 %collective-permute-done.25 = bf16[64,512]{1,0:T(8,128)(2,1)S(1)} collective-permute-done((bf16[64,512]{1,0:T(8,128)(2,1)S(1)}, bf16[64,512]{1,0:T(8,128)(2,1)S(1)}, u32[]{:S(2)}, u32[]{:S(2)}) %collective-permute-start.25) | collective-permute-done | bytes 65568 | tf_op jit(solution)/shard_map/ppermute | solution.py:36
  66.0 2.5 %collective-permute-start.29 = (bf16[64,512]{1,0:T(8,128)(2,1)S(1)}, bf16[64,512]{1,0:T(8,128)(2,1)S(1)}, u32[]{:S(2)}, u32[]{:S(2)}) collective-permute-start(bf16[64,512]{1,0:T(8,128)(2,1)S(1)} %get-tuple-element.83.refs_2_), channel_id=1, source_target_pairs={{0,5},{1,4},{2,7},{3,6},{4,1},{5,0},{6,3},{7,2},{8,13},{9,12},{10,... | collective-permute-start | bytes 196616 | tf_op jit(solution)/shard_map/ppermute | solution.py:36
  68.5 1.2 %collective-permute-done.28.other = f32[64,128]{1,0:T(8,128)S(1)} collective-permute-done((f32[64,128]{1,0:T(8,128)S(1)}, f32[64,128]{1,0:T(8,128)S(1)}, u32[]{:S(2)}, u32[]{:S(2)}) %collective-permute-start.28) | collective-permute-done | bytes 32800 | tf_op jit(solution)/shard_map/ppermute | solution.py:36
  (79 shorter events, 19.2 us)
Async XLA Ops:
  4.4 4.9 %collective-permute-start.3 = (f32[64,512]{1,0:T(8,128)S(1)}, f32[64,512]{1,0:T(8,128)S(1)}, u32[]{:S(2)}, u32[]{:S(2)}) collective-permute-start(f32[64,512]{1,0:T(8,128)S(1)} %get-tuple-element.55), channel_id=1, source_target_pairs={{0,1},{1,0},{2,3},{3,2},{4,5},{5,4},{6,7},{7,6},{8,9},{9,8},{10,11... | collective-permute-start | bytes 393224 | tf_op jit(solution)/shard_map/ppermute | solution.py:36
  4.5 9.2 %collective-permute-start.2 = (f32[64,512]{1,0:T(8,128)S(1)}, f32[64,512]{1,0:T(8,128)S(1)}, u32[]{:S(2)}, u32[]{:S(2)}) collective-permute-start(f32[64,512]{1,0:T(8,128)S(1)} %get-tuple-element.52), channel_id=1, source_target_pairs={{0,1},{1,0},{2,3},{3,2},{4,5},{5,4},{6,7},{7,6},{8,9},{9,8},{10,11... | collective-permute-start | bytes 393224 | tf_op jit(solution)/shard_map/ppermute | solution.py:36
  4.9 5.6 %collective-permute-start.5 = (f32[64,512]{1,0:T(8,128)S(1)}, f32[64,512]{1,0:T(8,128)S(1)}, u32[]{:S(2)}, u32[]{:S(2)}) collective-permute-start(f32[64,512]{1,0:T(8,128)S(1)} %get-tuple-element.57), channel_id=1, source_target_pairs={{0,1},{1,0},{2,3},{3,2},{4,5},{5,4},{6,7},{7,6},{8,9},{9,8},{10,11... | collective-permute-start | bytes 393224 | tf_op jit(solution)/shard_map/ppermute | solution.py:36
  5.0 7.2 %collective-permute-start.7 = (f32[64,512]{1,0:T(8,128)S(1)}, f32[64,512]{1,0:T(8,128)S(1)}, u32[]{:S(2)}, u32[]{:S(2)}) collective-permute-start(f32[64,512]{1,0:T(8,128)S(1)} %get-tuple-element.59), channel_id=1, source_target_pairs={{0,1},{1,0},{2,3},{3,2},{4,5},{5,4},{6,7},{7,6},{8,9},{9,8},{10,11... | collective-permute-start | bytes 393224 | tf_op jit(solution)/shard_map/ppermute | solution.py:36
  5.5 8.2 %collective-permute-start.1 = (f32[144,128]{1,0:T(8,128)S(1)}, f32[144,128]{1,0:T(8,128)S(1)}, u32[]{:S(2)}, u32[]{:S(2)}) collective-permute-start(f32[144,128]{1,0:T(8,128)S(1)} %pad_maximum_fusion), channel_id=1, source_target_pairs={{0,8},{1,9},{2,10},{3,11},{4,12},{5,13},{6,14},{7,15},{8,0},{9,1},... | collective-permute-start | bytes 221192 | tf_op jit(solution)/shard_map/ppermute | solution.py:36
  9.4 4.3 %collective-permute-start.4 = (bf16[64,512]{1,0:T(8,128)(2,1)S(1)}, bf16[64,512]{1,0:T(8,128)(2,1)S(1)}, u32[]{:S(2)}, u32[]{:S(2)}) collective-permute-start(bf16[64,512]{1,0:T(8,128)(2,1)S(1)} %add_convert_fusion.2), channel_id=1, source_target_pairs={{0,3},{1,2},{2,1},{3,0},{4,7},{5,6},{6,5},{7,4},{8,11},{9,10},{10,... | collective-permute-start | bytes 196616 | tf_op jit(solution)/shard_map/ppermute | solution.py:36
  10.6 5.5 %collective-permute-start.6 = (bf16[64,512]{1,0:T(8,128)(2,1)S(1)}, bf16[64,512]{1,0:T(8,128)(2,1)S(1)}, u32[]{:S(2)}, u32[]{:S(2)}) collective-permute-start(bf16[64,512]{1,0:T(8,128)(2,1)S(1)} %add_convert_fusion.1), channel_id=1, source_target_pairs={{0,6},{1,7},{2,4},{3,5},{4,2},{5,3},{6,0},{7,1},{8,14},{9,15},{10,... | collective-permute-start | bytes 196616 | tf_op jit(solution)/shard_map/ppermute | solution.py:36
  16.4 12.5 %collective-permute-start.10 = (bf16[2,4,256,512]{3,2,1,0:T(8,128)(2,1)S(1)}, bf16[2,4,256,512]{3,2,1,0:T(8,128)(2,1)S(1)}, u32[]{:S(2)}, u32[]{:S(2)}) collective-permute-start(bf16[2,4,256,512]{3,2,1,0:T(8,128)(2,1)S(1)} %shard_map.95.a_ref.refs_0_.a), channel_id=1, source_target_pairs={{0,1},{1,0},{2,3},{3,2},{4,5},{5,4},{6,7},{7,6},{8,9},{9,8},{10,11... | collective-permute-start | bytes 6291464 | tf_op jit(solution)/shard_map/ppermute | solution.py:36
  16.6 6.7 %collective-permute-start.9 = (bf16[64,512]{1,0:T(8,128)(2,1)S(1)}, bf16[64,512]{1,0:T(8,128)(2,1)S(1)}, u32[]{:S(2)}, u32[]{:S(2)}) collective-permute-start(bf16[64,512]{1,0:T(8,128)(2,1)S(1)} %get-tuple-element.98), channel_id=1, source_target_pairs={{0,8},{1,9},{2,10},{3,11},{4,12},{5,13},{6,14},{7,15},{8,0},{9,1},... | collective-permute-start | bytes 196616 | tf_op jit(solution)/shard_map/ppermute | solution.py:36
  17.9 11.0 %collective-permute-start.13 = (f32[2,256,64]{2,1,0:T(8,128)S(1)}, f32[2,256,64]{2,1,0:T(8,128)S(1)}, u32[]{:S(2)}, u32[]{:S(2)}) collective-permute-start(f32[2,256,64]{2,1,0:T(8,128)S(1)} %get-tuple-element.64), channel_id=1, source_target_pairs={{0,1},{1,0},{2,3},{3,2},{4,5},{5,4},{6,7},{7,6},{8,9},{9,8},{10,11... | collective-permute-start | bytes 393224 | tf_op jit(solution)/shard_map/ppermute | solution.py:36
  23.3 5.3 %collective-permute-start.12 = (bf16[64,512]{1,0:T(8,128)(2,1)S(1)}, bf16[64,512]{1,0:T(8,128)(2,1)S(1)}, u32[]{:S(2)}, u32[]{:S(2)}) collective-permute-start(bf16[64,512]{1,0:T(8,128)(2,1)S(1)} %get-tuple-element.96.refs_2_), channel_id=1, source_target_pairs={{0,6},{1,7},{2,4},{3,5},{4,2},{5,3},{6,0},{7,1},{8,14},{9,15},{10,... | collective-permute-start | bytes 196616 | tf_op jit(solution)/shard_map/ppermute | solution.py:36
  24.4 4.5 %collective-permute-start.11 = (bf16[64,512]{1,0:T(8,128)(2,1)S(1)}, bf16[64,512]{1,0:T(8,128)(2,1)S(1)}, u32[]{:S(2)}, u32[]{:S(2)}) collective-permute-start(bf16[64,512]{1,0:T(8,128)(2,1)S(1)} %get-tuple-element.96.refs_2_), channel_id=1, source_target_pairs={{0,3},{1,2},{2,1},{3,0},{4,7},{5,6},{6,5},{7,4},{8,11},{9,10},{10,... | collective-permute-start | bytes 196616 | tf_op jit(solution)/shard_map/ppermute | solution.py:36
  24.4 5.5 %collective-permute-start.14 = (bf16[64,512]{1,0:T(8,128)(2,1)S(1)}, bf16[64,512]{1,0:T(8,128)(2,1)S(1)}, u32[]{:S(2)}, u32[]{:S(2)}) collective-permute-start(bf16[64,512]{1,0:T(8,128)(2,1)S(1)} %get-tuple-element.96.refs_2_), channel_id=1, source_target_pairs={{0,5},{1,4},{2,7},{3,6},{4,1},{5,0},{6,3},{7,2},{8,13},{9,12},{10,... | collective-permute-start | bytes 196616 | tf_op jit(solution)/shard_map/ppermute | solution.py:36
  30.8 4.2 %collective-permute-start.15 = (bf16[64,512]{1,0:T(8,128)(2,1)S(1)}, bf16[64,512]{1,0:T(8,128)(2,1)S(1)}, u32[]{:S(2)}, u32[]{:S(2)}) collective-permute-start(bf16[64,512]{1,0:T(8,128)(2,1)S(1)} %get-tuple-element.69), channel_id=1, source_target_pairs={{0,3},{1,2},{2,1},{3,0},{4,7},{5,6},{6,5},{7,4},{8,11},{9,10},{10,... | collective-permute-start | bytes 196616 | tf_op jit(solution)/shard_map/ppermute | solution.py:36
  31.4 5.5 %collective-permute-start.16 = (bf16[64,512]{1,0:T(8,128)(2,1)S(1)}, bf16[64,512]{1,0:T(8,128)(2,1)S(1)}, u32[]{:S(2)}, u32[]{:S(2)}) collective-permute-start(bf16[64,512]{1,0:T(8,128)(2,1)S(1)} %get-tuple-element.70), channel_id=1, source_target_pairs={{0,6},{1,7},{2,4},{3,5},{4,2},{5,3},{6,0},{7,1},{8,14},{9,15},{10,... | collective-permute-start | bytes 196616 | tf_op jit(solution)/shard_map/ppermute | solution.py:36
  37.3 6.8 %collective-permute-start.18 = (bf16[64,512]{1,0:T(8,128)(2,1)S(1)}, bf16[64,512]{1,0:T(8,128)(2,1)S(1)}, u32[]{:S(2)}, u32[]{:S(2)}) collective-permute-start(bf16[64,512]{1,0:T(8,128)(2,1)S(1)} %fusion), channel_id=1, source_target_pairs={{0,8},{1,9},{2,10},{3,11},{4,12},{5,13},{6,14},{7,15},{8,0},{9,1},... | collective-permute-start | bytes 196616 | tf_op jit(solution)/shard_map/ppermute | solution.py:36
  44.2 5.3 %collective-permute-start.20 = (bf16[64,512]{1,0:T(8,128)(2,1)S(1)}, bf16[64,512]{1,0:T(8,128)(2,1)S(1)}, u32[]{:S(2)}, u32[]{:S(2)}) collective-permute-start(bf16[64,512]{1,0:T(8,128)(2,1)S(1)} %get-tuple-element.94.refs_2_), channel_id=1, source_target_pairs={{0,6},{1,7},{2,4},{3,5},{4,2},{5,3},{6,0},{7,1},{8,14},{9,15},{10,... | collective-permute-start | bytes 196616 | tf_op jit(solution)/shard_map/ppermute | solution.py:36
  45.0 4.9 %collective-permute-start.19 = (bf16[64,512]{1,0:T(8,128)(2,1)S(1)}, bf16[64,512]{1,0:T(8,128)(2,1)S(1)}, u32[]{:S(2)}, u32[]{:S(2)}) collective-permute-start(bf16[64,512]{1,0:T(8,128)(2,1)S(1)} %get-tuple-element.94.refs_2_), channel_id=1, source_target_pairs={{0,3},{1,2},{2,1},{3,0},{4,7},{5,6},{6,5},{7,4},{8,11},{9,10},{10,... | collective-permute-start | bytes 196616 | tf_op jit(solution)/shard_map/ppermute | solution.py:36
  45.0 5.8 %collective-permute-start.21 = (bf16[64,512]{1,0:T(8,128)(2,1)S(1)}, bf16[64,512]{1,0:T(8,128)(2,1)S(1)}, u32[]{:S(2)}, u32[]{:S(2)}) collective-permute-start(bf16[64,512]{1,0:T(8,128)(2,1)S(1)} %get-tuple-element.94.refs_2_), channel_id=1, source_target_pairs={{0,5},{1,4},{2,7},{3,6},{4,1},{5,0},{6,3},{7,2},{8,13},{9,12},{10,... | collective-permute-start | bytes 196616 | tf_op jit(solution)/shard_map/ppermute | solution.py:36
  52.3 5.5 %collective-permute-start.23 = (bf16[64,512]{1,0:T(8,128)(2,1)S(1)}, bf16[64,512]{1,0:T(8,128)(2,1)S(1)}, u32[]{:S(2)}, u32[]{:S(2)}) collective-permute-start(bf16[64,512]{1,0:T(8,128)(2,1)S(1)} %get-tuple-element.78), channel_id=1, source_target_pairs={{0,6},{1,7},{2,4},{3,5},{4,2},{5,3},{6,0},{7,1},{8,14},{9,15},{10,... | collective-permute-start | bytes 196616 | tf_op jit(solution)/shard_map/ppermute | solution.py:36
  58.3 6.8 %collective-permute-start.25 = (bf16[64,512]{1,0:T(8,128)(2,1)S(1)}, bf16[64,512]{1,0:T(8,128)(2,1)S(1)}, u32[]{:S(2)}, u32[]{:S(2)}) collective-permute-start(bf16[64,512]{1,0:T(8,128)(2,1)S(1)} %fusion.1), channel_id=1, source_target_pairs={{0,8},{1,9},{2,10},{3,11},{4,12},{5,13},{6,14},{7,15},{8,0},{9,1},... | collective-permute-start | bytes 196616 | tf_op jit(solution)/shard_map/ppermute | solution.py:36
  65.2 5.3 %collective-permute-start.27 = (bf16[64,512]{1,0:T(8,128)(2,1)S(1)}, bf16[64,512]{1,0:T(8,128)(2,1)S(1)}, u32[]{:S(2)}, u32[]{:S(2)}) collective-permute-start(bf16[64,512]{1,0:T(8,128)(2,1)S(1)} %get-tuple-element.83.refs_2_), channel_id=1, source_target_pairs={{0,6},{1,7},{2,4},{3,5},{4,2},{5,3},{6,0},{7,1},{8,14},{9,15},{10,... | collective-permute-start | bytes 196616 | tf_op jit(solution)/shard_map/ppermute | solution.py:36
  65.7 4.8 %collective-permute-start.26 = (bf16[64,512]{1,0:T(8,128)(2,1)S(1)}, bf16[64,512]{1,0:T(8,128)(2,1)S(1)}, u32[]{:S(2)}, u32[]{:S(2)}) collective-permute-start(bf16[64,512]{1,0:T(8,128)(2,1)S(1)} %get-tuple-element.83.refs_2_), channel_id=1, source_target_pairs={{0,3},{1,2},{2,1},{3,0},{4,7},{5,6},{6,5},{7,4},{8,11},{9,10},{10,... | collective-permute-start | bytes 196616 | tf_op jit(solution)/shard_map/ppermute | solution.py:36
  66.0 5.5 %collective-permute-start.29 = (bf16[64,512]{1,0:T(8,128)(2,1)S(1)}, bf16[64,512]{1,0:T(8,128)(2,1)S(1)}, u32[]{:S(2)}, u32[]{:S(2)}) collective-permute-start(bf16[64,512]{1,0:T(8,128)(2,1)S(1)} %get-tuple-element.83.refs_2_), channel_id=1, source_target_pairs={{0,5},{1,4},{2,7},{3,6},{4,1},{5,0},{6,3},{7,2},{8,13},{9,12},{10,... | collective-permute-start | bytes 196616 | tf_op jit(solution)/shard_map/ppermute | solution.py:36
  (12 other events, 42.9 us)

commit v9 on v8

--- a/solution.py
+++ b/solution.py
@@ -140,15 +140,6 @@
     out[...] = both.T
 
 
-def join_rows_kernel(mine, other, out):
-    first = group() == 0
-    out[...] = jnp.where(
-        first,
-        jnp.concatenate([mine[...], other[...]], 1),
-        jnp.concatenate([other[...], mine[...]], 1),
-    )
-
-
 def variables_kernel(mine, other, *refs):
     fars, (primal_ref, cost_ref, limit_ref) = refs[:-3], refs[-3:]
     far, _, core = place()
@@ -230,6 +221,17 @@
 
 def finish_kernel(a, base, last, out):
     out[...] = stepped_dual(a, base, last, place()[1])
+
+
+def join_rows_kernel(a, base, last, other, out):
+    first = group() == 0
+    mine = stepped_dual(a, base, last, place()[1])
+    theirs = other[...]
+    out[...] = jnp.where(
+        first,
+        jnp.concatenate([mine, theirs], 1),
+        jnp.concatenate([theirs, mine], 1),
+    )
 
 
 def body(
@@ -353,16 +355,18 @@
                 made.update(zip(late, out))
             pieces = [made[k] for k in range(1, QUAD)]
 
-    mine, other = [
-        call(finish_kernel, side, a[i], bases[i], around[-1])
-        for i in range(2)
-    ]
+    other = call(finish_kernel, side, a[1], bases[1], around[-1])
     first, second, _ = lax.optimization_barrier((*held, other))
     primal = call(
         join_variables_kernel, jax.ShapeDtypeStruct((width, scenarios), F32), first, second
     )
     dual = call(
-        join_rows_kernel, jax.ShapeDtypeStruct((rows, scenarios), F32), mine, swap(other, 1)
+        join_rows_kernel,
+        jax.ShapeDtypeStruct((rows, scenarios), F32),
+        a[0],
+        bases[0],
+        around[-1],
+        swap(other, 1),
     )
     return (primal, dual)
 

time: 74.2 us -> 74.4 us (level)
    pallas_call x17 -> x16, Pallas kernels: 8.76 us -> 8.7 us  [call(): pl.pallas_call(kernel, out_shape=out_shape, in_specs=[VMEM] * len(operand...]
where the time goes in v9:
time: 74.4 us; the launch traced here: 74.2 us
  starting transfers between devices  31 us (42%)
  waiting for transfers between devices  30.5 us (41%)
  Pallas kernels  10.8 us (15%)
  other arithmetic  1.01 us (1%)
  between operations  0.91 us (1%)
    ppermute x31, starting transfers between devices, swap(): lax.ppermute(x, 'row', [(i, i ^ mask) for i in range(lax.axis_size('row'))])  31 us
    ppermute x31, waiting for transfers between devices, swap(): lax.ppermute(x, 'row', [(i, i ^ mask) for i in range(lax.axis_size('row'))])  30.5 us
    pallas_call x16, Pallas kernels, call(): pl.pallas_call(kernel, out_shape=out_shape, in_specs=[VMEM] * len(operand...  8.7 us
    pallas_call x1, Pallas kernels, dense(): pl.pallas_call(functools.partial(dense_kernel, span, chunks), out_shape=j...  2.06 us
  transfers between devices with their start and end apart: 31, of which 18 were waited for; matrix products, arithmetic and copies ran while one was open for 0% of the time, Pallas kernels for 7%

profile of v9, /device:TPU:0, one launch (start us, length us, event | category | flops | bytes accessed | tf_op | source)
XLA Modules:
  0.0 74.2 jit_solution(17129083181226465580)
XLA Ops:
  1.3 2.1 %shard_map.95.a_ref.refs_0_.a = bf16[2,4,256,512]{3,2,1,0:T(8,128)(2,1)S(1)} custom-call(s32[64]{0:T(128)S(1)} %multiply_add_fusion.at_hbm, bf16[64,128,128]{2,1,0:T(8,128)(2,1)} %tile_hbm.1), custom_call_target="tpu_custom_call" | custom-call | tf_op jit(solution)/shard_map/pallas_call | solution.py:85
  5.5 3.9 %collective-permute-start.1 = (f32[144,128]{1,0:T(8,128)S(1)}, f32[144,128]{1,0:T(8,128)S(1)}, u32[]{:S(2)}, u32[]{:S(2)}) collective-permute-start(f32[144,128]{1,0:T(8,128)S(1)} %pad_maximum_fusion), channel_id=1, source_target_pairs={{0,8},{1,9},{2,10},{3,11},{4,12},{5,13},{6,14},{7,15},{8,0},{9,1},... | collective-permute-start | bytes 221192 | tf_op jit(solution)/shard_map/ppermute | solution.py:36
  9.4 1.2 %collective-permute-start.4 = (bf16[64,512]{1,0:T(8,128)(2,1)S(1)}, bf16[64,512]{1,0:T(8,128)(2,1)S(1)}, u32[]{:S(2)}, u32[]{:S(2)}) collective-permute-start(bf16[64,512]{1,0:T(8,128)(2,1)S(1)} %add_convert_fusion.2), channel_id=1, source_target_pairs={{0,3},{1,2},{2,1},{3,0},{4,7},{5,6},{6,5},{7,4},{8,11},{9,10},{10,... | collective-permute-start | bytes 196616 | tf_op jit(solution)/shard_map/ppermute | solution.py:36
  10.6 1.6 %collective-permute-start.6 = (bf16[64,512]{1,0:T(8,128)(2,1)S(1)}, bf16[64,512]{1,0:T(8,128)(2,1)S(1)}, u32[]{:S(2)}, u32[]{:S(2)}) collective-permute-start(bf16[64,512]{1,0:T(8,128)(2,1)S(1)} %add_convert_fusion.1), channel_id=1, source_target_pairs={{0,6},{1,7},{2,4},{3,5},{4,2},{5,3},{6,0},{7,1},{8,14},{9,15},{10,... | collective-permute-start | bytes 196616 | tf_op jit(solution)/shard_map/ppermute | solution.py:36
  12.6 1.1 %collective-permute-done.1.refs_0_ = f32[144,128]{1,0:T(8,128)S(1)} collective-permute-done((f32[144,128]{1,0:T(8,128)S(1)}, f32[144,128]{1,0:T(8,128)S(1)}, u32[]{:S(2)}, u32[]{:S(2)}) %collective-permute-start.1) | collective-permute-done | bytes 73760 | tf_op jit(solution)/shard_map/ppermute | solution.py:36
  13.7 2.4 %collective-permute-done.6 = bf16[64,512]{1,0:T(8,128)(2,1)S(1)} collective-permute-done((bf16[64,512]{1,0:T(8,128)(2,1)S(1)}, bf16[64,512]{1,0:T(8,128)(2,1)S(1)}, u32[]{:S(2)}, u32[]{:S(2)}) %collective-permute-start.6) | collective-permute-done | bytes 65568 | tf_op jit(solution)/shard_map/ppermute | solution.py:36
  16.6 1.0 %collective-permute-start.9 = (bf16[64,512]{1,0:T(8,128)(2,1)S(1)}, bf16[64,512]{1,0:T(8,128)(2,1)S(1)}, u32[]{:S(2)}, u32[]{:S(2)}) collective-permute-start(bf16[64,512]{1,0:T(8,128)(2,1)S(1)} %get-tuple-element.98), channel_id=1, source_target_pairs={{0,8},{1,9},{2,10},{3,11},{4,12},{5,13},{6,14},{7,15},{8,0},{9,1},... | collective-permute-start | bytes 196616 | tf_op jit(solution)/shard_map/ppermute | solution.py:36
  18.1 5.2 %collective-permute-done.9 = bf16[64,512]{1,0:T(8,128)(2,1)S(1)} collective-permute-done((bf16[64,512]{1,0:T(8,128)(2,1)S(1)}, bf16[64,512]{1,0:T(8,128)(2,1)S(1)}, u32[]{:S(2)}, u32[]{:S(2)}) %collective-permute-start.9) | collective-permute-done | bytes 65568 | tf_op jit(solution)/shard_map/ppermute | solution.py:36
  23.3 1.1 %collective-permute-start.12 = (bf16[64,512]{1,0:T(8,128)(2,1)S(1)}, bf16[64,512]{1,0:T(8,128)(2,1)S(1)}, u32[]{:S(2)}, u32[]{:S(2)}) collective-permute-start(bf16[64,512]{1,0:T(8,128)(2,1)S(1)} %get-tuple-element.96.refs_2_), channel_id=1, source_target_pairs={{0,6},{1,7},{2,4},{3,5},{4,2},{5,3},{6,0},{7,1},{8,14},{9,15},{10,... | collective-permute-start | bytes 196616 | tf_op jit(solution)/shard_map/ppermute | solution.py:36
  24.4 2.2 %collective-permute-start.14 = (bf16[64,512]{1,0:T(8,128)(2,1)S(1)}, bf16[64,512]{1,0:T(8,128)(2,1)S(1)}, u32[]{:S(2)}, u32[]{:S(2)}) collective-permute-start(bf16[64,512]{1,0:T(8,128)(2,1)S(1)} %get-tuple-element.96.refs_2_), channel_id=1, source_target_pairs={{0,5},{1,4},{2,7},{3,6},{4,1},{5,0},{6,3},{7,2},{8,13},{9,12},{10,... | collective-permute-start | bytes 196616 | tf_op jit(solution)/shard_map/ppermute | solution.py:36
  26.6 2.1 %collective-permute-done.12.refs_4_ = bf16[64,512]{1,0:T(8,128)(2,1)S(1)} collective-permute-done((bf16[64,512]{1,0:T(8,128)(2,1)S(1)}, bf16[64,512]{1,0:T(8,128)(2,1)S(1)}, u32[]{:S(2)}, u32[]{:S(2)}) %collective-permute-start.12) | collective-permute-done | bytes 65568 | tf_op jit(solution)/shard_map/ppermute | solution.py:36
  31.4 1.7 %collective-permute-start.16 = (bf16[64,512]{1,0:T(8,128)(2,1)S(1)}, bf16[64,512]{1,0:T(8,128)(2,1)S(1)}, u32[]{:S(2)}, u32[]{:S(2)}) collective-permute-start(bf16[64,512]{1,0:T(8,128)(2,1)S(1)} %get-tuple-element.70), channel_id=1, source_target_pairs={{0,6},{1,7},{2,4},{3,5},{4,2},{5,3},{6,0},{7,1},{8,14},{9,15},{10,... | collective-permute-start | bytes 196616 | tf_op jit(solution)/shard_map/ppermute | solution.py:36
  35.0 2.0 %collective-permute-done.16.refs_5_ = bf16[64,512]{1,0:T(8,128)(2,1)S(1)} collective-permute-done((bf16[64,512]{1,0:T(8,128)(2,1)S(1)}, bf16[64,512]{1,0:T(8,128)(2,1)S(1)}, u32[]{:S(2)}, u32[]{:S(2)}) %collective-permute-start.16) | collective-permute-done | bytes 65568 | tf_op jit(solution)/shard_map/ppermute | solution.py:36
  37.3 2.6 %collective-permute-start.18 = (bf16[64,512]{1,0:T(8,128)(2,1)S(1)}, bf16[64,512]{1,0:T(8,128)(2,1)S(1)}, u32[]{:S(2)}, u32[]{:S(2)}) collective-permute-start(bf16[64,512]{1,0:T(8,128)(2,1)S(1)} %fusion), channel_id=1, source_target_pairs={{0,8},{1,9},{2,10},{3,11},{4,12},{5,13},{6,14},{7,15},{8,0},{9,1},... | collective-permute-start | bytes 196616 | tf_op jit(solution)/shard_map/ppermute | solution.py:36
  39.9 4.3 %collective-permute-done.18 = bf16[64,512]{1,0:T(8,128)(2,1)S(1)} collective-permute-done((bf16[64,512]{1,0:T(8,128)(2,1)S(1)}, bf16[64,512]{1,0:T(8,128)(2,1)S(1)}, u32[]{:S(2)}, u32[]{:S(2)}) %collective-permute-start.18) | collective-permute-done | bytes 65568 | tf_op jit(solution)/shard_map/ppermute | solution.py:36
  45.0 2.5 %collective-permute-start.21 = (bf16[64,512]{1,0:T(8,128)(2,1)S(1)}, bf16[64,512]{1,0:T(8,128)(2,1)S(1)}, u32[]{:S(2)}, u32[]{:S(2)}) collective-permute-start(bf16[64,512]{1,0:T(8,128)(2,1)S(1)} %get-tuple-element.94.refs_2_), channel_id=1, source_target_pairs={{0,5},{1,4},{2,7},{3,6},{4,1},{5,0},{6,3},{7,2},{8,13},{9,12},{10,... | collective-permute-start | bytes 196616 | tf_op jit(solution)/shard_map/ppermute | solution.py:36
  47.5 2.1 %collective-permute-done.20.refs_4_ = bf16[64,512]{1,0:T(8,128)(2,1)S(1)} collective-permute-done((bf16[64,512]{1,0:T(8,128)(2,1)S(1)}, bf16[64,512]{1,0:T(8,128)(2,1)S(1)}, u32[]{:S(2)}, u32[]{:S(2)}) %collective-permute-start.20) | collective-permute-done | bytes 65568 | tf_op jit(solution)/shard_map/ppermute | solution.py:36
  52.3 1.8 %collective-permute-start.23 = (bf16[64,512]{1,0:T(8,128)(2,1)S(1)}, bf16[64,512]{1,0:T(8,128)(2,1)S(1)}, u32[]{:S(2)}, u32[]{:S(2)}) collective-permute-start(bf16[64,512]{1,0:T(8,128)(2,1)S(1)} %get-tuple-element.78), channel_id=1, source_target_pairs={{0,6},{1,7},{2,4},{3,5},{4,2},{5,3},{6,0},{7,1},{8,14},{9,15},{10,... | collective-permute-start | bytes 196616 | tf_op jit(solution)/shard_map/ppermute | solution.py:36
  55.9 1.9 %collective-permute-done.23.refs_5_ = bf16[64,512]{1,0:T(8,128)(2,1)S(1)} collective-permute-done((bf16[64,512]{1,0:T(8,128)(2,1)S(1)}, bf16[64,512]{1,0:T(8,128)(2,1)S(1)}, u32[]{:S(2)}, u32[]{:S(2)}) %collective-permute-start.23) | collective-permute-done | bytes 65568 | tf_op jit(solution)/shard_map/ppermute | solution.py:36
  58.3 2.4 %collective-permute-start.25 = (bf16[64,512]{1,0:T(8,128)(2,1)S(1)}, bf16[64,512]{1,0:T(8,128)(2,1)S(1)}, u32[]{:S(2)}, u32[]{:S(2)}) collective-permute-start(bf16[64,512]{1,0:T(8,128)(2,1)S(1)} %fusion.1), channel_id=1, source_target_pairs={{0,8},{1,9},{2,10},{3,11},{4,12},{5,13},{6,14},{7,15},{8,0},{9,1},... | collective-permute-start | bytes 196616 | tf_op jit(solution)/shard_map/ppermute | solution.py:36
  60.7 4.4 %collective-permute-done.25 = bf16[64,512]{1,0:T(8,128)(2,1)S(1)} collective-permute-done((bf16[64,512]{1,0:T(8,128)(2,1)S(1)}, bf16[64,512]{1,0:T(8,128)(2,1)S(1)}, u32[]{:S(2)}, u32[]{:S(2)}) %collective-permute-start.25) | collective-permute-done | bytes 65568 | tf_op jit(solution)/shard_map/ppermute | solution.py:36
  66.0 2.5 %collective-permute-start.29 = (bf16[64,512]{1,0:T(8,128)(2,1)S(1)}, bf16[64,512]{1,0:T(8,128)(2,1)S(1)}, u32[]{:S(2)}, u32[]{:S(2)}) collective-permute-start(bf16[64,512]{1,0:T(8,128)(2,1)S(1)} %get-tuple-element.83.refs_2_), channel_id=1, source_target_pairs={{0,5},{1,4},{2,7},{3,6},{4,1},{5,0},{6,3},{7,2},{8,13},{9,12},{10,... | collective-permute-start | bytes 196616 | tf_op jit(solution)/shard_map/ppermute | solution.py:36
  68.5 1.2 %collective-permute-done.28.other = f32[64,128]{1,0:T(8,128)S(1)} collective-permute-done((f32[64,128]{1,0:T(8,128)S(1)}, f32[64,128]{1,0:T(8,128)S(1)}, u32[]{:S(2)}, u32[]{:S(2)}) %collective-permute-start.28) | collective-permute-done | bytes 32800 | tf_op jit(solution)/shard_map/ppermute | solution.py:36
  73.2 1.0 %shard_map.111 = f32[256,128]{1,0:T(8,128)} custom-call(bf16[2,4,256,512]{3,2,1,0:T(8,128)(2,1)S(1)} %shard_map.95.a_ref.refs_0_.a, f32[256,64]{1,0:T(8,128)S(1)} %get-tuple-element.91.base, bf16[64,512]{1,0:T(8,128)(2,1)S(1)} %collective-permute-done.29.last, f32[256,64]{1,0:T(8,128)S(1)} %collective-permute-done.30.other), custom_call_target="tpu_custom_call" | custom-call | tf_op jit(solution)/shard_map/pallas_call | solution.py:257
  (78 shorter events, 19.4 us)
Async XLA Ops:
  4.4 4.9 %collective-permute-start.3 = (f32[64,512]{1,0:T(8,128)S(1)}, f32[64,512]{1,0:T(8,128)S(1)}, u32[]{:S(2)}, u32[]{:S(2)}) collective-permute-start(f32[64,512]{1,0:T(8,128)S(1)} %get-tuple-element.55), channel_id=1, source_target_pairs={{0,1},{1,0},{2,3},{3,2},{4,5},{5,4},{6,7},{7,6},{8,9},{9,8},{10,11... | collective-permute-start | bytes 393224 | tf_op jit(solution)/shard_map/ppermute | solution.py:36
  4.5 9.2 %collective-permute-start.2 = (f32[64,512]{1,0:T(8,128)S(1)}, f32[64,512]{1,0:T(8,128)S(1)}, u32[]{:S(2)}, u32[]{:S(2)}) collective-permute-start(f32[64,512]{1,0:T(8,128)S(1)} %get-tuple-element.52), channel_id=1, source_target_pairs={{0,1},{1,0},{2,3},{3,2},{4,5},{5,4},{6,7},{7,6},{8,9},{9,8},{10,11... | collective-permute-start | bytes 393224 | tf_op jit(solution)/shard_map/ppermute | solution.py:36
  4.9 5.6 %collective-permute-start.5 = (f32[64,512]{1,0:T(8,128)S(1)}, f32[64,512]{1,0:T(8,128)S(1)}, u32[]{:S(2)}, u32[]{:S(2)}) collective-permute-start(f32[64,512]{1,0:T(8,128)S(1)} %get-tuple-element.57), channel_id=1, source_target_pairs={{0,1},{1,0},{2,3},{3,2},{4,5},{5,4},{6,7},{7,6},{8,9},{9,8},{10,11... | collective-permute-start | bytes 393224 | tf_op jit(solution)/shard_map/ppermute | solution.py:36
  5.0 7.2 %collective-permute-start.7 = (f32[64,512]{1,0:T(8,128)S(1)}, f32[64,512]{1,0:T(8,128)S(1)}, u32[]{:S(2)}, u32[]{:S(2)}) collective-permute-start(f32[64,512]{1,0:T(8,128)S(1)} %get-tuple-element.59), channel_id=1, source_target_pairs={{0,1},{1,0},{2,3},{3,2},{4,5},{5,4},{6,7},{7,6},{8,9},{9,8},{10,11... | collective-permute-start | bytes 393224 | tf_op jit(solution)/shard_map/ppermute | solution.py:36
  5.5 8.2 %collective-permute-start.1 = (f32[144,128]{1,0:T(8,128)S(1)}, f32[144,128]{1,0:T(8,128)S(1)}, u32[]{:S(2)}, u32[]{:S(2)}) collective-permute-start(f32[144,128]{1,0:T(8,128)S(1)} %pad_maximum_fusion), channel_id=1, source_target_pairs={{0,8},{1,9},{2,10},{3,11},{4,12},{5,13},{6,14},{7,15},{8,0},{9,1},... | collective-permute-start | bytes 221192 | tf_op jit(solution)/shard_map/ppermute | solution.py:36
  9.4 4.3 %collective-permute-start.4 = (bf16[64,512]{1,0:T(8,128)(2,1)S(1)}, bf16[64,512]{1,0:T(8,128)(2,1)S(1)}, u32[]{:S(2)}, u32[]{:S(2)}) collective-permute-start(bf16[64,512]{1,0:T(8,128)(2,1)S(1)} %add_convert_fusion.2), channel_id=1, source_target_pairs={{0,3},{1,2},{2,1},{3,0},{4,7},{5,6},{6,5},{7,4},{8,11},{9,10},{10,... | collective-permute-start | bytes 196616 | tf_op jit(solution)/shard_map/ppermute | solution.py:36
  10.6 5.5 %collective-permute-start.6 = (bf16[64,512]{1,0:T(8,128)(2,1)S(1)}, bf16[64,512]{1,0:T(8,128)(2,1)S(1)}, u32[]{:S(2)}, u32[]{:S(2)}) collective-permute-start(bf16[64,512]{1,0:T(8,128)(2,1)S(1)} %add_convert_fusion.1), channel_id=1, source_target_pairs={{0,6},{1,7},{2,4},{3,5},{4,2},{5,3},{6,0},{7,1},{8,14},{9,15},{10,... | collective-permute-start | bytes 196616 | tf_op jit(solution)/shard_map/ppermute | solution.py:36
  16.4 12.5 %collective-permute-start.10 = (bf16[2,4,256,512]{3,2,1,0:T(8,128)(2,1)S(1)}, bf16[2,4,256,512]{3,2,1,0:T(8,128)(2,1)S(1)}, u32[]{:S(2)}, u32[]{:S(2)}) collective-permute-start(bf16[2,4,256,512]{3,2,1,0:T(8,128)(2,1)S(1)} %shard_map.95.a_ref.refs_0_.a), channel_id=1, source_target_pairs={{0,1},{1,0},{2,3},{3,2},{4,5},{5,4},{6,7},{7,6},{8,9},{9,8},{10,11... | collective-permute-start | bytes 6291464 | tf_op jit(solution)/shard_map/ppermute | solution.py:36
  16.6 6.7 %collective-permute-start.9 = (bf16[64,512]{1,0:T(8,128)(2,1)S(1)}, bf16[64,512]{1,0:T(8,128)(2,1)S(1)}, u32[]{:S(2)}, u32[]{:S(2)}) collective-permute-start(bf16[64,512]{1,0:T(8,128)(2,1)S(1)} %get-tuple-element.98), channel_id=1, source_target_pairs={{0,8},{1,9},{2,10},{3,11},{4,12},{5,13},{6,14},{7,15},{8,0},{9,1},... | collective-permute-start | bytes 196616 | tf_op jit(solution)/shard_map/ppermute | solution.py:36
  17.9 11.0 %collective-permute-start.13 = (f32[2,256,64]{2,1,0:T(8,128)S(1)}, f32[2,256,64]{2,1,0:T(8,128)S(1)}, u32[]{:S(2)}, u32[]{:S(2)}) collective-permute-start(f32[2,256,64]{2,1,0:T(8,128)S(1)} %get-tuple-element.64), channel_id=1, source_target_pairs={{0,1},{1,0},{2,3},{3,2},{4,5},{5,4},{6,7},{7,6},{8,9},{9,8},{10,11... | collective-permute-start | bytes 393224 | tf_op jit(solution)/shard_map/ppermute | solution.py:36
  23.3 5.3 %collective-permute-start.12 = (bf16[64,512]{1,0:T(8,128)(2,1)S(1)}, bf16[64,512]{1,0:T(8,128)(2,1)S(1)}, u32[]{:S(2)}, u32[]{:S(2)}) collective-permute-start(bf16[64,512]{1,0:T(8,128)(2,1)S(1)} %get-tuple-element.96.refs_2_), channel_id=1, source_target_pairs={{0,6},{1,7},{2,4},{3,5},{4,2},{5,3},{6,0},{7,1},{8,14},{9,15},{10,... | collective-permute-start | bytes 196616 | tf_op jit(solution)/shard_map/ppermute | solution.py:36
  24.4 4.5 %collective-permute-start.11 = (bf16[64,512]{1,0:T(8,128)(2,1)S(1)}, bf16[64,512]{1,0:T(8,128)(2,1)S(1)}, u32[]{:S(2)}, u32[]{:S(2)}) collective-permute-start(bf16[64,512]{1,0:T(8,128)(2,1)S(1)} %get-tuple-element.96.refs_2_), channel_id=1, source_target_pairs={{0,3},{1,2},{2,1},{3,0},{4,7},{5,6},{6,5},{7,4},{8,11},{9,10},{10,... | collective-permute-start | bytes 196616 | tf_op jit(solution)/shard_map/ppermute | solution.py:36
  24.4 5.5 %collective-permute-start.14 = (bf16[64,512]{1,0:T(8,128)(2,1)S(1)}, bf16[64,512]{1,0:T(8,128)(2,1)S(1)}, u32[]{:S(2)}, u32[]{:S(2)}) collective-permute-start(bf16[64,512]{1,0:T(8,128)(2,1)S(1)} %get-tuple-element.96.refs_2_), channel_id=1, source_target_pairs={{0,5},{1,4},{2,7},{3,6},{4,1},{5,0},{6,3},{7,2},{8,13},{9,12},{10,... | collective-permute-start | bytes 196616 | tf_op jit(solution)/shard_map/ppermute | solution.py:36
  30.8 4.2 %collective-permute-start.15 = (bf16[64,512]{1,0:T(8,128)(2,1)S(1)}, bf16[64,512]{1,0:T(8,128)(2,1)S(1)}, u32[]{:S(2)}, u32[]{:S(2)}) collective-permute-start(bf16[64,512]{1,0:T(8,128)(2,1)S(1)} %get-tuple-element.69), channel_id=1, source_target_pairs={{0,3},{1,2},{2,1},{3,0},{4,7},{5,6},{6,5},{7,4},{8,11},{9,10},{10,... | collective-permute-start | bytes 196616 | tf_op jit(solution)/shard_map/ppermute | solution.py:36
  31.4 5.5 %collective-permute-start.16 = (bf16[64,512]{1,0:T(8,128)(2,1)S(1)}, bf16[64,512]{1,0:T(8,128)(2,1)S(1)}, u32[]{:S(2)}, u32[]{:S(2)}) collective-permute-start(bf16[64,512]{1,0:T(8,128)(2,1)S(1)} %get-tuple-element.70), channel_id=1, source_target_pairs={{0,6},{1,7},{2,4},{3,5},{4,2},{5,3},{6,0},{7,1},{8,14},{9,15},{10,... | collective-permute-start | bytes 196616 | tf_op jit(solution)/shard_map/ppermute | solution.py:36
  37.3 6.8 %collective-permute-start.18 = (bf16[64,512]{1,0:T(8,128)(2,1)S(1)}, bf16[64,512]{1,0:T(8,128)(2,1)S(1)}, u32[]{:S(2)}, u32[]{:S(2)}) collective-permute-start(bf16[64,512]{1,0:T(8,128)(2,1)S(1)} %fusion), channel_id=1, source_target_pairs={{0,8},{1,9},{2,10},{3,11},{4,12},{5,13},{6,14},{7,15},{8,0},{9,1},... | collective-permute-start | bytes 196616 | tf_op jit(solution)/shard_map/ppermute | solution.py:36
  44.2 5.3 %collective-permute-start.20 = (bf16[64,512]{1,0:T(8,128)(2,1)S(1)}, bf16[64,512]{1,0:T(8,128)(2,1)S(1)}, u32[]{:S(2)}, u32[]{:S(2)}) collective-permute-start(bf16[64,512]{1,0:T(8,128)(2,1)S(1)} %get-tuple-element.94.refs_2_), channel_id=1, source_target_pairs={{0,6},{1,7},{2,4},{3,5},{4,2},{5,3},{6,0},{7,1},{8,14},{9,15},{10,... | collective-permute-start | bytes 196616 | tf_op jit(solution)/shard_map/ppermute | solution.py:36
  45.0 4.9 %collective-permute-start.19 = (bf16[64,512]{1,0:T(8,128)(2,1)S(1)}, bf16[64,512]{1,0:T(8,128)(2,1)S(1)}, u32[]{:S(2)}, u32[]{:S(2)}) collective-permute-start(bf16[64,512]{1,0:T(8,128)(2,1)S(1)} %get-tuple-element.94.refs_2_), channel_id=1, source_target_pairs={{0,3},{1,2},{2,1},{3,0},{4,7},{5,6},{6,5},{7,4},{8,11},{9,10},{10,... | collective-permute-start | bytes 196616 | tf_op jit(solution)/shard_map/ppermute | solution.py:36
  45.0 5.8 %collective-permute-start.21 = (bf16[64,512]{1,0:T(8,128)(2,1)S(1)}, bf16[64,512]{1,0:T(8,128)(2,1)S(1)}, u32[]{:S(2)}, u32[]{:S(2)}) collective-permute-start(bf16[64,512]{1,0:T(8,128)(2,1)S(1)} %get-tuple-element.94.refs_2_), channel_id=1, source_target_pairs={{0,5},{1,4},{2,7},{3,6},{4,1},{5,0},{6,3},{7,2},{8,13},{9,12},{10,... | collective-permute-start | bytes 196616 | tf_op jit(solution)/shard_map/ppermute | solution.py:36
  52.3 5.5 %collective-permute-start.23 = (bf16[64,512]{1,0:T(8,128)(2,1)S(1)}, bf16[64,512]{1,0:T(8,128)(2,1)S(1)}, u32[]{:S(2)}, u32[]{:S(2)}) collective-permute-start(bf16[64,512]{1,0:T(8,128)(2,1)S(1)} %get-tuple-element.78), channel_id=1, source_target_pairs={{0,6},{1,7},{2,4},{3,5},{4,2},{5,3},{6,0},{7,1},{8,14},{9,15},{10,... | collective-permute-start | bytes 196616 | tf_op jit(solution)/shard_map/ppermute | solution.py:36
  58.3 6.8 %collective-permute-start.25 = (bf16[64,512]{1,0:T(8,128)(2,1)S(1)}, bf16[64,512]{1,0:T(8,128)(2,1)S(1)}, u32[]{:S(2)}, u32[]{:S(2)}) collective-permute-start(bf16[64,512]{1,0:T(8,128)(2,1)S(1)} %fusion.1), channel_id=1, source_target_pairs={{0,8},{1,9},{2,10},{3,11},{4,12},{5,13},{6,14},{7,15},{8,0},{9,1},... | collective-permute-start | bytes 196616 | tf_op jit(solution)/shard_map/ppermute | solution.py:36
  65.2 5.3 %collective-permute-start.27 = (bf16[64,512]{1,0:T(8,128)(2,1)S(1)}, bf16[64,512]{1,0:T(8,128)(2,1)S(1)}, u32[]{:S(2)}, u32[]{:S(2)}) collective-permute-start(bf16[64,512]{1,0:T(8,128)(2,1)S(1)} %get-tuple-element.83.refs_2_), channel_id=1, source_target_pairs={{0,6},{1,7},{2,4},{3,5},{4,2},{5,3},{6,0},{7,1},{8,14},{9,15},{10,... | collective-permute-start | bytes 196616 | tf_op jit(solution)/shard_map/ppermute | solution.py:36
  65.7 4.8 %collective-permute-start.26 = (bf16[64,512]{1,0:T(8,128)(2,1)S(1)}, bf16[64,512]{1,0:T(8,128)(2,1)S(1)}, u32[]{:S(2)}, u32[]{:S(2)}) collective-permute-start(bf16[64,512]{1,0:T(8,128)(2,1)S(1)} %get-tuple-element.83.refs_2_), channel_id=1, source_target_pairs={{0,3},{1,2},{2,1},{3,0},{4,7},{5,6},{6,5},{7,4},{8,11},{9,10},{10,... | collective-permute-start | bytes 196616 | tf_op jit(solution)/shard_map/ppermute | solution.py:36
  66.0 5.5 %collective-permute-start.29 = (bf16[64,512]{1,0:T(8,128)(2,1)S(1)}, bf16[64,512]{1,0:T(8,128)(2,1)S(1)}, u32[]{:S(2)}, u32[]{:S(2)}) collective-permute-start(bf16[64,512]{1,0:T(8,128)(2,1)S(1)} %get-tuple-element.83.refs_2_), channel_id=1, source_target_pairs={{0,5},{1,4},{2,7},{3,6},{4,1},{5,0},{6,3},{7,2},{8,13},{9,12},{10,... | collective-permute-start | bytes 196616 | tf_op jit(solution)/shard_map/ppermute | solution.py:36
  (12 other events, 42.8 us)
